TPU v7x, 256 devices: a whole 4x4x8 slice. The times are simulated.
256 devices in a mesh: real: 4 (over x), cell: 64 (over y, z, core).
Axes of the slice: x: 4, y: 4, z: 8, core: 2. Of those that a mesh axis runs over, the one named last changes fastest.
Arguments:
- soil_heat_field: float32 [2048, 256, 512], P('cell', None, 'real'), may hold values from -250 to 250, as said below
- seed_subspace: float32 [512, 128], replicated, may hold values from -6 to 6
Outputs:
- core_tensor: float32 [2048, 256, 128], P('cell', None, 'real')
- mode_factor: float32 [512, 128], replicated
- triangle: float32 [512, 512], replicated
Inputs may be any that keep to these rules, and one draw needn't show every extreme that they name: `soil_heat_field`: real values.
All inputs are finite; a program needn't handle non-finite values.
Results may differ from a plain program's by a relative error of at most 0.00024.
Values sent between devices are 32-bit elements; how exact they have to be, the bound alone decides.
No kernel may reach another device: no remote copies, remote signals or barrier semaphores. Data moves between devices by JAX's collectives and lax.ppermute only.
A program may use at most 64 MiB of HBM per device.

v0:
```python
import jax
import jax.numpy as jnp
from jax import lax
from jax.sharding import PartitionSpec as P

ITERS = 3


def swapped(block, axis, stride):
    count = lax.axis_size(axis)
    route = []
    for low in range(count):
        high = low | 1 << stride
        if high != low and high < count:
            route += [(low, high), (high, low)]
    return lax.ppermute(block, axis, route)


def gram_of(array_operand):
    return lax.dot_general(
        array_operand,
        array_operand,
        (((0,), (0,)), ((), ())),
        precision=lax.Precision.HIGHEST,
        preferred_element_type=jnp.float32,
    )


def orthonormal(gram, seed_subspace):
    basis_block = seed_subspace
    for step_index in range(ITERS):
        imaged = jnp.dot(
            gram, basis_block, precision=lax.Precision.HIGHEST, preferred_element_type=jnp.float32
        )
        cholesky_lower = jnp.linalg.cholesky(gram_of(imaged))
        basis_block = lax.linalg.triangular_solve(
            cholesky_lower, imaged, left_side=False, lower=True, transpose_a=True
        )
    return basis_block


def local(soil_heat_field, seed_subspace):
    permuted_array = lax.all_to_all(
        soil_heat_field, "real", split_axis=1, concat_axis=2, tiled=True
    )
    flattened_mode_array = permuted_array.reshape(-1, permuted_array.shape[2])
    total_rows = flattened_mode_array.shape[0] * lax.axis_size(("real", "cell"))
    own_gram = gram_of(flattened_mode_array) / total_rows
    summed = own_gram
    for level in range(lax.axis_size(("real", "cell")).bit_length() - 1):
        summed = summed + swapped(summed, ("real", "cell"), level)
    triangle = jnp.linalg.cholesky(summed).T
    mode_factor = orthonormal(summed, seed_subspace)
    compressed_array = jnp.dot(
        flattened_mode_array,
        mode_factor,
        precision=lax.Precision.HIGHEST,
        preferred_element_type=jnp.float32,
    )
    compressed_array = compressed_array.reshape(
        permuted_array.shape[0], permuted_array.shape[1], -1
    )
    core_tensor = lax.all_to_all(compressed_array, "real", split_axis=2, concat_axis=1, tiled=True)
    return (core_tensor, mode_factor, triangle)


def solution(mesh):
    return jax.shard_map(
        local,
        mesh=mesh,
        in_specs=(P("cell", None, "real"), P()),
        out_specs=(P("cell", None, "real"), P(), P()),
        check_vma=False,
    )
```

profile of v0, /device:TPU:1, one launch (start us, length us, event | category | flops | bytes accessed | tf_op | source)
XLA Modules:
  0.0 491.2 jit_solution(1299835492257867962)
XLA Ops:
  0.6 4.7 copy.44
  5.3 52.5 %all_to_all.33 = f32[32,256,128]{2,0,1:T(8,128)S(1)} all-to-all(f32[32,256,128]{2,0,1:T(8,128)S(1)} %copy.44), channel_id=1, replica_groups=mesh['real'=4,'cell'=64] {'real'}, dimensions={1} | all-to-all | bytes 8388608 | tf_op jit(solution)/shard_map/all_to_all | solution.py:43
  57.8 2.7 copy.45
  60.5 6.8 %fusion.9 = f32[512,512]{0,1:T(8,128)S(1)} fusion(f32[256,8,4,128]{3,2,1,0:T(4,128)S(1)} %bitcast.96), kind=kOutput, calls=%fused_computation.7 | convolution fusion | flops 6442713088 | bytes 5242880 | tf_op jit(solution)/shard_map/dot_general | solution.py:20
  67.3 2.2 collective-permute-start
  69.5 2.3 collective-permute-done
  72.0 1.7 collective-permute-start.1
  73.7 23.1 %collective-permute-done.1 = f32[512,512]{0,1:T(8,128)S(1)} collective-permute-done((f32[512,512]{0,1:T(8,128)S(1)}, f32[512,512]{0,1:T(8,128)S(1)}, u32[]{:S(2)}, u32[]{:S(2)}) %collective-permute-start.1) | collective-permute-done | bytes 1048608 | tf_op jit(solution)/shard_map/ppermute | solution.py:16
  97.0 3.3 collective-permute-start.2
  100.3 45.1 %collective-permute-done.2 = f32[512,512]{0,1:T(8,128)S(1)} collective-permute-done((f32[512,512]{0,1:T(8,128)S(1)}, f32[512,512]{0,1:T(8,128)S(1)}, u32[]{:S(2)}, u32[]{:S(2)}) %collective-permute-start.2) | collective-permute-done | bytes 1048608 | tf_op jit(solution)/shard_map/ppermute | solution.py:16
  145.6 6.5 %collective-permute-start.3 = (f32[512,512]{0,1:T(8,128)S(1)}, f32[512,512]{0,1:T(8,128)S(1)}, u32[]{:S(2)}, u32[]{:S(2)}) collective-permute-start(f32[512,512]{0,1:T(8,128)S(1)} %add.72), channel_id=1, source_target_pairs={{0,8},{8,0},{1,9},{9,1},{2,10},{10,2},{3,11},{11,3},{4,12},{12,4},... | collective-permute-start | bytes 3145736 | tf_op jit(solution)/shard_map/ppermute | solution.py:16
  152.1 45.4 %collective-permute-done.3 = f32[512,512]{0,1:T(8,128)S(1)} collective-permute-done((f32[512,512]{0,1:T(8,128)S(1)}, f32[512,512]{0,1:T(8,128)S(1)}, u32[]{:S(2)}, u32[]{:S(2)}) %collective-permute-start.3) | collective-permute-done | bytes 1048608 | tf_op jit(solution)/shard_map/ppermute | solution.py:16
  197.7 1.4 collective-permute-start.4
  199.1 21.7 %collective-permute-done.4 = f32[512,512]{0,1:T(8,128)S(1)} collective-permute-done((f32[512,512]{0,1:T(8,128)S(1)}, f32[512,512]{0,1:T(8,128)S(1)}, u32[]{:S(2)}, u32[]{:S(2)}) %collective-permute-start.4) | collective-permute-done | bytes 1048608 | tf_op jit(solution)/shard_map/ppermute | solution.py:16
  221.0 3.0 collective-permute-start.5
  224.0 20.9 %collective-permute-done.5 = f32[512,512]{0,1:T(8,128)S(1)} collective-permute-done((f32[512,512]{0,1:T(8,128)S(1)}, f32[512,512]{0,1:T(8,128)S(1)}, u32[]{:S(2)}, u32[]{:S(2)}) %collective-permute-start.5) | collective-permute-done | bytes 1048608 | tf_op jit(solution)/shard_map/ppermute | solution.py:16
  245.5 21.0 %collective-permute-done.6 = f32[512,512]{0,1:T(8,128)S(1)} collective-permute-done((f32[512,512]{0,1:T(8,128)S(1)}, f32[512,512]{0,1:T(8,128)S(1)}, u32[]{:S(2)}, u32[]{:S(2)}) %collective-permute-start.6) | collective-permute-done | bytes 1048608 | tf_op jit(solution)/shard_map/ppermute | solution.py:16
  266.7 1.2 collective-permute-start.7
  267.9 20.8 %collective-permute-done.7 = f32[512,512]{0,1:T(8,128)S(1)} collective-permute-done((f32[512,512]{0,1:T(8,128)S(1)}, f32[512,512]{0,1:T(8,128)S(1)}, u32[]{:S(2)}, u32[]{:S(2)}) %collective-permute-start.7) | collective-permute-done | bytes 1048608 | tf_op jit(solution)/shard_map/ppermute | solution.py:16
  288.9 1.8 fusion.56
  290.7 0.6 fusion.57
  291.4 11.7 %cholesky.325 = f32[128,128]{1,0:T(8,128)S(1)} custom-call(f32[128,128]{1,0:T(8,128)S(1)} %fusion.37), custom_call_target="Cholesky" | custom-call | tf_op jit(solution)/shard_map/jit(cholesky)/cholesky | solution.py:35
  303.1 0.6 compare_reduce_fusion.2
  303.8 0.7 fusion.21
  304.4 9.8 %custom-call.37 = f32[1,128,128]{1,2,0:T(8,128)S(1)} custom-call(f32[1,128,128]{2,1,0:T(8,128)S(1)} %fusion.21), custom_call_target="InvertDiagBlocksLowerTriangular" | custom-call | tf_op jit(solution)/shard_map/triangular_solve/custom-call.8 | solution.py:36
  314.7 1.8 fusion.58
  316.5 0.6 fusion.59
  317.2 11.9 %cholesky.336 = f32[128,128]{1,0:T(8,128)S(1)} custom-call(f32[128,128]{1,0:T(8,128)S(1)} %fusion.35), custom_call_target="Cholesky" | custom-call | tf_op jit(solution)/shard_map/jit(cholesky)/cholesky | solution.py:35
  329.1 0.6 compare_reduce_fusion.1
  329.7 0.7 fusion.22
  330.4 9.8 %custom-call.38 = f32[1,128,128]{1,2,0:T(8,128)S(1)} custom-call(f32[1,128,128]{2,1,0:T(8,128)S(1)} %fusion.22), custom_call_target="InvertDiagBlocksLowerTriangular" | custom-call | tf_op jit(solution)/shard_map/triangular_solve/custom-call.8 | solution.py:36
  340.6 1.8 fusion.60
  343.2 11.7 %cholesky.347 = f32[128,128]{1,0:T(8,128)S(1)} custom-call(f32[128,128]{1,0:T(8,128)S(1)} %fusion.33), custom_call_target="Cholesky" | custom-call | tf_op jit(solution)/shard_map/jit(cholesky)/cholesky | solution.py:35
  354.9 0.6 compare_reduce_fusion
  355.6 0.7 fusion.23
  356.2 10.0 %custom-call.39 = f32[1,128,128]{1,2,0:T(8,128)S(1)} custom-call(f32[1,128,128]{2,1,0:T(8,128)S(1)} %fusion.23), custom_call_target="InvertDiagBlocksLowerTriangular" | custom-call | tf_op jit(solution)/shard_map/triangular_solve/custom-call.8 | solution.py:36
  366.6 6.6 %fusion.6 = f32[2048,128]{0,1:T(8,128)S(1)} fusion(f32[512,128]{0,1:T(8,128)S(1)} %convolution_bitcast_fusion, f32[256,8,4,128]{3,2,1,0:T(4,128)} %bitcast.97), kind=kOutput, calls=%fused_computation.6 | convolution fusion | flops 1610612736 | bytes 5505024 | tf_op jit(solution)/shard_map/dot_general | solution.py:54
  373.2 0.8 copy.55
  374.0 1.3 copy.54
  375.4 1.3 copy.50
  376.7 3.1 copy.51
  379.7 2.4 reshape.63
  382.1 3.9 all-to-all-start.1
  386.1 1.4 fusion.12
  387.5 11.7 %cholesky.131 = f32[128,128]{1,0:T(8,128)S(1)} custom-call(f32[128,128]{1,0:T(8,128)S(1)} %cholesky.356), custom_call_target="Cholesky" | custom-call | tf_op jit(solution)/shard_map/jit(cholesky)/cholesky | solution.py:52
  399.4 9.8 %custom-call.32 = f32[1,128,128]{1,2,0:T(8,128)S(1)} custom-call(f32[1,128,128]{2,1,0:T(8,128)S(1)} %get-tuple-element.29), custom_call_target="InvertDiagBlocksLowerTriangular" | custom-call | tf_op jit(solution)/shard_map/jit(cholesky)/cholesky | solution.py:52
  409.9 0.7 copy-done.2
  410.6 11.7 %cholesky.244 = f32[128,128]{1,0:T(8,128)S(1)} custom-call(f32[128,128]{1,0:T(8,128)S(1)} %cholesky.360), custom_call_target="Cholesky" | custom-call | tf_op jit(solution)/shard_map/jit(cholesky)/cholesky | solution.py:52
  422.3 9.9 %custom-call.33 = f32[1,128,128]{1,2,0:T(8,128)S(1)} custom-call(f32[1,128,128]{2,1,0:T(8,128)S(1)} %get-tuple-element.26), custom_call_target="InvertDiagBlocksLowerTriangular" | custom-call | tf_op jit(solution)/shard_map/jit(cholesky)/cholesky | solution.py:52
  432.3 1.2 convolution_dynamic-update-slice_fusion
  433.8 0.6 cholesky.365
  434.5 13.2 %cholesky.265 = f32[128,128]{1,0:T(8,128)} custom-call(f32[128,128]{1,0:T(8,128)} %cholesky.365), custom_call_target="Cholesky" | custom-call | tf_op jit(solution)/shard_map/jit(cholesky)/cholesky | solution.py:52
  447.7 1.5 fusion.54
  449.1 11.3 %custom-call.34 = f32[1,128,128]{1,2,0:T(8,128)} custom-call(f32[1,128,128]{2,1,0:T(8,128)} %get-tuple-element.23), custom_call_target="InvertDiagBlocksLowerTriangular" | custom-call | tf_op jit(solution)/shard_map/jit(cholesky)/cholesky | solution.py:52
  460.4 1.0 convolution_dynamic-update-slice_fusion.1
  461.8 11.7 %cholesky.282 = f32[128,128]{1,0:T(8,128)S(1)} custom-call(f32[128,128]{1,0:T(8,128)S(1)} %slice_subtract_fusion.2), custom_call_target="Cholesky" | custom-call | tf_op jit(solution)/shard_map/jit(cholesky)/cholesky | solution.py:52
  473.6 0.7 compare_reduce_fusion.5
  475.6 0.6 compare_reduce_fusion.4
  476.9 0.6 compare_reduce_fusion.3
  478.4 1.3 copy.56
  480.4 3.7 reduce.28
  484.1 1.0 reshape.64
  485.1 2.7 copy.53
  487.8 3.2 all_to_all.30
  (40 shorter events, 6.8 us)
Async XLA Ops:
  0.6 288.2 %copy-start = (f32[512,128]{1,0:T(8,128)S(1)}, f32[512,128]{1,0:T(8,128)}, u32[]{:S(2)}) copy-start(f32[512,128]{1,0:T(8,128)} %param.6) | copy-start | bytes 786436
  60.5 11.5 %copy-start.1 = (f32[32,4,64,128]{3,1,2,0:T(4,128)}, f32[32,4,64,128]{3,1,2,0:T(4,128)S(1)}, u32[]{:S(2)}) copy-start(f32[32,4,64,128]{3,1,2,0:T(4,128)S(1)} %copy.45) | copy-start | bytes 12582916
  67.3 4.5 collective-permute-start
  72.0 24.8 %collective-permute-start.1 = (f32[512,512]{0,1:T(8,128)S(1)}, f32[512,512]{0,1:T(8,128)S(1)}, u32[]{:S(2)}, u32[]{:S(2)}) collective-permute-start(f32[512,512]{0,1:T(8,128)S(1)} %add.70), channel_id=1, source_target_pairs={{0,2},{2,0},{1,3},{3,1},{4,6},{6,4},{5,7},{7,5},{8,10},{10,8},{9,1... | collective-permute-start | bytes 3145736 | tf_op jit(solution)/shard_map/ppermute | solution.py:16
  97.0 48.4 %collective-permute-start.2 = (f32[512,512]{0,1:T(8,128)S(1)}, f32[512,512]{0,1:T(8,128)S(1)}, u32[]{:S(2)}, u32[]{:S(2)}) collective-permute-start(f32[512,512]{0,1:T(8,128)S(1)} %add.71), channel_id=1, source_target_pairs={{0,4},{4,0},{1,5},{5,1},{2,6},{6,2},{3,7},{7,3},{8,12},{12,8},{9,1... | collective-permute-start | bytes 3145736 | tf_op jit(solution)/shard_map/ppermute | solution.py:16
  145.6 51.8 %collective-permute-start.3 = (f32[512,512]{0,1:T(8,128)S(1)}, f32[512,512]{0,1:T(8,128)S(1)}, u32[]{:S(2)}, u32[]{:S(2)}) collective-permute-start(f32[512,512]{0,1:T(8,128)S(1)} %add.72), channel_id=1, source_target_pairs={{0,8},{8,0},{1,9},{9,1},{2,10},{10,2},{3,11},{11,3},{4,12},{12,4},... | collective-permute-start | bytes 3145736 | tf_op jit(solution)/shard_map/ppermute | solution.py:16
  197.7 23.1 %collective-permute-start.4 = (f32[512,512]{0,1:T(8,128)S(1)}, f32[512,512]{0,1:T(8,128)S(1)}, u32[]{:S(2)}, u32[]{:S(2)}) collective-permute-start(f32[512,512]{0,1:T(8,128)S(1)} %add.73), channel_id=1, source_target_pairs={{0,16},{16,0},{1,17},{17,1},{2,18},{18,2},{3,19},{19,3},{4,20},{20... | collective-permute-start | bytes 3145736 | tf_op jit(solution)/shard_map/ppermute | solution.py:16
  221.0 23.9 %collective-permute-start.5 = (f32[512,512]{0,1:T(8,128)S(1)}, f32[512,512]{0,1:T(8,128)S(1)}, u32[]{:S(2)}, u32[]{:S(2)}) collective-permute-start(f32[512,512]{0,1:T(8,128)S(1)} %add.74), channel_id=1, source_target_pairs={{0,32},{32,0},{1,33},{33,1},{2,34},{34,2},{3,35},{35,3},{4,36},{36... | collective-permute-start | bytes 3145736 | tf_op jit(solution)/shard_map/ppermute | solution.py:16
  245.1 21.4 %collective-permute-start.6 = (f32[512,512]{0,1:T(8,128)S(1)}, f32[512,512]{0,1:T(8,128)S(1)}, u32[]{:S(2)}, u32[]{:S(2)}) collective-permute-start(f32[512,512]{0,1:T(8,128)S(1)} %add.75), channel_id=1, source_target_pairs={{0,64},{64,0},{1,65},{65,1},{2,66},{66,2},{3,67},{67,3},{4,68},{68... | collective-permute-start | bytes 3145736 | tf_op jit(solution)/shard_map/ppermute | solution.py:16
  266.7 21.9 %collective-permute-start.7 = (f32[512,512]{0,1:T(8,128)S(1)}, f32[512,512]{0,1:T(8,128)S(1)}, u32[]{:S(2)}, u32[]{:S(2)}) collective-permute-start(f32[512,512]{0,1:T(8,128)S(1)} %add.76), channel_id=1, source_target_pairs={{0,128},{128,0},{1,129},{129,1},{2,130},{130,2},{3,131},{131,3},{4... | collective-permute-start | bytes 3145736 | tf_op jit(solution)/shard_map/ppermute | solution.py:16
  382.1 97.7 %all-to-all-start.1 = ((f32[4,1,65536]{2,1,0:T(1,128)}), f32[4,1,65536]{2,1,0:T(1,128)S(1)}, u32[]{:S(2)}, u32[]{:S(2)}) async-start(f32[4,1,65536]{2,1,0:T(1,128)} %reshape.63), calls=%async_computation.1 | async-start | bytes 2097152 | tf_op jit(solution)/shard_map/all_to_all | solution.py:63
  409.9 0.7 copy-start.2
where the time goes:
time: 500 us; the launch traced here: 491 us
  waiting for transfers between devices  200 us (40%)
  other arithmetic  159 us (32%)
  blocking collectives  52.5 us (10%)
  local copies, waits for them, and re-layouts  26.7 us (5%)
  matrix products  25.4 us (5%)
  starting transfers between devices  23.5 us (5%)
    ppermute x8, waiting for transfers between devices, swapped(): return lax.ppermute(block, axis, route)  200 us
    another operation x14, other arithmetic, local(): triangle = jnp.linalg.cholesky(summed).T  82.9 us
    all_to_all x1, blocking collectives, local(): lax.all_to_all(soil_heat_field, 'real', split_axis=1, concat_axis=2, tile...  52.5 us
    another operation x9, other arithmetic, orthonormal(): cholesky_lower = jnp.linalg.cholesky(gram_of(imaged))  37.3 us
    another operation x6, other arithmetic, orthonormal(): lax.linalg.triangular_solve(cholesky_lower, imaged, left_side=False, lowe...  31.6 us
    ppermute x8, starting transfers between devices, swapped(): return lax.ppermute(block, axis, route)  19.6 us
    unnamed x11, local copies, waits for them, and re-layouts  10.9 us
  transfers between devices with their start and end apart: 9, of which 9 were waited for; matrix products, arithmetic and copies ran while one was open for 18% of the time, Pallas kernels for 0%

commit v1 on v0

v1 whole, which is shorter than its diff:
```python
import jax
import jax.numpy as jnp
from jax import lax
from jax.experimental import pallas as pl
from jax.experimental.pallas import tpu as pltpu
from jax.sharding import Mesh, PartitionSpec as P

ITERS = 3
HIGHEST = lax.Precision.HIGHEST
NB = 4
W = 128
PAIRS = [(k, l) for k in range(NB) for l in range(k, NB)]
VMEM_LIMIT = 56 * 1024 * 1024


def split(x):
    high = x.astype(jnp.bfloat16)
    return high, (x - high.astype(jnp.float32)).astype(jnp.bfloat16)


def contract(a, b, dims):
    return lax.dot_general(a, b, (dims, ((), ())), preferred_element_type=jnp.float32)


def gram_kernel(scale, x_ref, out_ref, hh, hl):
    step = pl.program_id(0)
    rows = jnp.concatenate([x_ref[k] for k in range(NB)], axis=1)
    high, low = split(rows)
    left = high.T
    part_hh = contract(left, high, ((1,), (0,)))
    part_hl = contract(left, low, ((1,), (0,)))

    @pl.when(step == 0)
    def _():
        hh[...] = part_hh
        hl[...] = part_hl

    @pl.when(step > 0)
    def _():
        hh[...] += part_hh
        hl[...] += part_hl

    @pl.when(step == pl.num_programs(0) - 1)
    def _():
        for n, (k, l) in enumerate(PAIRS):
            ks, ls = slice(W * k, W * k + W), slice(W * l, W * l + W)
            out_ref[n] = (hh[ks, ls] + (hl[ks, ls] + hl[ls, ks].T)) * scale


def gram_blocks(blocks, scale):
    rows = blocks.shape[1]
    step = 512
    return pl.pallas_call(
        lambda *refs: gram_kernel(scale, *refs),
        grid=(rows // step,),
        in_specs=[pl.BlockSpec((NB, step, W), lambda i: (0, i, 0))],
        out_specs=pl.BlockSpec((len(PAIRS), W, W), lambda i: (0, 0, 0)),
        out_shape=jax.ShapeDtypeStruct((len(PAIRS), W, W), jnp.float32),
        scratch_shapes=[pltpu.VMEM((NB * W, NB * W), jnp.float32)] * 2,
        compiler_params=pltpu.CompilerParams(vmem_limit_bytes=VMEM_LIMIT),
        cost_estimate=pl.CostEstimate(
            flops=4 * rows * (NB * W) ** 2, bytes_accessed=4 * rows * NB * W, transcendentals=0
        ),
        name="gram_blocks",
    )(blocks)


def reciprocal(d):
    r = pl.reciprocal(d, approx=True)
    r = r * (2.0 - d * r)
    return r * (2.0 - d * r)


def lanes(x, l):
    return jnp.broadcast_to(x[:, l : l + 1], (8, W))


def sublanes(x, i):
    return jnp.broadcast_to(x[i : i + 1, :], (8, W))


def factor(panels):
    count = len(panels)
    left = list(panels)
    sub = lax.broadcasted_iota(jnp.int32, (8, W), 0)
    lane = lax.broadcasted_iota(jnp.int32, (8, W), 1)
    right = [jnp.where(lane == sub + 8 * p, 1.0, 0.0).astype(jnp.float32) for p in range(count)]
    upper, inverse = [], []
    for p in range(count):
        rows0, rows1 = left[p], right[p]
        col = [lanes(rows0, 8 * p + j) for j in range(8)]
        s = {(i, j): sublanes(col[j], i) for j in range(8) for i in range(j, 8)}
        later = range(p + 1, count)
        cols = {q: [lanes(left[q], 8 * p + j) for j in range(8)] for q in later}
        for j in range(8):
            r = reciprocal(s[j, j])
            m = {i: s[i, j] * r for i in range(j + 1, 8)}
            for k in range(j + 1, 8):
                for i in range(k, 8):
                    s[i, k] = s[i, k] - m[i] * s[k, j]
            mine = jnp.where(sub > j, col[j] * r, 0.0)
            row0, row1 = sublanes(rows0, j), sublanes(rows1, j)
            for k in range(j + 1, 8):
                col[k] = col[k] - mine * s[k, j]
            rows0 = rows0 - mine * row0
            rows1 = rows1 - mine * row1
            for q in later:
                theirs = cols[q][j] * r
                for k in range(j + 1, 8):
                    cols[q][k] = cols[q][k] - theirs * s[k, j]
                left[q] = left[q] - theirs * row0
                right[q] = right[q] - theirs * row1
        pivots = s[0, 0]
        for i in range(1, 8):
            pivots = jnp.where(sub == i, s[i, i], pivots)
        scale = lax.rsqrt(pivots)
        upper.append(jnp.where(lane >= sub + 8 * p, rows0 * scale, 0.0))
        inverse.append(rows1 * scale)
    return upper, inverse


def panels_of(matrix):
    return [matrix[8 * p : 8 * p + 8, :] for p in range(matrix.shape[0] // 8)]


def exact(a, b, dims=((1,), (0,))):
    return lax.dot_general(
        a, b, (dims, ((), ())), precision=HIGHEST, preferred_element_type=jnp.float32
    )


def orthonormal_kernel(g_ref, seed_ref, basis_ref, mode_ref, gram):
    for n, (k, l) in enumerate(PAIRS):
        block = g_ref[n]
        gram[W * k : W * k + W, W * l : W * l + W] = block
        if k != l:
            gram[W * l : W * l + W, W * k : W * k + W] = block.T
    basis_ref[...] = seed_ref[...]

    def step(_, carry):
        imaged = exact(basis_ref[...], gram[...])
        small = exact(imaged, imaged, ((1,), (1,)))
        _, inverse = factor(panels_of(small))
        basis_ref[...] = exact(jnp.concatenate(inverse, axis=0), imaged)
        return carry

    lax.fori_loop(0, ITERS, step, 0)
    mode_ref[...] = basis_ref[...].T


def orthonormal(gram, seed_rows):
    size = NB * W
    return pl.pallas_call(
        orthonormal_kernel,
        out_shape=[
            jax.ShapeDtypeStruct(seed_rows.shape, jnp.float32),
            jax.ShapeDtypeStruct(seed_rows.shape[::-1], jnp.float32),
        ],
        scratch_shapes=[pltpu.VMEM((size, size), jnp.float32)],
        compiler_params=pltpu.CompilerParams(vmem_limit_bytes=VMEM_LIMIT),
        cost_estimate=pl.CostEstimate(
            flops=40_000_000_000, bytes_accessed=4 * size * size, transcendentals=0
        ),
        name="orthonormal",
    )(gram, seed_rows)


def triangle_kernel(g_ref, out_ref, rest):
    out_ref[...] = jnp.zeros_like(out_ref)
    for n, (k, l) in enumerate(PAIRS):
        rest[W * k : W * k + W, W * l : W * l + W] = g_ref[n]

    def step(b, carry):
        start = pl.multiple_of(b * W, W)
        own = pl.ds(start, W)
        upper, inverse = factor([rest[pl.ds(start + 8 * p, 8), own] for p in range(W // 8)])
        inverse = jnp.concatenate(inverse, axis=0)

        @pl.when(b < NB - 1)
        def _():
            keep = lax.broadcasted_iota(jnp.int32, (W, NB * W), 1) >= (b + 1) * W
            row = jnp.where(keep, exact(inverse, rest[own, :]), 0.0)
            out_ref[own, :] = row

            def down(c, carry):
                at = pl.ds(pl.multiple_of(c * W, W), W)
                rest[at, :] -= exact(out_ref[own, at].T, out_ref[own, :])
                return carry

            lax.fori_loop(b + 1, NB, down, 0)

        out_ref[own, own] = jnp.concatenate(upper, axis=0)
        return carry

    lax.fori_loop(0, NB, step, 0)


def triangle_of(gram):
    size = NB * W
    return pl.pallas_call(
        triangle_kernel,
        out_shape=jax.ShapeDtypeStruct((size, size), jnp.float32),
        scratch_shapes=[pltpu.VMEM((size, size), jnp.float32)],
        compiler_params=pltpu.CompilerParams(vmem_limit_bytes=VMEM_LIMIT),
        cost_estimate=pl.CostEstimate(
            flops=40_000_000_000, bytes_accessed=8 * size * size, transcendentals=0
        ),
        name="triangle",
    )(gram)


def core_kernel(basis_ref, x_ref, out_ref):
    rows = jnp.concatenate([x_ref[k, 0] for k in range(NB)], axis=1)
    high, low = split(rows)
    basis_high, basis_low = split(basis_ref[...])
    dims = ((1,), (1,))
    core = contract(basis_high, high, dims) + (
        contract(basis_high, low, dims) + contract(basis_low, high, dims)
    )
    part = core.shape[0] // NB
    for j in range(NB):
        out_ref[j, 0] = core[part * j : part * j + part, :]


def core_parts(basis, blocks):
    _, cells, snaps, _ = blocks.shape
    part = basis.shape[0] // NB
    return pl.pallas_call(
        core_kernel,
        grid=(cells,),
        in_specs=[
            pl.BlockSpec(basis.shape, lambda i: (0, 0)),
            pl.BlockSpec((NB, 1, snaps, W), lambda i: (0, i, 0, 0)),
        ],
        out_specs=pl.BlockSpec((NB, 1, part, snaps), lambda i: (0, i, 0, 0)),
        out_shape=jax.ShapeDtypeStruct((NB, cells, part, snaps), jnp.float32),
        compiler_params=pltpu.CompilerParams(vmem_limit_bytes=VMEM_LIMIT),
        cost_estimate=pl.CostEstimate(
            flops=6 * cells * snaps * NB * W * W,
            bytes_accessed=5 * cells * snaps * NB * W,
            transcendentals=0,
        ),
        name="core_parts",
    )(basis, blocks)


def exchanged(block, axis, bits):
    count = lax.axis_size(axis)
    return lax.ppermute(block, axis, [(i, i ^ bits) for i in range(count)])


def summed_over_devices(part):
    half = part.shape[0] // 2
    core = lax.axis_index("core")
    keep = lax.dynamic_slice_in_dim(part, core * half, half, 0)
    send = lax.dynamic_slice_in_dim(part, (1 - core) * half, half, 0)
    own = keep + exchanged(send, "core", 1)
    shares = lax.all_to_all(
        own.reshape(NB, half // NB, W), "x", split_axis=0, concat_axis=0, tiled=True
    )
    own = (shares[0] + shares[1]) + (shares[2] + shares[3])
    two, one, three = (exchanged(own, "y", bits) for bits in (2, 1, 3))
    own = (own + one) + (two + three)
    for bits in (1, 2, 4):
        own = own + exchanged(own, "z", bits)
    copies = jnp.broadcast_to(own[None], (NB, *own.shape))
    whole = lax.all_to_all(copies, "x", split_axis=0, concat_axis=0, tiled=True)
    whole = whole.reshape(half, W)
    return lax.all_gather(whole, "core", axis=0, tiled=True)


def to_owners(parts):
    me = lax.axis_index("x")
    arrived = [lax.dynamic_index_in_dim(parts, me, 0, keepdims=False)]
    sent = {
        bits: exchanged(
            lax.dynamic_index_in_dim(parts, me ^ bits, 0, keepdims=False), "x", bits
        )
        for bits in (2, 1, 3)
    }
    arrived += [sent[bits] for bits in (1, 2, 3)]
    low, high = (me & 1) == 1, (me & 2) == 2
    a, b, c, d = arrived
    a, b = jnp.where(low, b, a), jnp.where(low, a, b)
    c, d = jnp.where(low, d, c), jnp.where(low, c, d)
    a, c = jnp.where(high, c, a), jnp.where(high, a, c)
    b, d = jnp.where(high, d, b), jnp.where(high, b, d)
    return jnp.stack([a, b, c, d])


def local(soil_heat_field, seed_subspace):
    cells, snaps, width = soil_heat_field.shape
    devices = lax.axis_size(("x", "y", "z", "core"))
    blocks = lax.all_to_all(soil_heat_field, "x", split_axis=0, concat_axis=0, tiled=True)
    blocks = blocks.reshape(NB, cells // NB * snaps, width)
    total_rows = blocks.shape[1] * devices
    own_gram = gram_blocks(blocks, 1.0 / total_rows)
    gram = summed_over_devices(own_gram.reshape(-1, W)).reshape(own_gram.shape)
    basis, mode_factor = orthonormal(gram, seed_subspace.T)
    parts = core_parts(basis, blocks.reshape(NB, cells // NB, snaps, width))
    core_tensor = to_owners(parts)
    triangle = triangle_of(gram)
    core_tensor = core_tensor.reshape(cells, -1, snaps).transpose(0, 2, 1)
    return (core_tensor, mode_factor, triangle)


def solution(mesh):
    fine = Mesh(mesh.devices.reshape(4, -1, 8, 2), ("x", "y", "z", "core"))
    cell = ("y", "z", "core")
    return jax.shard_map(
        local,
        mesh=fine,
        in_specs=(P(cell, None, "x"), P()),
        out_specs=(P(cell, None, "x"), P(), P()),
        check_vma=False,
    )
```

time: 500 us -> 188 us (0.38); the launches traced: 491 us -> 188 us
  other arithmetic: 159 us -> 3.28 us
  waiting for transfers between devices: 200 us -> 64.9 us
  Pallas kernels: 0 us -> 65.6 us
  blocking collectives: 52.5 us -> 18 us
  matrix products: 25.4 us -> 0 us
  local copies, waits for them, and re-layouts: 26.7 us -> 3.8 us
  starting transfers between devices: 23.5 us -> 31.5 us
    ppermute x8 -> x10, waiting for transfers between devices: 200 us -> 13.1 us  [exchanged(): return lax.ppermute(block, axis, [(i, i ^ bits) for i in range(count)])]
    another operation x29 -> x2, other arithmetic: 152 us -> 2.19 us  [to_owners(): return jnp.stack([a, b, c, d])]
    pallas_call x0 -> x4, Pallas kernels: none -> 65.6 us  [the longest x1 27.5 us: triangle_of(): pl.pallas_call(triangle_kernel, out_shape=jax.ShapeDtypeStruct((size, siz...]
    all_to_all x1 -> x2, waiting for transfers between devices: 0.19 us -> 51.8 us  [the longest x1 46.8 us: local(): lax.all_to_all(soil_heat_field, 'x', split_axis=0, concat_axis=0, tiled=T...]
    all_to_all x1, blocking collectives: 52.5 us -> 9.2 us  [summed_over_devices(): lax.all_to_all(own.reshape(NB, half // NB, W), 'x', split_axis=0, concat_...]
    dot_general x8 -> x0, matrix products: 20.6 us -> none  [the longest x4 8.59 us: gram_of(): lax.dot_general(array_operand, array_operand, (((0,), (0,)), ((), ())), p...]
    unnamed x11 -> x3, local copies, waits for them, and re-layouts: 10.9 us -> 0.84 us
    all_to_all x4 -> x0, local copies, waits for them, and re-layouts: 9.12 us -> none  [the longest x3 6.42 us: local(): lax.all_to_all(compressed_array, 'real', split_axis=2, concat_axis=1, til...]
  transfers between devices with their start and end apart: 9 -> 12, of which waited for: 9 -> 8; matrix products, arithmetic and copies ran while one was open for 18% -> 0% of each run, Pallas kernels for 0% -> 15%
where the time goes in v1:
time: 188 us
  Pallas kernels  65.6 us (35%)
  waiting for transfers between devices  64.9 us (35%)
  starting transfers between devices  31.5 us (17%)
  blocking collectives  18 us (10%)
  local copies, waits for them, and re-layouts  3.8 us (2%)
  other arithmetic  3.28 us (2%)
    all_to_all x1, waiting for transfers between devices, local(): lax.all_to_all(soil_heat_field, 'x', split_axis=0, concat_axis=0, tiled=T...  46.8 us
    pallas_call x1, Pallas kernels, triangle_of(): pl.pallas_call(triangle_kernel, out_shape=jax.ShapeDtypeStruct((size, siz...  27.5 us
    pallas_call x1, Pallas kernels, orthonormal(): pl.pallas_call(orthonormal_kernel, out_shape=[jax.ShapeDtypeStruct(seed_r...  24.3 us
    ppermute x10, starting transfers between devices, exchanged(): return lax.ppermute(block, axis, [(i, i ^ bits) for i in range(count)])  23.1 us
    ppermute x10, waiting for transfers between devices, exchanged(): return lax.ppermute(block, axis, [(i, i ^ bits) for i in range(count)])  13.1 us
    all_to_all x1, blocking collectives, summed_over_devices(): lax.all_to_all(own.reshape(NB, half // NB, W), 'x', split_axis=0, concat_...  9.2 us
    all_gather x1, blocking collectives, summed_over_devices(): return lax.all_gather(whole, 'core', axis=0, tiled=True)  8.8 us
    pallas_call x1, Pallas kernels, core_parts(): pl.pallas_call(core_kernel, grid=(cells,), in_specs=[pl.BlockSpec(basis.s...  7.38 us
  transfers between devices with their start and end apart: 12, of which 8 were waited for; matrix products, arithmetic and copies ran while one was open for 0% of the time, Pallas kernels for 15%

profile of v1, /device:TPU:1, one launch (start us, length us, event | category | flops | bytes accessed | tf_op | source)
XLA Modules:
  0.0 187.7 jit_solution(2558773827101630221)
XLA Ops:
  0.6 4.9 %all-to-all-start = ((f32[32,256,128]{2,1,0:T(8,128)}), f32[32,256,128]{2,1,0:T(8,128)}, u32[]{:S(2)}, u32[]{:S(2)}) async-start(f32[32,256,128]{2,1,0:T(8,128)} %param.2), calls=%async_computation | async-start | bytes 8388608 | tf_op jit(solution)/shard_map/all_to_all | solution.py:294
  5.5 46.8 %all-to-all-done = f32[32,256,128]{2,1,0:T(8,128)} async-done(((f32[32,256,128]{2,1,0:T(8,128)}), f32[32,256,128]{2,1,0:T(8,128)}, u32[]{:S(2)}, u32[]{:S(2)}) %all-to-all-start) | async-done | bytes 4194336 | tf_op jit(solution)/shard_map/all_to_all | solution.py:294
  52.3 6.4 %gram_blocks.1 = f32[10,128,128]{2,1,0:T(8,128)} custom-call(f32[4,2048,128]{2,1,0:T(8,128)} %bitcast.refs_0_), custom_call_target="tpu_custom_call" | custom-call | flops 2147483648 | bytes 4194304 | tf_op jit(solution)/shard_map/gram_blocks/pallas_call | solution.py:53
  58.7 0.0 copy-start
  58.7 1.0 constant_dynamic-slice_fusion
  59.8 3.7 %collective-permute-start = (f32[640,128]{1,0:T(8,128)S(1)}, f32[640,128]{1,0:T(8,128)S(1)}, u32[]{:S(2)}, u32[]{:S(2)}) collective-permute-start(f32[640,128]{1,0:T(8,128)S(1)} %constant_dynamic-slice_fusion), channel_id=1, source_target_pairs={{0,1},{1,0},{2,3},{3,2},{4,5},{5,4},{6,7},{7,6},{8,9},{9,8},{10,11... | collective-permute-start | bytes 983048 | tf_op jit(solution)/shard_map/ppermute | solution.py:249
  63.4 1.3 collective-permute-done
  64.7 1.0 dynamic-slice_add_fusion
  65.7 9.2 %all_to_all.15 = f32[4,160,128]{2,1,0:T(8,128)S(1)} all-to-all(f32[4,160,128]{2,1,0:T(8,128)S(1)} %bitcast.39), channel_id=1, replica_groups=mesh['x'=4,'y'=4,'z'=8,'core'=2] {'x'}, dimensions={0} | all-to-all | bytes 655360 | tf_op jit(solution)/shard_map/all_to_all | solution.py:258
  74.9 1.6 collective-permute-start.1
  76.5 2.6 %collective-permute-start.2 = (f32[160,128]{1,0:T(8,128)S(1)}, f32[160,128]{1,0:T(8,128)S(1)}, u32[]{:S(2)}, u32[]{:S(2)}) collective-permute-start(f32[160,128]{1,0:T(8,128)S(1)} %fusion.1), channel_id=1, source_target_pairs={{0,32},{16,48},{32,0},{48,16},{1,33},{17,49},{33,1},{49,17},{2,34}... | collective-permute-start | bytes 245768 | tf_op jit(solution)/shard_map/ppermute | solution.py:249
  79.2 0.0 collective-permute-start.3
  79.2 0.0 collective-permute-done.1
  79.2 2.7 %collective-permute-done.2 = f32[160,128]{1,0:T(8,128)S(1)} collective-permute-done((f32[160,128]{1,0:T(8,128)S(1)}, f32[160,128]{1,0:T(8,128)S(1)}, u32[]{:S(2)}, u32[]{:S(2)}) %collective-permute-start.2) | collective-permute-done | bytes 81952 | tf_op jit(solution)/shard_map/ppermute | solution.py:249
  81.9 2.7 %collective-permute-done.3 = f32[160,128]{1,0:T(8,128)S(1)} collective-permute-done((f32[160,128]{1,0:T(8,128)S(1)}, f32[160,128]{1,0:T(8,128)S(1)}, u32[]{:S(2)}, u32[]{:S(2)}) %collective-permute-start.3) | collective-permute-done | bytes 81952 | tf_op jit(solution)/shard_map/ppermute | solution.py:249
  84.6 1.7 collective-permute-start.4
  86.3 1.8 collective-permute-done.4
  88.2 3.1 %collective-permute-start.5 = (f32[160,128]{1,0:T(8,128)S(1)}, f32[160,128]{1,0:T(8,128)S(1)}, u32[]{:S(2)}, u32[]{:S(2)}) collective-permute-start(f32[160,128]{1,0:T(8,128)S(1)} %add.64), channel_id=1, source_target_pairs={{0,4},{2,6},{4,0},{6,2},{8,12},{10,14},{12,8},{14,10},{1,5},{3,7},... | collective-permute-start | bytes 245768 | tf_op jit(solution)/shard_map/ppermute | solution.py:249
  91.2 1.8 collective-permute-done.5
  93.1 7.1 %collective-permute-start.6 = (f32[160,128]{1,0:T(8,128)S(1)}, f32[160,128]{1,0:T(8,128)S(1)}, u32[]{:S(2)}, u32[]{:S(2)}) collective-permute-start(f32[160,128]{1,0:T(8,128)S(1)} %add.65), channel_id=1, source_target_pairs={{0,8},{2,10},{4,12},{6,14},{8,0},{10,2},{12,4},{14,6},{1,9},{3,11}... | collective-permute-start | bytes 245768 | tf_op jit(solution)/shard_map/ppermute | solution.py:249
  100.1 2.8 %collective-permute-done.6 = f32[160,128]{1,0:T(8,128)S(1)} collective-permute-done((f32[160,128]{1,0:T(8,128)S(1)}, f32[160,128]{1,0:T(8,128)S(1)}, u32[]{:S(2)}, u32[]{:S(2)}) %collective-permute-start.6) | collective-permute-done | bytes 81952 | tf_op jit(solution)/shard_map/ppermute | solution.py:249
  102.9 0.7 broadcast_in_dim.2
  103.7 3.5 %all-to-all-start.2 = ((f32[4,160,128]{2,1,0:T(8,128)}), f32[4,160,128]{2,1,0:T(8,128)S(1)}, u32[]{:S(2)}, u32[]{:S(2)}) async-start(f32[4,160,128]{2,1,0:T(8,128)} %broadcast_in_dim.2), calls=%async_computation.2 | async-start | bytes 655360 | tf_op jit(solution)/shard_map/all_to_all | solution.py:267
  107.1 0.0 copy-done
  107.1 0.8 copy.5
  108.0 5.0 %all-to-all-done.2 = f32[4,160,128]{2,1,0:T(8,128)S(1)} async-done(((f32[4,160,128]{2,1,0:T(8,128)}), f32[4,160,128]{2,1,0:T(8,128)S(1)}, u32[]{:S(2)}, u32[]{:S(2)}) %all-to-all-start.2) | async-done | bytes 327712 | tf_op jit(solution)/shard_map/all_to_all | solution.py:267
  113.0 8.8 %all_gather.3 = f32[1280,128]{1,0:T(8,128)} all-gather(f32[640,128]{1,0:T(8,128)S(1)} %bitcast.40), channel_id=1, replica_groups=mesh['x'=4,'y'=4,'z'=8,'core'=2] {'core'}, dimensions={0}, use_global_device_ids=true | all-gather | bytes 983040 | tf_op jit(solution)/shard_map/all_gather | solution.py:269
  121.8 24.3 %orthonormal.1 = (f32[128,512]{1,0:T(8,128)}, f32[512,128]{1,0:T(8,128)}) custom-call(f32[10,128,128]{2,1,0:T(8,128)} %bitcast.44, f32[128,512]{1,0:T(8,128)} %bitcast.46), custom_call_target="tpu_custom_call" | custom-call | flops 40000000000 | bytes 1048576 | tf_op jit(solution)/shard_map/orthonormal/pallas_call | solution.py:153
  146.1 7.4 %core_parts.1 = f32[4,8,32,256]{3,2,1,0:T(8,128)} custom-call(f32[128,512]{1,0:T(8,128)} %get-tuple-element.5.basis_ref, f32[4,8,256,128]{3,2,1,0:T(8,128)} %bitcast.7.x_ref), custom_call_target="tpu_custom_call" | custom-call | flops 805306368 | bytes 5242880 | tf_op jit(solution)/shard_map/core_parts/pallas_call | solution.py:228
  153.4 1.2 dynamic-slice_bitcast_fusion
  154.6 1.0 collective-permute-start.7
  155.6 1.2 collective-permute-start.8
  156.8 1.2 collective-permute-start.9
  158.0 27.5 %triangle.1 = f32[512,512]{1,0:T(8,128)} custom-call(f32[10,128,128]{2,1,0:T(8,128)} %bitcast.45), custom_call_target="tpu_custom_call" | custom-call | flops 40000000000 | bytes 2097152 | tf_op jit(solution)/shard_map/triangle/pallas_call | solution.py:200
  185.5 0.0 collective-permute-done.7
  185.5 0.0 collective-permute-done.8
  185.5 0.0 collective-permute-done.9
  185.5 1.1 select_bitcast_fusion.3
  186.6 1.1 pad_maximum_fusion
  (5 shorter events, 0.1 us)
Async XLA Ops:
  0.6 51.7 %all-to-all-start = ((f32[32,256,128]{2,1,0:T(8,128)}), f32[32,256,128]{2,1,0:T(8,128)}, u32[]{:S(2)}, u32[]{:S(2)}) async-start(f32[32,256,128]{2,1,0:T(8,128)} %param.2), calls=%async_computation | async-start | bytes 8388608 | tf_op jit(solution)/shard_map/all_to_all | solution.py:294
  58.7 48.4 %copy-start = (f32[512,128]{1,0:T(8,128)S(1)}, f32[512,128]{1,0:T(8,128)}, u32[]{:S(2)}) copy-start(f32[512,128]{1,0:T(8,128)} %param.3) | copy-start | bytes 786436
  59.8 4.9 %collective-permute-start = (f32[640,128]{1,0:T(8,128)S(1)}, f32[640,128]{1,0:T(8,128)S(1)}, u32[]{:S(2)}, u32[]{:S(2)}) collective-permute-start(f32[640,128]{1,0:T(8,128)S(1)} %constant_dynamic-slice_fusion), channel_id=1, source_target_pairs={{0,1},{1,0},{2,3},{3,2},{4,5},{5,4},{6,7},{7,6},{8,9},{9,8},{10,11... | collective-permute-start | bytes 983048 | tf_op jit(solution)/shard_map/ppermute | solution.py:249
  74.9 4.2 %collective-permute-start.1 = (f32[160,128]{1,0:T(8,128)S(1)}, f32[160,128]{1,0:T(8,128)S(1)}, u32[]{:S(2)}, u32[]{:S(2)}) collective-permute-start(f32[160,128]{1,0:T(8,128)S(1)} %fusion.1), channel_id=1, source_target_pairs={{0,16},{16,0},{32,48},{48,32},{1,17},{17,1},{33,49},{49,33},{2,18}... | collective-permute-start | bytes 245768 | tf_op jit(solution)/shard_map/ppermute | solution.py:249
  76.5 5.3 %collective-permute-start.2 = (f32[160,128]{1,0:T(8,128)S(1)}, f32[160,128]{1,0:T(8,128)S(1)}, u32[]{:S(2)}, u32[]{:S(2)}) collective-permute-start(f32[160,128]{1,0:T(8,128)S(1)} %fusion.1), channel_id=1, source_target_pairs={{0,32},{16,48},{32,0},{48,16},{1,33},{17,49},{33,1},{49,17},{2,34}... | collective-permute-start | bytes 245768 | tf_op jit(solution)/shard_map/ppermute | solution.py:249
  79.2 5.4 %collective-permute-start.3 = (f32[160,128]{1,0:T(8,128)S(1)}, f32[160,128]{1,0:T(8,128)S(1)}, u32[]{:S(2)}, u32[]{:S(2)}) collective-permute-start(f32[160,128]{1,0:T(8,128)S(1)} %fusion.1), channel_id=1, source_target_pairs={{0,48},{16,32},{32,16},{48,0},{1,49},{17,33},{33,17},{49,1},{2,50}... | collective-permute-start | bytes 245768 | tf_op jit(solution)/shard_map/ppermute | solution.py:249
  84.6 3.6 %collective-permute-start.4 = (f32[160,128]{1,0:T(8,128)S(1)}, f32[160,128]{1,0:T(8,128)S(1)}, u32[]{:S(2)}, u32[]{:S(2)}) collective-permute-start(f32[160,128]{1,0:T(8,128)S(1)} %add_add_fusion), channel_id=1, source_target_pairs={{0,2},{2,0},{4,6},{6,4},{8,10},{10,8},{12,14},{14,12},{1,3},{3,1},... | collective-permute-start | bytes 245768 | tf_op jit(solution)/shard_map/ppermute | solution.py:249
  88.2 4.9 %collective-permute-start.5 = (f32[160,128]{1,0:T(8,128)S(1)}, f32[160,128]{1,0:T(8,128)S(1)}, u32[]{:S(2)}, u32[]{:S(2)}) collective-permute-start(f32[160,128]{1,0:T(8,128)S(1)} %add.64), channel_id=1, source_target_pairs={{0,4},{2,6},{4,0},{6,2},{8,12},{10,14},{12,8},{14,10},{1,5},{3,7},... | collective-permute-start | bytes 245768 | tf_op jit(solution)/shard_map/ppermute | solution.py:249
  93.1 9.8 %collective-permute-start.6 = (f32[160,128]{1,0:T(8,128)S(1)}, f32[160,128]{1,0:T(8,128)S(1)}, u32[]{:S(2)}, u32[]{:S(2)}) collective-permute-start(f32[160,128]{1,0:T(8,128)S(1)} %add.65), channel_id=1, source_target_pairs={{0,8},{2,10},{4,12},{6,14},{8,0},{10,2},{12,4},{14,6},{1,9},{3,11}... | collective-permute-start | bytes 245768 | tf_op jit(solution)/shard_map/ppermute | solution.py:249
  103.7 9.3 %all-to-all-start.2 = ((f32[4,160,128]{2,1,0:T(8,128)}), f32[4,160,128]{2,1,0:T(8,128)S(1)}, u32[]{:S(2)}, u32[]{:S(2)}) async-start(f32[4,160,128]{2,1,0:T(8,128)} %broadcast_in_dim.2), calls=%async_computation.2 | async-start | bytes 655360 | tf_op jit(solution)/shard_map/all_to_all | solution.py:267
  154.6 30.9 %collective-permute-start.7 = (f32[8,32,256]{2,1,0:T(8,128)S(1)}, f32[8,32,256]{2,1,0:T(8,128)S(1)}, u32[]{:S(2)}, u32[]{:S(2)}) collective-permute-start(f32[8,32,256]{2,1,0:T(8,128)S(1)} %get-tuple-element.13), channel_id=1, source_target_pairs={{0,192},{64,128},{128,64},{192,0},{1,193},{65,129},{129,65},{193,1... | collective-permute-start | bytes 786440 | tf_op jit(solution)/shard_map/ppermute | solution.py:249
  155.6 29.9 %collective-permute-start.8 = (f32[8,32,256]{2,1,0:T(8,128)S(1)}, f32[8,32,256]{2,1,0:T(8,128)S(1)}, u32[]{:S(2)}, u32[]{:S(2)}) collective-permute-start(f32[8,32,256]{2,1,0:T(8,128)S(1)} %get-tuple-element.12), channel_id=1, source_target_pairs={{0,128},{64,192},{128,0},{192,64},{1,129},{65,193},{129,1},{193,65... | collective-permute-start | bytes 786440 | tf_op jit(solution)/shard_map/ppermute | solution.py:249
  156.8 28.7 %collective-permute-start.9 = (f32[8,32,256]{2,1,0:T(8,128)S(1)}, f32[8,32,256]{2,1,0:T(8,128)S(1)}, u32[]{:S(2)}, u32[]{:S(2)}) collective-permute-start(f32[8,32,256]{2,1,0:T(8,128)S(1)} %get-tuple-element.11), channel_id=1, source_target_pairs={{0,64},{64,0},{128,192},{192,128},{1,65},{65,1},{129,193},{193,129... | collective-permute-start | bytes 786440 | tf_op jit(solution)/shard_map/ppermute | solution.py:249

commit v2 on v1

v2 whole, which is shorter than its diff:
```python
import jax
import jax.numpy as jnp
from jax import lax
from jax.experimental import pallas as pl
from jax.experimental.pallas import tpu as pltpu
from jax.sharding import Mesh, PartitionSpec as P

ITERS = 3
HIGHEST = lax.Precision.HIGHEST
NB = 4
W = 128
PAIRS = [(k, l) for k in range(NB) for l in range(k, NB)]
COUNTS = (3, 3, 2)
VMEM_LIMIT = 14 * 1024 * 1024


def split(x):
    high = x.astype(jnp.bfloat16)
    return high, (x - high.astype(jnp.float32)).astype(jnp.bfloat16)


def contract(a, b, dims):
    return lax.dot_general(a, b, (dims, ((), ())), preferred_element_type=jnp.float32)


def gram_kernel(scale, first, me_ref, *refs):
    pieces, refs = refs[:NB], refs[NB:]
    before, (out_ref, high_ref, low_ref, rows) = refs[:-4], refs[-4:]
    me = me_ref[0]
    for b, piece in enumerate(pieces):
        place = pl.multiple_of((me ^ b) * W, W)
        rows[:, pl.ds(place, W)] = piece[...].reshape(rows.shape[0], W)
    high, low = split(rows[...])
    high_ref[...] = high
    low_ref[...] = low
    left = high.T
    hh = contract(left, high, ((1,), (0,)))
    hl = contract(left, low, ((1,), (0,)))
    for n, (k, l) in enumerate(PAIRS):
        ks, ls = slice(W * k, W * k + W), slice(W * l, W * l + W)
        part = (hh[ks, ls] + (hl[ks, ls] + hl[ls, ks].T)) * scale
        out_ref[n] = part if first else before[0][n] + part


def gram_chunk(me, field, start, cells, arrived, before, scale):
    snaps = field.shape[2]
    rows = cells * snaps
    gram = jax.ShapeDtypeStruct((len(PAIRS), W, W), jnp.float32)
    halves = jax.ShapeDtypeStruct((rows, NB * W), jnp.bfloat16)
    whole = lambda shape: pl.BlockSpec(shape, lambda i, me: (0,) * len(shape))
    own = pl.BlockSpec(
        (pl.Squeezed(), pl.Element(cells), pl.Element(snaps), pl.Element(W)),
        lambda i, me: (me[0], start, 0, 0),
    )
    return pl.pallas_call(
        lambda *refs: gram_kernel(scale, before is None, *refs),
        grid_spec=pltpu.PrefetchScalarGridSpec(
            num_scalar_prefetch=1,
            grid=(1,),
            in_specs=[own]
            + [whole((cells, snaps, W))] * (NB - 1)
            + ([] if before is None else [whole(gram.shape)]),
            out_specs=[whole(gram.shape), whole(halves.shape), whole(halves.shape)],
            scratch_shapes=[pltpu.VMEM((rows, NB * W), jnp.float32)],
        ),
        out_shape=[gram, halves, halves],
        compiler_params=pltpu.CompilerParams(vmem_limit_bytes=VMEM_LIMIT),
        cost_estimate=pl.CostEstimate(
            flops=4 * rows * (NB * W) ** 2, bytes_accessed=8 * rows * NB * W, transcendentals=0
        ),
        name="gram_chunk",
    )(me, field, *arrived, *([] if before is None else [before]))


def reciprocal(d):
    r = pltpu.reciprocal(d, approx=True)
    return r * (2.0 - d * r)


def lanes(x, l):
    return jnp.broadcast_to(x[:, l : l + 1], (8, W))


def sublanes(x, i):
    return jnp.broadcast_to(x[i : i + 1, :], (8, W))


def factor(panels):
    count = len(panels)
    left = list(panels)
    sub = lax.broadcasted_iota(jnp.int32, (8, W), 0)
    lane = lax.broadcasted_iota(jnp.int32, (8, W), 1)
    right = [jnp.where(lane == sub + 8 * p, 1.0, 0.0).astype(jnp.float32) for p in range(count)]
    upper, inverse = [], []
    for p in range(count):
        rows0, rows1 = left[p], right[p]
        col = [lanes(rows0, 8 * p + j) for j in range(8)]
        s = {(i, j): sublanes(col[j], i) for j in range(8) for i in range(j, 8)}
        later = range(p + 1, count)
        cols = {q: [lanes(left[q], 8 * p + j) for j in range(8)] for q in later}
        for j in range(8):
            r = reciprocal(s[j, j])
            m = {i: s[i, j] * r for i in range(j + 1, 8)}
            for k in range(j + 1, 8):
                for i in range(k, 8):
                    s[i, k] = s[i, k] - m[i] * s[k, j]
            mine = jnp.where(sub > j, col[j] * r, 0.0)
            row0, row1 = sublanes(rows0, j), sublanes(rows1, j)
            for k in range(j + 1, 8):
                col[k] = col[k] - mine * s[k, j]
            rows0 = rows0 - mine * row0
            rows1 = rows1 - mine * row1
            for q in later:
                theirs = cols[q][j] * r
                for k in range(j + 1, 8):
                    cols[q][k] = cols[q][k] - theirs * s[k, j]
                left[q] = left[q] - theirs * row0
                right[q] = right[q] - theirs * row1
        pivots = s[0, 0]
        for i in range(1, 8):
            pivots = jnp.where(sub == i, s[i, i], pivots)
        scale = lax.rsqrt(pivots)
        upper.append(jnp.where(lane >= sub + 8 * p, rows0 * scale, 0.0))
        inverse.append(rows1 * scale)
    return upper, inverse


def panels_of(matrix):
    return [matrix[8 * p : 8 * p + 8, :] for p in range(matrix.shape[0] // 8)]


def exact(a, b, dims=((1,), (0,))):
    return lax.dot_general(
        a, b, (dims, ((), ())), precision=HIGHEST, preferred_element_type=jnp.float32
    )


def orthonormal_steps(g_ref, seed_ref, basis_ref, gram):
    for n, (k, l) in enumerate(PAIRS):
        block = g_ref[n]
        gram[W * k : W * k + W, W * l : W * l + W] = block
        if k != l:
            gram[W * l : W * l + W, W * k : W * k + W] = block.T
    basis_ref[...] = seed_ref[...]

    def step(_, carry):
        imaged = exact(basis_ref[...], gram[...])
        small = exact(imaged, imaged, ((1,), (1,)))
        _, inverse = factor(panels_of(small))
        basis_ref[...] = exact(jnp.concatenate(inverse, axis=0), imaged)
        return carry

    lax.fori_loop(0, ITERS, step, 0)


def triangle_steps(g_ref, out_ref, rest):
    out_ref[...] = jnp.zeros_like(out_ref)
    for n, (k, l) in enumerate(PAIRS):
        rest[W * k : W * k + W, W * l : W * l + W] = g_ref[n]

    def step(b, carry):
        start = pl.multiple_of(b * W, W)
        own = pl.ds(start, W)
        upper, inverse = factor([rest[pl.ds(start + 8 * p, 8), own] for p in range(W // 8)])
        inverse = jnp.concatenate(inverse, axis=0)

        @pl.when(b < NB - 1)
        def _():
            keep = lax.broadcasted_iota(jnp.int32, (W, NB * W), 1) >= (b + 1) * W
            row = jnp.where(keep, exact(inverse, rest[own, :]), 0.0)
            out_ref[own, :] = row

            def down(c, carry):
                at = pl.ds(pl.multiple_of(c * W, W), W)
                rest[at, :] -= exact(out_ref[own, at].T, out_ref[own, :])
                return carry

            lax.fori_loop(b + 1, NB, down, 0)

        out_ref[own, own] = jnp.concatenate(upper, axis=0)
        return carry

    lax.fori_loop(0, NB, step, 0)


def either_kernel(core_ref, g_ref, seed_ref, basis_ref, triangle_ref, gram):
    @pl.when(core_ref[0] == 0)
    def _():
        orthonormal_steps(g_ref, seed_ref, basis_ref, gram)

    @pl.when(core_ref[0] != 0)
    def _():
        triangle_steps(g_ref, triangle_ref, gram)


def basis_or_triangle(core, gram, seed_rows):
    size = NB * W
    vmem = pl.BlockSpec(memory_space=pltpu.VMEM)
    return pl.pallas_call(
        either_kernel,
        in_specs=[pl.BlockSpec(memory_space=pltpu.SMEM), vmem, vmem],
        out_specs=[vmem, vmem],
        out_shape=[
            jax.ShapeDtypeStruct(seed_rows.shape, jnp.float32),
            jax.ShapeDtypeStruct((size, size), jnp.float32),
        ],
        scratch_shapes=[pltpu.VMEM((size, size), jnp.float32)],
        compiler_params=pltpu.CompilerParams(vmem_limit_bytes=VMEM_LIMIT),
        cost_estimate=pl.CostEstimate(
            flops=40_000_000_000, bytes_accessed=8 * size * size, transcendentals=0
        ),
        name="basis_or_triangle",
    )(core, gram, seed_rows)


def core_kernel(counts, snaps, me_ref, own_ref, other_ref, *refs):
    halves, (mode_ref, *outs), basis = refs[: 2 * len(counts)], refs[2 * len(counts) : -1], refs[-1]
    me, part = me_ref[0], own_ref.shape[0] // NB
    basis[...] = jnp.where(me_ref[1] == 0, own_ref[...], other_ref[...])
    mode_ref[...] = basis[...].T
    turned = [basis[pl.ds(pl.multiple_of((me ^ b) * part, part), part), :] for b in range(NB)]
    high, low = split(jnp.concatenate(turned, axis=0).T)
    weights = jnp.concatenate([high, low], axis=1)
    cell = 0
    for c, count in enumerate(counts):
        high_ref, low_ref = halves[2 * c : 2 * c + 2]
        for i in range(count):
            rows = slice(snaps * i, snaps * i + snaps)
            both = contract(high_ref[rows, :], weights, ((1,), (0,)))
            more = contract(low_ref[rows, :], high, ((1,), (0,)))
            core = (both[:, :W] + (both[:, W:] + more)).T
            for b in range(NB):
                outs[b][cell] = core[part * b : part * b + part, :]
            cell += 1


def core_parts(place, own_basis, other_basis, halves, counts, snaps):
    rank, size = own_basis.shape
    cells = sum(counts)
    operands = [half for pair in halves for half in pair]
    vmem = pl.BlockSpec(memory_space=pltpu.VMEM)
    return pl.pallas_call(
        lambda *refs: core_kernel(counts, snaps, *refs),
        in_specs=[pl.BlockSpec(memory_space=pltpu.SMEM)] + [vmem] * (2 + len(operands)),
        out_specs=[vmem] * (1 + NB),
        out_shape=[jax.ShapeDtypeStruct((size, rank), jnp.float32)]
        + [jax.ShapeDtypeStruct((cells, rank // NB, snaps), jnp.float32)] * NB,
        scratch_shapes=[pltpu.VMEM((rank, size), jnp.float32)],
        compiler_params=pltpu.CompilerParams(vmem_limit_bytes=VMEM_LIMIT),
        cost_estimate=pl.CostEstimate(
            flops=6 * cells * snaps * size * rank,
            bytes_accessed=5 * cells * snaps * size,
            transcendentals=0,
        ),
        name="core_parts",
    )(place, own_basis, other_basis, *operands)


def placed_kernel(me_ref, *refs):
    parts, (out_ref, sems) = refs[:NB], refs[NB:]
    copies = [
        pltpu.make_async_copy(part, out_ref.at[me_ref[0] ^ b], sems.at[b])
        for b, part in enumerate(parts)
    ]
    for copy in copies:
        copy.start()
    for copy in copies:
        copy.wait()


def placed(me, parts):
    anywhere = pl.BlockSpec(memory_space=pl.ANY)
    return pl.pallas_call(
        placed_kernel,
        in_specs=[pl.BlockSpec(memory_space=pltpu.SMEM)] + [anywhere] * NB,
        out_specs=anywhere,
        out_shape=jax.ShapeDtypeStruct((NB, *parts[0].shape), jnp.float32),
        scratch_shapes=[pltpu.SemaphoreType.DMA((NB,))],
        name="placed",
    )(me, *parts)


def exchanged(block, axis, bits):
    count = lax.axis_size(axis)
    return lax.ppermute(block, axis, [(i, i ^ bits) for i in range(count)])


def summed_over_devices(part):
    axes = ("x", "core")
    count = lax.axis_size(axes)
    shares = lax.all_to_all(
        part.reshape(count, -1, W), axes, split_axis=0, concat_axis=0, tiled=True
    )
    own = shares.sum(axis=0)
    two, one, three = (exchanged(own, "y", bits) for bits in (2, 1, 3))
    own = (own + one) + (two + three)
    for bits in (1, 2, 4):
        own = own + exchanged(own, "z", bits)
    copies = jnp.broadcast_to(own[None], (count, *own.shape))
    whole = lax.all_to_all(copies, axes, split_axis=0, concat_axis=0, tiled=True)
    return whole.reshape(-1, W)


def local(soil_heat_field, seed_subspace):
    cells, snaps, width = soil_heat_field.shape
    devices = lax.axis_size(("x", "y", "z", "core"))
    me, core = lax.axis_index("x"), lax.axis_index("core")
    place = jnp.stack([me, core]).astype(jnp.int32)
    field = soil_heat_field.reshape(NB, cells // NB, snaps, width)
    scale = 1.0 / (cells // NB * snaps * devices)
    counts = COUNTS

    gram, halves, start = None, [], 0
    arrived = []
    for count in counts:
        got = {}
        for bits in (2, 1, 3):
            send = lax.dynamic_slice(
                field, (me ^ bits, start, 0, 0), (1, count, snaps, width)
            )[0]
            got[bits] = exchanged(send, "x", bits)
        arrived.append([got[bits] for bits in (1, 2, 3)])
        start += count
    start = 0
    for count, others in zip(counts, arrived):
        gram, high, low = gram_chunk(place, field, start, count, others, gram, scale)
        halves.append((high, low))
        start += count

    gram = summed_over_devices(gram.reshape(-1, W)).reshape(gram.shape)
    basis, triangle = basis_or_triangle(place[1:], gram, seed_subspace.T)
    other_basis = exchanged(basis, "core", 1)
    triangle, other_basis = lax.optimization_barrier((triangle, other_basis))
    other_triangle = exchanged(triangle, "core", 1)
    mode_factor, *parts = core_parts(place, basis, other_basis, halves, counts, snaps)
    sent = {bits: exchanged(parts[bits], "x", bits) for bits in (2, 1, 3)}
    triangle = jnp.where(core == 0, other_triangle, triangle)
    core_tensor = placed(place, [parts[0]] + [sent[bits] for bits in (1, 2, 3)])
    core_tensor = core_tensor.reshape(cells, -1, snaps).transpose(0, 2, 1)
    return (core_tensor, mode_factor, triangle)


def solution(mesh):
    fine = Mesh(mesh.devices.reshape(4, -1, 8, 2), ("x", "y", "z", "core"))
    cell = ("y", "z", "core")
    return jax.shard_map(
        local,
        mesh=fine,
        in_specs=(P(cell, None, "x"), P()),
        out_specs=(P(cell, None, "x"), P(), P()),
        check_vma=False,
    )
```

time: 188 us -> 204 us (1.085)
  local copies, waits for them, and re-layouts: 3.8 us -> 19.7 us
  starting transfers between devices: 31.5 us -> 40.6 us
  waiting for transfers between devices: 64.9 us -> 57 us
  Pallas kernels: 65.6 us -> 63.3 us
    all_to_all x2 -> x1, waiting for transfers between devices: 51.8 us -> 10.1 us  [summed_over_devices(): lax.all_to_all(copies, axes, split_axis=0, concat_axis=0, tiled=True)]
    ppermute x10 -> x20, waiting for transfers between devices: 13.1 us -> 46.9 us  [exchanged(): return lax.ppermute(block, axis, [(i, i ^ bits) for i in range(count)])]
    unnamed x3 -> x45, local copies, waits for them, and re-layouts: 0.84 us -> 15.1 us
    all_to_all x1, blocking collectives: 9.2 us -> 20 us  [summed_over_devices(): lax.all_to_all(part.reshape(count, -1, W), axes, split_axis=0, concat_axi...]
    all_gather x1 -> x0, blocking collectives: 8.8 us -> none  [summed_over_devices(): return lax.all_gather(whole, 'core', axis=0, tiled=True)]
    ppermute x10 -> x20, starting transfers between devices: 23.1 us -> 31.5 us  [exchanged(): return lax.ppermute(block, axis, [(i, i ^ bits) for i in range(count)])]
    squeeze x1 -> x2, local copies, waits for them, and re-layouts: 1.17 us -> 3.81 us  [local(): lax.dynamic_slice(field, (me ^ bits, start, 0, 0), (1, count, snaps, width))]
    pallas_call x4 -> x6, Pallas kernels: 65.6 us -> 63.3 us  [the longest x1 33.6 us: placed(): pl.pallas_call(placed_kernel, in_specs=[pl.BlockSpec(memory_space=pltpu.S...]
  transfers between devices with their start and end apart: 12 -> 21, of which waited for: 8 -> 12; matrix products, arithmetic and copies ran while one was open for 0% -> 1% of each run, Pallas kernels for 15% -> 20%
where the time goes in v2:
time: 204 us; the launch traced here: 203 us
  Pallas kernels  63.3 us (31%)
  waiting for transfers between devices  57 us (28%)
  starting transfers between devices  40.6 us (20%)
  blocking collectives  20 us (10%)
  local copies, waits for them, and re-layouts  19.7 us (10%)
    ppermute x20, waiting for transfers between devices, exchanged(): return lax.ppermute(block, axis, [(i, i ^ bits) for i in range(count)])  46.9 us
    pallas_call x1, Pallas kernels, placed(): pl.pallas_call(placed_kernel, in_specs=[pl.BlockSpec(memory_space=pltpu.S...  33.6 us
    ppermute x20, starting transfers between devices, exchanged(): return lax.ppermute(block, axis, [(i, i ^ bits) for i in range(count)])  31.5 us
    pallas_call x1, Pallas kernels, basis_or_triangle(): pl.pallas_call(either_kernel, in_specs=[pl.BlockSpec(memory_space=pltpu.S...  21.4 us
    all_to_all x1, blocking collectives, summed_over_devices(): lax.all_to_all(part.reshape(count, -1, W), axes, split_axis=0, concat_axi...  20 us
    unnamed x45, local copies, waits for them, and re-layouts  15.1 us
    all_to_all x1, waiting for transfers between devices, summed_over_devices(): lax.all_to_all(copies, axes, split_axis=0, concat_axis=0, tiled=True)  10.1 us
    all_to_all x1, starting transfers between devices, summed_over_devices(): lax.all_to_all(copies, axes, split_axis=0, concat_axis=0, tiled=True)  9.07 us
  transfers between devices with their start and end apart: 21, of which 12 were waited for; matrix products, arithmetic and copies ran while one was open for 1% of the time, Pallas kernels for 20%

profile of v2, /device:TPU:1, one launch (start us, length us, event | category | flops | bytes accessed | tf_op | source)
XLA Modules:
  0.0 202.8 jit_solution(1290483815427647868)
XLA Ops:
  0.7 2.7 %dynamic-slice_bitcast_fusion = (f32[3,256,128]{2,1,0:T(8,128)S(1)}, f32[3,256,128]{2,1,0:T(8,128)}, f32[3,256,128]{2,1,0:T(8,128)S(1)}, f32[3,256,128]{2,1,0:T(...) fusion(f32[4,8,256,128]{3,2,1,0:T(8,128)} %bitcast.27, s32[]{:T(128)S(6)} %select_n.25, s32[]{:T(128)S(6)} %select_n.24, ...), kind=kLoop, calls=%fused_computation.1 | loop fusion | bytes 4718604 | tf_op jit(solution)/shard_map/squeeze | solution.py:318
  3.3 3.3 %collective-permute-start.8 = (f32[3,256,128]{2,1,0:T(8,128)S(1)}, f32[3,256,128]{2,1,0:T(8,128)S(1)}, u32[]{:S(2)}, u32[]{:S(2)}) collective-permute-start(f32[3,256,128]{2,1,0:T(8,128)S(1)} %get-tuple-element.39), channel_id=1, source_target_pairs={{0,192},{64,128},{128,64},{192,0},{1,193},{65,129},{129,65},{193,1... | collective-permute-start | bytes 1179656 | tf_op jit(solution)/shard_map/ppermute | solution.py:285
  6.6 0.5 collective-permute-start.7
  7.1 0.1 collective-permute-start.6
  7.2 2.7 %collective-permute-start.5 = (f32[3,256,128]{2,1,0:T(8,128)S(1)}, f32[3,256,128]{2,1,0:T(8,128)S(1)}, u32[]{:S(2)}, u32[]{:S(2)}) collective-permute-start(f32[3,256,128]{2,1,0:T(8,128)S(1)} %get-tuple-element.42), channel_id=1, source_target_pairs={{0,192},{64,128},{128,64},{192,0},{1,193},{65,129},{129,65},{193,1... | collective-permute-start | bytes 1179656 | tf_op jit(solution)/shard_map/ppermute | solution.py:285
  9.9 0.5 collective-permute-start.4
  10.4 14.7 %collective-permute-done.8.refs_4_ = f32[3,256,128]{2,1,0:T(8,128)S(1)} collective-permute-done((f32[3,256,128]{2,1,0:T(8,128)S(1)}, f32[3,256,128]{2,1,0:T(8,128)S(1)}, u32[]{:S(2)}, u32[]{:S(2)}) %collective-permute-start.8) | collective-permute-done | bytes 393248 | tf_op jit(solution)/shard_map/ppermute | solution.py:285
  25.0 0.0 collective-permute-start.3
  25.0 1.2 dynamic-slice_bitcast_fusion.6
  26.2 0.0 collective-permute-done.7.refs_3_
  26.2 0.7 copy-done.11
  27.0 3.9 %collective-permute-start.2 = (f32[2,256,128]{2,1,0:T(8,128)S(1)}, f32[2,256,128]{2,1,0:T(8,128)S(1)}, u32[]{:S(2)}, u32[]{:S(2)}) collective-permute-start(f32[2,256,128]{2,1,0:T(8,128)S(1)} %get-tuple-element.45), channel_id=1, source_target_pairs={{0,192},{64,128},{128,64},{192,0},{1,193},{65,129},{129,65},{193,1... | collective-permute-start | bytes 786440 | tf_op jit(solution)/shard_map/ppermute | solution.py:285
  30.9 0.7 copy-done.13
  31.6 1.2 collective-permute-start.1
  32.8 9.1 %collective-permute-done.5.refs_4_ = f32[3,256,128]{2,1,0:T(8,128)S(1)} collective-permute-done((f32[3,256,128]{2,1,0:T(8,128)S(1)}, f32[3,256,128]{2,1,0:T(8,128)S(1)}, u32[]{:S(2)}, u32[]{:S(2)}) %collective-permute-start.5) | collective-permute-done | bytes 393248 | tf_op jit(solution)/shard_map/ppermute | solution.py:285
  41.9 0.1 pad_add_fusion.refs_0_.me_ref
  41.9 2.2 %copy-done = f32[32,256,128]{2,1,0:T(8,128)S(1)} copy-done((f32[32,256,128]{2,1,0:T(8,128)S(1)}, f32[32,256,128]{2,1,0:T(8,128)}, u32[]{:S(2)}) %copy-start) | copy-done | bytes 4194328
  44.1 1.0 copy-done.12
  45.1 1.0 copy-done.14
  46.1 1.9 gram_chunk.3
  48.1 0.0 copy-start.9
  48.1 0.7 copy-done.9
  48.8 1.0 copy-done.10
  49.8 1.9 gram_chunk.4
  51.7 0.0 copy-start.1
  51.7 0.9 copy-done.1
  52.6 0.0 copy-start.21
  52.6 1.6 gram_chunk.5
  54.2 0.8 copy-done.5
  55.0 0.8 copy-done.7
  55.9 20.0 %all_to_all.10 = f32[8,160,128]{2,1,0:T(8,128)S(1)} all-to-all(f32[8,160,128]{2,1,0:T(8,128)S(1)} %bitcast.33), channel_id=1, replica_groups=mesh['x'=4,'y'=4,'z'=8,'core'=2] {'x','core'}, dimensions={0} | all-to-all | bytes 1310720 | tf_op jit(solution)/shard_map/all_to_all | solution.py:291
  75.8 1.6 collective-permute-start.11
  77.5 0.3 collective-permute-start.10
  77.8 1.4 collective-permute-start.9
  79.2 1.2 collective-permute-done.11
  80.4 1.9 collective-permute-done.10
  82.4 1.6 collective-permute-start.12
  84.0 1.8 collective-permute-done.12
  85.9 3.1 %collective-permute-start.13 = (f32[160,128]{1,0:T(8,128)S(1)}, f32[160,128]{1,0:T(8,128)S(1)}, u32[]{:S(2)}, u32[]{:S(2)}) collective-permute-start(f32[160,128]{1,0:T(8,128)S(1)} %add.39), channel_id=1, source_target_pairs={{0,4},{2,6},{4,0},{6,2},{8,12},{10,14},{12,8},{14,10},{1,5},{3,7},... | collective-permute-start | bytes 245768 | tf_op jit(solution)/shard_map/ppermute | solution.py:285
  89.0 1.8 collective-permute-done.13
  90.8 7.3 %collective-permute-start.14 = (f32[160,128]{1,0:T(8,128)S(1)}, f32[160,128]{1,0:T(8,128)S(1)}, u32[]{:S(2)}, u32[]{:S(2)}) collective-permute-start(f32[160,128]{1,0:T(8,128)S(1)} %add.40), channel_id=1, source_target_pairs={{0,8},{2,10},{4,12},{6,14},{8,0},{10,2},{12,4},{14,6},{1,9},{3,11}... | collective-permute-start | bytes 245768 | tf_op jit(solution)/shard_map/ppermute | solution.py:285
  98.0 2.7 %collective-permute-done.14 = f32[160,128]{1,0:T(8,128)S(1)} collective-permute-done((f32[160,128]{1,0:T(8,128)S(1)}, f32[160,128]{1,0:T(8,128)S(1)}, u32[]{:S(2)}, u32[]{:S(2)}) %collective-permute-start.14) | collective-permute-done | bytes 81952 | tf_op jit(solution)/shard_map/ppermute | solution.py:285
  100.8 0.9 broadcast_in_dim.2
  101.6 9.1 %all-to-all-start.1 = ((f32[8,160,128]{2,1,0:T(8,128)}), f32[8,160,128]{2,1,0:T(8,128)S(1)}, u32[]{:S(2)}, u32[]{:S(2)}) async-start(f32[8,160,128]{2,1,0:T(8,128)} %broadcast_in_dim.2), calls=%async_computation.1 | async-start | bytes 1310720 | tf_op jit(solution)/shard_map/all_to_all | solution.py:300
  110.7 0.8 copy.5
  111.5 10.1 %all-to-all-done.1 = f32[8,160,128]{2,1,0:T(8,128)S(1)} async-done(((f32[8,160,128]{2,1,0:T(8,128)}), f32[8,160,128]{2,1,0:T(8,128)S(1)}, u32[]{:S(2)}, u32[]{:S(2)}) %all-to-all-start.1) | async-done | bytes 655392 | tf_op jit(solution)/shard_map/all_to_all | solution.py:300
  121.6 0.8 copy-done.3
  122.5 1.1 copy-done.4
  123.5 0.9 copy-done.16
  124.5 21.4 %basis_or_triangle.1 = (f32[128,512]{1,0:T(8,128)S(1)}, f32[512,512]{1,0:T(8,128)S(1)}) custom-call(s32[1]{0:T(128)} %bitcast.1.core_ref, f32[10,128,128]{2,1,0:T(8,128)S(1)} %bitcast.32, f32[128,512]{1,0:T(8,128)S(1)} %bitcast.34), custom_call_target="tpu_custom_call" | custom-call | flops 40000000000 | bytes 2097152 | tf_op jit(solution)/shard_map/basis_or_triangle/pallas_call | solution.py:199
  145.9 0.1 collective-permute-start.15
  146.0 1.5 collective-permute-done.15.refs_2_
  147.6 0.1 collective-permute-start.19
  147.7 2.9 %core_parts.1 = (f32[512,128]{1,0:T(8,128)}, f32[8,32,256]{2,1,0:T(8,128)S(1)}, f32[8,32,256]{2,1,0:T(8,128)}, f32[8,32,256]{2,1,0:T(8,128)}, f32[8,32,256]{2,1,0:T(8,128)}) custom-call(s32[2]{0:T(128)S(1)} %pad_add_fusion.refs_0_.me_ref, f32[128,512]{1,0:T(8,128)S(1)} %get-tuple-element.24.refs_1_, f32[128,512]{1,0:T(8,128)S(1)} %collective-permute-done.15.refs_2_, ...), custom_call_target="tpu_custom_call" | custom-call | flops 805306368 | bytes 5242880 | tf_op jit(solution)/shard_map/core_parts/pallas_call | solution.py:242
  150.6 0.7 copy-done.15
  151.3 0.3 collective-permute-start.16
  151.6 1.8 collective-permute-start.17
  153.4 1.8 collective-permute-start.18
  155.2 3.9 %collective-permute-done.16.refs_1_ = f32[8,32,256]{2,1,0:T(8,128)S(1)} collective-permute-done((f32[8,32,256]{2,1,0:T(8,128)}, f32[8,32,256]{2,1,0:T(8,128)S(1)}, u32[]{:S(2)}, u32[]{:S(2)}) %collective-permute-start.16) | collective-permute-done | bytes 262176 | tf_op jit(solution)/shard_map/ppermute | solution.py:285
  159.0 6.2 %collective-permute-done.17.refs_2_ = f32[8,32,256]{2,1,0:T(8,128)S(1)} collective-permute-done((f32[8,32,256]{2,1,0:T(8,128)}, f32[8,32,256]{2,1,0:T(8,128)S(1)}, u32[]{:S(2)}, u32[]{:S(2)}) %collective-permute-start.17) | collective-permute-done | bytes 262176 | tf_op jit(solution)/shard_map/ppermute | solution.py:285
  165.3 2.0 collective-permute-done.18.refs_3_
  167.3 0.7 copy-done.20
  168.0 33.6 %placed.1 = f32[4,8,32,256]{3,2,1,0:T(8,128)} custom-call(s32[2]{0:T(128)} %copy-done.17, f32[8,32,256]{2,1,0:T(8,128)} %copy-done.15, f32[8,32,256]{2,1,0:T(8,128)} %copy-done.18, f32[8,32,256]{2,1,0:T(8,128)} %copy-done.19, f32[8,32,256]{2,1,0:T(8,128)} %copy-done.20), custom_call_target="tpu_custom_call" | custom-call | tf_op jit(solution)/shard_map/placed/pallas_call | solution.py:273
  201.6 1.2 broadcast_select_fusion
  (40 shorter events, 0.2 us)
Async XLA Ops:
  3.3 21.7 %collective-permute-start.8 = (f32[3,256,128]{2,1,0:T(8,128)S(1)}, f32[3,256,128]{2,1,0:T(8,128)S(1)}, u32[]{:S(2)}, u32[]{:S(2)}) collective-permute-start(f32[3,256,128]{2,1,0:T(8,128)S(1)} %get-tuple-element.39), channel_id=1, source_target_pairs={{0,192},{64,128},{128,64},{192,0},{1,193},{65,129},{129,65},{193,1... | collective-permute-start | bytes 1179656 | tf_op jit(solution)/shard_map/ppermute | solution.py:285
  6.6 19.6 %collective-permute-start.7 = (f32[3,256,128]{2,1,0:T(8,128)}, f32[3,256,128]{2,1,0:T(8,128)S(1)}, u32[]{:S(2)}, u32[]{:S(2)}) collective-permute-start(f32[3,256,128]{2,1,0:T(8,128)} %get-tuple-element.40), channel_id=1, source_target_pairs={{0,128},{64,192},{128,0},{192,64},{1,129},{65,193},{129,1},{193,65... | collective-permute-start | bytes 1179656 | tf_op jit(solution)/shard_map/ppermute | solution.py:285
  7.1 23.7 %collective-permute-start.6 = (f32[3,256,128]{2,1,0:T(8,128)S(1)}, f32[3,256,128]{2,1,0:T(8,128)S(1)}, u32[]{:S(2)}, u32[]{:S(2)}) collective-permute-start(f32[3,256,128]{2,1,0:T(8,128)S(1)} %get-tuple-element.41), channel_id=1, source_target_pairs={{0,64},{64,0},{128,192},{192,128},{1,65},{65,1},{129,193},{193,129... | collective-permute-start | bytes 1179656 | tf_op jit(solution)/shard_map/ppermute | solution.py:285
  7.2 34.7 %collective-permute-start.5 = (f32[3,256,128]{2,1,0:T(8,128)S(1)}, f32[3,256,128]{2,1,0:T(8,128)S(1)}, u32[]{:S(2)}, u32[]{:S(2)}) collective-permute-start(f32[3,256,128]{2,1,0:T(8,128)S(1)} %get-tuple-element.42), channel_id=1, source_target_pairs={{0,192},{64,128},{128,64},{192,0},{1,193},{65,129},{129,65},{193,1... | collective-permute-start | bytes 1179656 | tf_op jit(solution)/shard_map/ppermute | solution.py:285
  9.9 38.2 %collective-permute-start.4 = (f32[3,256,128]{2,1,0:T(8,128)}, f32[3,256,128]{2,1,0:T(8,128)S(1)}, u32[]{:S(2)}, u32[]{:S(2)}) collective-permute-start(f32[3,256,128]{2,1,0:T(8,128)} %get-tuple-element.43), channel_id=1, source_target_pairs={{0,128},{64,192},{128,0},{192,64},{1,129},{65,193},{129,1},{193,65... | collective-permute-start | bytes 1179656 | tf_op jit(solution)/shard_map/ppermute | solution.py:285
  25.0 23.0 %collective-permute-start.3 = (f32[3,256,128]{2,1,0:T(8,128)S(1)}, f32[3,256,128]{2,1,0:T(8,128)S(1)}, u32[]{:S(2)}, u32[]{:S(2)}) collective-permute-start(f32[3,256,128]{2,1,0:T(8,128)S(1)} %get-tuple-element.44), channel_id=1, source_target_pairs={{0,64},{64,0},{128,192},{192,128},{1,65},{65,1},{129,193},{193,129... | collective-permute-start | bytes 1179656 | tf_op jit(solution)/shard_map/ppermute | solution.py:285
  26.2 0.7 copy-start.11
  27.0 25.7 %collective-permute-start.2 = (f32[2,256,128]{2,1,0:T(8,128)S(1)}, f32[2,256,128]{2,1,0:T(8,128)S(1)}, u32[]{:S(2)}, u32[]{:S(2)}) collective-permute-start(f32[2,256,128]{2,1,0:T(8,128)S(1)} %get-tuple-element.45), channel_id=1, source_target_pairs={{0,192},{64,128},{128,64},{192,0},{1,193},{65,129},{129,65},{193,1... | collective-permute-start | bytes 786440 | tf_op jit(solution)/shard_map/ppermute | solution.py:285
  30.9 0.7 copy-start.13
  31.6 21.0 %collective-permute-start.1 = (f32[2,256,128]{2,1,0:T(8,128)S(1)}, f32[2,256,128]{2,1,0:T(8,128)S(1)}, u32[]{:S(2)}, u32[]{:S(2)}) collective-permute-start(f32[2,256,128]{2,1,0:T(8,128)S(1)} %get-tuple-element.46), channel_id=1, source_target_pairs={{0,128},{64,192},{128,0},{192,64},{1,129},{65,193},{129,1},{193,65... | collective-permute-start | bytes 786440 | tf_op jit(solution)/shard_map/ppermute | solution.py:285
  41.8 10.8 %collective-permute-start = (f32[2,256,128]{2,1,0:T(8,128)S(1)}, f32[2,256,128]{2,1,0:T(8,128)S(1)}, u32[]{:S(2)}, u32[]{:S(2)}) collective-permute-start(f32[2,256,128]{2,1,0:T(8,128)S(1)} %get-tuple-element.47), channel_id=1, source_target_pairs={{0,64},{64,0},{128,192},{192,128},{1,65},{65,1},{129,193},{193,129... | collective-permute-start | bytes 786440 | tf_op jit(solution)/shard_map/ppermute | solution.py:285
  41.9 2.2 %copy-start = (f32[32,256,128]{2,1,0:T(8,128)S(1)}, f32[32,256,128]{2,1,0:T(8,128)}, u32[]{:S(2)}) copy-start(f32[32,256,128]{2,1,0:T(8,128)} %param.2) | copy-start | bytes 12582916
  44.1 1.0 copy-start.12
  45.1 1.0 copy-start.14
  46.1 101.6 %copy-start.17 = (s32[2]{0:T(128)}, s32[2]{0:T(128)S(1)}, u32[]{:S(2)}) copy-start(s32[2]{0:T(128)S(1)} %pad_add_fusion.refs_0_.me_ref) | copy-start | bytes 28
  48.1 0.7 copy-start.9
  48.8 1.0 copy-start.10
  51.7 0.9 copy-start.1
  52.6 58.1 %copy-start.21 = (f32[512,128]{1,0:T(8,128)S(1)}, f32[512,128]{1,0:T(8,128)}, u32[]{:S(2)}) copy-start(f32[512,128]{1,0:T(8,128)} %param.3) | copy-start | bytes 786436
  54.2 0.8 copy-start.5
  55.0 0.8 copy-start.7
  75.8 4.6 %collective-permute-start.11 = (f32[160,128]{1,0:T(8,128)S(1)}, f32[160,128]{1,0:T(8,128)S(1)}, u32[]{:S(2)}, u32[]{:S(2)}) collective-permute-start(f32[160,128]{1,0:T(8,128)S(1)} %reduce_sum.9), channel_id=1, source_target_pairs={{0,48},{16,32},{32,16},{48,0},{1,49},{17,33},{33,17},{49,1},{2,50}... | collective-permute-start | bytes 245768 | tf_op jit(solution)/shard_map/ppermute | solution.py:285
  77.5 4.9 %collective-permute-start.10 = (f32[160,128]{1,0:T(8,128)S(1)}, f32[160,128]{1,0:T(8,128)S(1)}, u32[]{:S(2)}, u32[]{:S(2)}) collective-permute-start(f32[160,128]{1,0:T(8,128)S(1)} %reduce_sum.9), channel_id=1, source_target_pairs={{0,32},{16,48},{32,0},{48,16},{1,33},{17,49},{33,1},{49,17},{2,34}... | collective-permute-start | bytes 245768 | tf_op jit(solution)/shard_map/ppermute | solution.py:285
  77.8 4.6 %collective-permute-start.9 = (f32[160,128]{1,0:T(8,128)S(1)}, f32[160,128]{1,0:T(8,128)S(1)}, u32[]{:S(2)}, u32[]{:S(2)}) collective-permute-start(f32[160,128]{1,0:T(8,128)S(1)} %reduce_sum.9), channel_id=1, source_target_pairs={{0,16},{16,0},{32,48},{48,32},{1,17},{17,1},{33,49},{49,33},{2,18}... | collective-permute-start | bytes 245768 | tf_op jit(solution)/shard_map/ppermute | solution.py:285
  82.4 3.5 %collective-permute-start.12 = (f32[160,128]{1,0:T(8,128)S(1)}, f32[160,128]{1,0:T(8,128)S(1)}, u32[]{:S(2)}, u32[]{:S(2)}) collective-permute-start(f32[160,128]{1,0:T(8,128)S(1)} %add_add_fusion), channel_id=1, source_target_pairs={{0,2},{2,0},{4,6},{6,4},{8,10},{10,8},{12,14},{14,12},{1,3},{3,1},... | collective-permute-start | bytes 245768 | tf_op jit(solution)/shard_map/ppermute | solution.py:285
  85.9 4.9 %collective-permute-start.13 = (f32[160,128]{1,0:T(8,128)S(1)}, f32[160,128]{1,0:T(8,128)S(1)}, u32[]{:S(2)}, u32[]{:S(2)}) collective-permute-start(f32[160,128]{1,0:T(8,128)S(1)} %add.39), channel_id=1, source_target_pairs={{0,4},{2,6},{4,0},{6,2},{8,12},{10,14},{12,8},{14,10},{1,5},{3,7},... | collective-permute-start | bytes 245768 | tf_op jit(solution)/shard_map/ppermute | solution.py:285
  90.8 9.9 %collective-permute-start.14 = (f32[160,128]{1,0:T(8,128)S(1)}, f32[160,128]{1,0:T(8,128)S(1)}, u32[]{:S(2)}, u32[]{:S(2)}) collective-permute-start(f32[160,128]{1,0:T(8,128)S(1)} %add.40), channel_id=1, source_target_pairs={{0,8},{2,10},{4,12},{6,14},{8,0},{10,2},{12,4},{14,6},{1,9},{3,11}... | collective-permute-start | bytes 245768 | tf_op jit(solution)/shard_map/ppermute | solution.py:285
  101.6 20.0 %all-to-all-start.1 = ((f32[8,160,128]{2,1,0:T(8,128)}), f32[8,160,128]{2,1,0:T(8,128)S(1)}, u32[]{:S(2)}, u32[]{:S(2)}) async-start(f32[8,160,128]{2,1,0:T(8,128)} %broadcast_in_dim.2), calls=%async_computation.1 | async-start | bytes 1310720 | tf_op jit(solution)/shard_map/all_to_all | solution.py:300
  121.6 0.8 copy-start.3
  122.5 1.1 copy-start.4
  123.5 0.9 copy-start.16
  124.5 23.2 %copy-start.2 = (bf16[768,512]{1,0:T(8,128)(2,1)S(1)}, bf16[768,512]{1,0:T(8,128)(2,1)}, u32[]{:S(2)}) copy-start(bf16[768,512]{1,0:T(8,128)(2,1)} %copy-done.1) | copy-start | bytes 2359300
  124.5 23.2 %copy-start.6 = (bf16[512,512]{1,0:T(8,128)(2,1)S(1)}, bf16[512,512]{1,0:T(8,128)(2,1)}, u32[]{:S(2)}) copy-start(bf16[512,512]{1,0:T(8,128)(2,1)} %copy-done.5) | copy-start | bytes 1572868
  124.5 23.2 %copy-start.8 = (bf16[512,512]{1,0:T(8,128)(2,1)S(1)}, bf16[512,512]{1,0:T(8,128)(2,1)}, u32[]{:S(2)}) copy-start(bf16[512,512]{1,0:T(8,128)(2,1)} %copy-done.7) | copy-start | bytes 1572868
  145.9 1.6 collective-permute-start.15
  147.6 54.0 %collective-permute-start.19 = (f32[512,512]{1,0:T(8,128)S(1)}, f32[512,512]{1,0:T(8,128)}, u32[]{:S(2)}, u32[]{:S(2)}) collective-permute-start(f32[512,512]{1,0:T(8,128)S(1)} %get-tuple-element.38), channel_id=1, source_target_pairs={{0,1},{1,0},{2,3},{3,2},{4,5},{5,4},{6,7},{7,6},{8,9},{9,8},{10,11... | collective-permute-start | bytes 3145736 | tf_op jit(solution)/shard_map/ppermute | solution.py:285
  150.6 0.7 copy-start.15
  151.3 7.7 %collective-permute-start.16 = (f32[8,32,256]{2,1,0:T(8,128)}, f32[8,32,256]{2,1,0:T(8,128)S(1)}, u32[]{:S(2)}, u32[]{:S(2)}) collective-permute-start(f32[8,32,256]{2,1,0:T(8,128)} %get-tuple-element.34), channel_id=1, source_target_pairs={{0,64},{64,0},{128,192},{192,128},{1,65},{65,1},{129,193},{193,129... | collective-permute-start | bytes 786440 | tf_op jit(solution)/shard_map/ppermute | solution.py:285
  151.6 13.7 %collective-permute-start.17 = (f32[8,32,256]{2,1,0:T(8,128)}, f32[8,32,256]{2,1,0:T(8,128)S(1)}, u32[]{:S(2)}, u32[]{:S(2)}) collective-permute-start(f32[8,32,256]{2,1,0:T(8,128)} %get-tuple-element.35), channel_id=1, source_target_pairs={{0,128},{64,192},{128,0},{192,64},{1,129},{65,193},{129,1},{193,65... | collective-permute-start | bytes 786440 | tf_op jit(solution)/shard_map/ppermute | solution.py:285
  153.4 13.9 %collective-permute-start.18 = (f32[8,32,256]{2,1,0:T(8,128)}, f32[8,32,256]{2,1,0:T(8,128)S(1)}, u32[]{:S(2)}, u32[]{:S(2)}) collective-permute-start(f32[8,32,256]{2,1,0:T(8,128)} %get-tuple-element.36), channel_id=1, source_target_pairs={{0,192},{64,128},{128,64},{192,0},{1,193},{65,129},{129,65},{193,1... | collective-permute-start | bytes 786440 | tf_op jit(solution)/shard_map/ppermute | solution.py:285
  159.0 8.2 %copy-start.18 = (f32[8,32,256]{2,1,0:T(8,128)}, f32[8,32,256]{2,1,0:T(8,128)S(1)}, u32[]{:S(2)}) copy-start(f32[8,32,256]{2,1,0:T(8,128)S(1)} %collective-permute-done.16.refs_1_) | copy-start | bytes 786436
  165.3 2.0 copy-start.19
  167.3 0.7 copy-start.20

commit v3 on v2

--- a/solution.py
+++ b/solution.py
@@ -11,7 +11,7 @@
 W = 128
 PAIRS = [(k, l) for k in range(NB) for l in range(k, NB)]
 COUNTS = (3, 3, 2)
-VMEM_LIMIT = 14 * 1024 * 1024
+VMEM_LIMIT = 60 * 1024 * 1024
 
 
 def split(x):
@@ -23,53 +23,66 @@
     return lax.dot_general(a, b, (dims, ((), ())), preferred_element_type=jnp.float32)
 
 
-def gram_kernel(scale, first, me_ref, *refs):
-    pieces, refs = refs[:NB], refs[NB:]
-    before, (out_ref, high_ref, low_ref, rows) = refs[:-4], refs[-4:]
+def gram_kernel(scale, start, me_ref, field, *refs):
+    others, refs = refs[: NB - 1], refs[NB - 1 :]
+    before, (out_ref, high_ref, low_ref, rows, high, low, total, sems) = refs[:-8], refs[-8:]
+    cells, snaps, size = rows.shape
     me = me_ref[0]
-    for b, piece in enumerate(pieces):
+    copies = []
+    for b, piece in enumerate((field.at[me, pl.ds(start, cells)], *others)):
         place = pl.multiple_of((me ^ b) * W, W)
-        rows[:, pl.ds(place, W)] = piece[...].reshape(rows.shape[0], W)
-    high, low = split(rows[...])
-    high_ref[...] = high
-    low_ref[...] = low
-    left = high.T
-    hh = contract(left, high, ((1,), (0,)))
-    hl = contract(left, low, ((1,), (0,)))
+        copies.append(pltpu.make_async_copy(piece, rows.at[:, :, pl.ds(place, W)], sems.at[b]))
+    if before:
+        copies.append(pltpu.make_async_copy(before[0], total, sems.at[NB]))
+    for copy in copies:
+        copy.start()
+    for copy in copies:
+        copy.wait()
+    high[...], low[...] = split(rows[...].reshape(cells * snaps, size))
+    halves = [
+        pltpu.make_async_copy(high, high_ref, sems.at[NB + 1]),
+        pltpu.make_async_copy(low, low_ref, sems.at[NB + 2]),
+    ]
+    for copy in halves:
+        copy.start()
+    left = high[...].T
+    hh = contract(left, high[...], ((1,), (0,)))
+    hl = contract(left, low[...], ((1,), (0,)))
     for n, (k, l) in enumerate(PAIRS):
         ks, ls = slice(W * k, W * k + W), slice(W * l, W * l + W)
         part = (hh[ks, ls] + (hl[ks, ls] + hl[ls, ks].T)) * scale
-        out_ref[n] = part if first else before[0][n] + part
+        total[n] = total[n] + part if before else part
+    result = pltpu.make_async_copy(total, out_ref, sems.at[NB + 3])
+    result.start()
+    for copy in (*halves, result):
+        copy.wait()
 
 
 def gram_chunk(me, field, start, cells, arrived, before, scale):
     snaps = field.shape[2]
     rows = cells * snaps
-    gram = jax.ShapeDtypeStruct((len(PAIRS), W, W), jnp.float32)
+    gram = (len(PAIRS), W, W)
     halves = jax.ShapeDtypeStruct((rows, NB * W), jnp.bfloat16)
-    whole = lambda shape: pl.BlockSpec(shape, lambda i, me: (0,) * len(shape))
-    own = pl.BlockSpec(
-        (pl.Squeezed(), pl.Element(cells), pl.Element(snaps), pl.Element(W)),
-        lambda i, me: (me[0], start, 0, 0),
-    )
+    anywhere = pl.BlockSpec(memory_space=pl.ANY)
+    operands = [field, *arrived] + ([] if before is None else [before])
     return pl.pallas_call(
-        lambda *refs: gram_kernel(scale, before is None, *refs),
-        grid_spec=pltpu.PrefetchScalarGridSpec(
-            num_scalar_prefetch=1,
-            grid=(1,),
-            in_specs=[own]
-            + [whole((cells, snaps, W))] * (NB - 1)
-            + ([] if before is None else [whole(gram.shape)]),
-            out_specs=[whole(gram.shape), whole(halves.shape), whole(halves.shape)],
-            scratch_shapes=[pltpu.VMEM((rows, NB * W), jnp.float32)],
-        ),
-        out_shape=[gram, halves, halves],
+        lambda *refs: gram_kernel(scale, start, *refs),
+        in_specs=[pl.BlockSpec(memory_space=pltpu.SMEM)] + [anywhere] * len(operands),
+        out_specs=[anywhere] * 3,
+        out_shape=[jax.ShapeDtypeStruct(gram, jnp.float32), halves, halves],
+        scratch_shapes=[
+            pltpu.VMEM((cells, snaps, NB * W), jnp.float32),
+            pltpu.VMEM(halves.shape, jnp.bfloat16),
+            pltpu.VMEM(halves.shape, jnp.bfloat16),
+            pltpu.VMEM(gram, jnp.float32),
+            pltpu.SemaphoreType.DMA((NB + 4,)),
+        ],
         compiler_params=pltpu.CompilerParams(vmem_limit_bytes=VMEM_LIMIT),
         cost_estimate=pl.CostEstimate(
             flops=4 * rows * (NB * W) ** 2, bytes_accessed=8 * rows * NB * W, transcendentals=0
         ),
         name="gram_chunk",
-    )(me, field, *arrived, *([] if before is None else [before]))
+    )(me, *operands)
 
 
 def reciprocal(d):
@@ -141,7 +154,7 @@
         gram[W * k : W * k + W, W * l : W * l + W] = block
         if k != l:
             gram[W * l : W * l + W, W * k : W * k + W] = block.T
-    basis_ref[...] = seed_ref[...]
+    basis_ref[...] = seed_ref[...].T
 
     def step(_, carry):
         imaged = exact(basis_ref[...], gram[...])
@@ -183,69 +196,124 @@
     lax.fori_loop(0, NB, step, 0)
 
 
-def either_kernel(core_ref, g_ref, seed_ref, basis_ref, triangle_ref, gram):
+def copied(*copies):
+    for copy in copies:
+        copy.start()
+    for copy in copies:
+        copy.wait()
+
+
+def either_kernel(core_ref, g_ref, seed_ref, basis_ref, triangle_ref, gram, blocks, seed, basis, triangle, sems):
+    copied(
+        pltpu.make_async_copy(g_ref, blocks, sems.at[0]),
+        pltpu.make_async_copy(seed_ref, seed, sems.at[1]),
+    )
+
     @pl.when(core_ref[0] == 0)
     def _():
-        orthonormal_steps(g_ref, seed_ref, basis_ref, gram)
+        orthonormal_steps(blocks, seed, basis, gram)
+        copied(pltpu.make_async_copy(basis, basis_ref, sems.at[2]))
 
     @pl.when(core_ref[0] != 0)
     def _():
-        triangle_steps(g_ref, triangle_ref, gram)
-
-
-def basis_or_triangle(core, gram, seed_rows):
+        triangle_steps(blocks, triangle, gram)
+        copied(pltpu.make_async_copy(triangle, triangle_ref, sems.at[3]))
+
+
+def basis_or_triangle(core, gram, seed):
     size = NB * W
-    vmem = pl.BlockSpec(memory_space=pltpu.VMEM)
+    anywhere = pl.BlockSpec(memory_space=pl.ANY)
     return pl.pallas_call(
         either_kernel,
-        in_specs=[pl.BlockSpec(memory_space=pltpu.SMEM), vmem, vmem],
-        out_specs=[vmem, vmem],
+        in_specs=[pl.BlockSpec(memory_space=pltpu.SMEM), anywhere, anywhere],
+        out_specs=[anywhere, anywhere],
         out_shape=[
-            jax.ShapeDtypeStruct(seed_rows.shape, jnp.float32),
+            jax.ShapeDtypeStruct(seed.shape[::-1], jnp.float32),
             jax.ShapeDtypeStruct((size, size), jnp.float32),
         ],
-        scratch_shapes=[pltpu.VMEM((size, size), jnp.float32)],
+        scratch_shapes=[
+            pltpu.VMEM((size, size), jnp.float32),
+            pltpu.VMEM(gram.shape, jnp.float32),
+            pltpu.VMEM(seed.shape, jnp.float32),
+            pltpu.VMEM(seed.shape[::-1], jnp.float32),
+            pltpu.VMEM((size, size), jnp.float32),
+            pltpu.SemaphoreType.DMA((4,)),
+        ],
         compiler_params=pltpu.CompilerParams(vmem_limit_bytes=VMEM_LIMIT),
         cost_estimate=pl.CostEstimate(
             flops=40_000_000_000, bytes_accessed=8 * size * size, transcendentals=0
         ),
         name="basis_or_triangle",
-    )(core, gram, seed_rows)
+    )(core, gram, seed)
 
 
 def core_kernel(counts, snaps, me_ref, own_ref, other_ref, *refs):
-    halves, (mode_ref, *outs), basis = refs[: 2 * len(counts)], refs[2 * len(counts) : -1], refs[-1]
-    me, part = me_ref[0], own_ref.shape[0] // NB
-    basis[...] = jnp.where(me_ref[1] == 0, own_ref[...], other_ref[...])
-    mode_ref[...] = basis[...].T
+    n = 2 * len(counts)
+    sources, refs = refs[:n], refs[n:]
+    mode_ref, *out_refs = refs[: 1 + NB]
+    refs = refs[1 + NB :]
+    halves, (basis, mode, parts, in_sems, out_sems) = refs[:n], refs[n:]
+    me, part = me_ref[0], basis.shape[0] // NB
+    arrivals = [
+        pltpu.make_async_copy(source, half, in_sems.at[i])
+        for i, (source, half) in enumerate(zip(sources, halves))
+    ]
+
+    @pl.when(me_ref[1] == 0)
+    def _():
+        copied(pltpu.make_async_copy(own_ref, basis, in_sems.at[n]))
+
+    @pl.when(me_ref[1] != 0)
+    def _():
+        copied(pltpu.make_async_copy(other_ref, basis, in_sems.at[n]))
+
+    for copy in arrivals:
+        copy.start()
+    mode[...] = basis[...].T
+    leaving = [pltpu.make_async_copy(mode, mode_ref, out_sems.at[NB])]
+    leaving[0].start()
     turned = [basis[pl.ds(pl.multiple_of((me ^ b) * part, part), part), :] for b in range(NB)]
     high, low = split(jnp.concatenate(turned, axis=0).T)
     weights = jnp.concatenate([high, low], axis=1)
     cell = 0
     for c, count in enumerate(counts):
         high_ref, low_ref = halves[2 * c : 2 * c + 2]
+        arrivals[2 * c].wait()
+        arrivals[2 * c + 1].wait()
         for i in range(count):
             rows = slice(snaps * i, snaps * i + snaps)
             both = contract(high_ref[rows, :], weights, ((1,), (0,)))
             more = contract(low_ref[rows, :], high, ((1,), (0,)))
             core = (both[:, :W] + (both[:, W:] + more)).T
             for b in range(NB):
-                outs[b][cell] = core[part * b : part * b + part, :]
+                parts[b, cell] = core[part * b : part * b + part, :]
             cell += 1
+    for b in range(NB):
+        leaving.append(pltpu.make_async_copy(parts.at[b], out_refs[b], out_sems.at[b]))
+        leaving[-1].start()
+    for copy in leaving:
+        copy.wait()
 
 
 def core_parts(place, own_basis, other_basis, halves, counts, snaps):
     rank, size = own_basis.shape
     cells = sum(counts)
     operands = [half for pair in halves for half in pair]
-    vmem = pl.BlockSpec(memory_space=pltpu.VMEM)
+    anywhere = pl.BlockSpec(memory_space=pl.ANY)
     return pl.pallas_call(
         lambda *refs: core_kernel(counts, snaps, *refs),
-        in_specs=[pl.BlockSpec(memory_space=pltpu.SMEM)] + [vmem] * (2 + len(operands)),
-        out_specs=[vmem] * (1 + NB),
+        in_specs=[pl.BlockSpec(memory_space=pltpu.SMEM)] + [anywhere] * (2 + len(operands)),
+        out_specs=[anywhere] * (1 + NB),
         out_shape=[jax.ShapeDtypeStruct((size, rank), jnp.float32)]
         + [jax.ShapeDtypeStruct((cells, rank // NB, snaps), jnp.float32)] * NB,
-        scratch_shapes=[pltpu.VMEM((rank, size), jnp.float32)],
+        scratch_shapes=[pltpu.VMEM(half.shape, half.dtype) for half in operands]
+        + [
+            pltpu.VMEM((rank, size), jnp.float32),
+            pltpu.VMEM((size, rank), jnp.float32),
+            pltpu.VMEM((NB, cells, rank // NB, snaps), jnp.float32),
+            pltpu.SemaphoreType.DMA((len(operands) + 1,)),
+            pltpu.SemaphoreType.DMA((NB + 1,)),
+        ],
         compiler_params=pltpu.CompilerParams(vmem_limit_bytes=VMEM_LIMIT),
         cost_estimate=pl.CostEstimate(
             flops=6 * cells * snaps * size * rank,
@@ -257,14 +325,20 @@
 
 
 def placed_kernel(me_ref, *refs):
-    parts, (out_ref, sems) = refs[:NB], refs[NB:]
-    copies = [
-        pltpu.make_async_copy(part, out_ref.at[me_ref[0] ^ b], sems.at[b])
-        for b, part in enumerate(parts)
+    parts, (out_ref, held, sems) = refs[:NB], refs[NB:]
+    arrivals = [
+        pltpu.make_async_copy(part, held.at[b], sems.at[b]) for b, part in enumerate(parts)
     ]
-    for copy in copies:
-        copy.start()
-    for copy in copies:
+    leaving = [
+        pltpu.make_async_copy(held.at[b], out_ref.at[me_ref[0] ^ b], sems.at[NB + b])
+        for b in range(NB)
+    ]
+    for copy in arrivals:
+        copy.start()
+    for arrival, copy in zip(arrivals, leaving):
+        arrival.wait()
+        copy.start()
+    for copy in leaving:
         copy.wait()
 
 
@@ -275,7 +349,11 @@
         in_specs=[pl.BlockSpec(memory_space=pltpu.SMEM)] + [anywhere] * NB,
         out_specs=anywhere,
         out_shape=jax.ShapeDtypeStruct((NB, *parts[0].shape), jnp.float32),
-        scratch_shapes=[pltpu.SemaphoreType.DMA((NB,))],
+        scratch_shapes=[
+            pltpu.VMEM((NB, *parts[0].shape), jnp.float32),
+            pltpu.SemaphoreType.DMA((2 * NB,)),
+        ],
+        compiler_params=pltpu.CompilerParams(vmem_limit_bytes=VMEM_LIMIT // 6),
         name="placed",
     )(me, *parts)
 
@@ -286,19 +364,24 @@
 
 
 def summed_over_devices(part):
-    axes = ("x", "core")
-    count = lax.axis_size(axes)
+    half = part.shape[0] // 2
+    core = lax.axis_index("core")
+    keep = lax.dynamic_slice_in_dim(part, core * half, half, 0)
+    send = lax.dynamic_slice_in_dim(part, (1 - core) * half, half, 0)
+    own = keep + exchanged(send, "core", 1)
     shares = lax.all_to_all(
-        part.reshape(count, -1, W), axes, split_axis=0, concat_axis=0, tiled=True
+        own.reshape(NB, half // NB, W), "x", split_axis=0, concat_axis=0, tiled=True
     )
-    own = shares.sum(axis=0)
+    own = (shares[0] + shares[1]) + (shares[2] + shares[3])
     two, one, three = (exchanged(own, "y", bits) for bits in (2, 1, 3))
     own = (own + one) + (two + three)
-    for bits in (1, 2, 4):
-        own = own + exchanged(own, "z", bits)
-    copies = jnp.broadcast_to(own[None], (count, *own.shape))
-    whole = lax.all_to_all(copies, axes, split_axis=0, concat_axis=0, tiled=True)
-    return whole.reshape(-1, W)
+    own = own + exchanged(own, "z", 1)
+    four, two, six = (exchanged(own, "z", bits) for bits in (4, 2, 6))
+    own = (own + two) + (four + six)
+    copies = jnp.broadcast_to(own[None], (NB, *own.shape))
+    whole = lax.all_to_all(copies, "x", split_axis=0, concat_axis=0, tiled=True)
+    whole = whole.reshape(half, W)
+    return lax.all_gather(whole, "core", axis=0, tiled=True)
 
 
 def local(soil_heat_field, seed_subspace):
@@ -311,14 +394,16 @@
     counts = COUNTS
 
     gram, halves, start = None, [], 0
-    arrived = []
+    arrived, later = [], field
     for count in counts:
-        got = {}
+        got, sends = {}, []
         for bits in (2, 1, 3):
             send = lax.dynamic_slice(
-                field, (me ^ bits, start, 0, 0), (1, count, snaps, width)
+                later, (me ^ bits, start, 0, 0), (1, count, snaps, width)
             )[0]
             got[bits] = exchanged(send, "x", bits)
+            sends.append(send)
+        later, *_ = lax.optimization_barrier((later, *sends))
         arrived.append([got[bits] for bits in (1, 2, 3)])
         start += count
     start = 0
@@ -328,14 +413,15 @@
         start += count
 
     gram = summed_over_devices(gram.reshape(-1, W)).reshape(gram.shape)
-    basis, triangle = basis_or_triangle(place[1:], gram, seed_subspace.T)
+    basis, triangle = basis_or_triangle(place[1:], gram, seed_subspace)
     other_basis = exchanged(basis, "core", 1)
     triangle, other_basis = lax.optimization_barrier((triangle, other_basis))
     other_triangle = exchanged(triangle, "core", 1)
     mode_factor, *parts = core_parts(place, basis, other_basis, halves, counts, snaps)
     sent = {bits: exchanged(parts[bits], "x", bits) for bits in (2, 1, 3)}
     triangle = jnp.where(core == 0, other_triangle, triangle)
-    core_tensor = placed(place, [parts[0]] + [sent[bits] for bits in (1, 2, 3)])
+    own_part, triangle = lax.optimization_barrier((parts[0], triangle))
+    core_tensor = placed(place, [own_part] + [sent[bits] for bits in (1, 2, 3)])
     core_tensor = core_tensor.reshape(cells, -1, snaps).transpose(0, 2, 1)
     return (core_tensor, mode_factor, triangle)
 

time: 204 us -> 165 us (0.81)
  Pallas kernels: 63.3 us -> 43.5 us
  local copies, waits for them, and re-layouts: 19.7 us -> 8.5 us
  waiting for transfers between devices: 57 us -> 46 us
  blocking collectives: 20 us -> 26.2 us
  starting transfers between devices: 40.6 us -> 36.1 us
    pallas_call x1, Pallas kernels: 33.6 us -> 1.65 us  [placed(): pl.pallas_call(placed_kernel, in_specs=[pl.BlockSpec(memory_space=pltpu.S...]
    unnamed x45 -> x22, local copies, waits for them, and re-layouts: 15.1 us -> 2.99 us
    all_to_all x1 -> x0, waiting for transfers between devices: 10.1 us -> none  [summed_over_devices(): lax.all_to_all(copies, axes, split_axis=0, concat_axis=0, tiled=True)]
    all_to_all x1 -> x0, starting transfers between devices: 9.07 us -> none  [summed_over_devices(): lax.all_to_all(copies, axes, split_axis=0, concat_axis=0, tiled=True)]
    all_gather x0 -> x1, blocking collectives: none -> 8.36 us  [summed_over_devices(): return lax.all_gather(whole, 'core', axis=0, tiled=True)]
    pallas_call x3, Pallas kernels: 5.42 us -> 12.2 us  [gram_chunk(): pl.pallas_call(lambda *refs: gram_kernel(scale, start, *refs), in_specs=[...]
    ppermute x20 -> x22, starting transfers between devices: 31.5 us -> 36.1 us  [exchanged(): return lax.ppermute(block, axis, [(i, i ^ bits) for i in range(count)])]
    pallas_call x1, Pallas kernels: 2.87 us -> 6 us  [core_parts(): pl.pallas_call(lambda *refs: core_kernel(counts, snaps, *refs), in_specs=...]
  transfers between devices with their start and end apart: 21 -> 22, of which waited for: 12 -> 15; matrix products, arithmetic and copies ran while one was open for 1% -> 3% of each run, Pallas kernels for 20% -> 9%
where the time goes in v3:
time: 165 us; the launch traced here: 164 us
  waiting for transfers between devices  46 us (28%)
  Pallas kernels  43.5 us (26%)
  starting transfers between devices  36.1 us (22%)
  blocking collectives  26.2 us (16%)
  local copies, waits for them, and re-layouts  8.5 us (5%)
  other arithmetic  2.9 us (2%)
    ppermute x22, waiting for transfers between devices, exchanged(): return lax.ppermute(block, axis, [(i, i ^ bits) for i in range(count)])  46 us
    ppermute x22, starting transfers between devices, exchanged(): return lax.ppermute(block, axis, [(i, i ^ bits) for i in range(count)])  36.1 us
    pallas_call x1, Pallas kernels, basis_or_triangle(): pl.pallas_call(either_kernel, in_specs=[pl.BlockSpec(memory_space=pltpu.S...  23.6 us
    pallas_call x3, Pallas kernels, gram_chunk(): pl.pallas_call(lambda *refs: gram_kernel(scale, start, *refs), in_specs=[...  12.2 us
    all_to_all x1, blocking collectives, summed_over_devices(): lax.all_to_all(own.reshape(NB, half // NB, W), 'x', split_axis=0, concat_...  9.54 us
    all_gather x1, blocking collectives, summed_over_devices(): return lax.all_gather(whole, 'core', axis=0, tiled=True)  8.36 us
    all_to_all x1, blocking collectives, summed_over_devices(): whole = lax.all_to_all(copies, 'x', split_axis=0, concat_axis=0, tiled=True)  8.25 us
    pallas_call x1, Pallas kernels, core_parts(): pl.pallas_call(lambda *refs: core_kernel(counts, snaps, *refs), in_specs=...  6 us
  transfers between devices with their start and end apart: 22, of which 15 were waited for; matrix products, arithmetic and copies ran while one was open for 3% of the time, Pallas kernels for 9%

profile of v3, /device:TPU:1, one launch (start us, length us, event | category | flops | bytes accessed | tf_op | source)
XLA Modules:
  0.0 164.1 jit_solution(12555004729249291737)
XLA Ops:
  0.7 1.3 dynamic-slice_bitcast_fusion.3
  2.0 3.4 %collective-permute-start.8 = (f32[3,256,128]{2,1,0:T(8,128)S(1)}, f32[3,256,128]{2,1,0:T(8,128)S(1)}, u32[]{:S(2)}, u32[]{:S(2)}) collective-permute-start(f32[3,256,128]{2,1,0:T(8,128)S(1)} %get-tuple-element.53), channel_id=1, source_target_pairs={{0,192},{64,128},{128,64},{192,0},{1,193},{65,129},{129,65},{193,1... | collective-permute-start | bytes 1179656 | tf_op jit(solution)/shard_map/ppermute | solution.py:363
  5.4 0.0 collective-permute-start.6
  5.4 1.3 collective-permute-start.7
  6.7 1.3 dynamic-slice_bitcast_fusion
  8.0 2.7 %collective-permute-start.5 = (f32[3,256,128]{2,1,0:T(8,128)S(1)}, f32[3,256,128]{2,1,0:T(8,128)S(1)}, u32[]{:S(2)}, u32[]{:S(2)}) collective-permute-start(f32[3,256,128]{2,1,0:T(8,128)S(1)} %get-tuple-element.50), channel_id=1, source_target_pairs={{0,192},{64,128},{128,64},{192,0},{1,193},{65,129},{129,65},{193,1... | collective-permute-start | bytes 1179656 | tf_op jit(solution)/shard_map/ppermute | solution.py:363
  10.6 0.0 collective-permute-start.3
  10.6 2.5 %collective-permute-done.8.refs_4_ = f32[3,256,128]{2,1,0:T(8,128)S(1)} collective-permute-done((f32[3,256,128]{2,1,0:T(8,128)S(1)}, f32[3,256,128]{2,1,0:T(8,128)S(1)}, u32[]{:S(2)}, u32[]{:S(2)}) %collective-permute-start.8) | collective-permute-done | bytes 393248 | tf_op jit(solution)/shard_map/ppermute | solution.py:363
  13.2 2.6 %collective-permute-start.4 = (f32[3,256,128]{2,1,0:T(8,128)S(1)}, f32[3,256,128]{2,1,0:T(8,128)S(1)}, u32[]{:S(2)}, u32[]{:S(2)}) collective-permute-start(f32[3,256,128]{2,1,0:T(8,128)S(1)} %get-tuple-element.52), channel_id=1, source_target_pairs={{0,128},{64,192},{128,0},{192,64},{1,129},{65,193},{129,1},{193,65... | collective-permute-start | bytes 1179656 | tf_op jit(solution)/shard_map/ppermute | solution.py:363
  15.7 1.9 %dynamic-slice_bitcast_fusion.6 = (f32[2,256,128]{2,1,0:T(8,128)}, f32[2,256,128]{2,1,0:T(8,128)S(1)}, f32[2,256,128]{2,1,0:T(8,128)S(1)}) fusion(f32[4,8,256,128]{3,2,1,0:T(8,128)} %bitcast.34, s32[]{:T(128)S(6)} %select_n.31, s32[]{:T(128)S(6)} %select_n.29, s32[]{:T(128)S(6)} %select_n.30), kind=kLoop, calls=%fused_computation.8 | loop fusion | bytes 1572876 | tf_op jit(solution)/shard_map/squeeze | solution.py:401
  17.6 0.0 collective-permute-done.6.refs_2_
  17.6 1.0 collective-permute-start.2
  18.6 3.0 %collective-permute-done.7.refs_3_ = f32[3,256,128]{2,1,0:T(8,128)} collective-permute-done((f32[3,256,128]{2,1,0:T(8,128)S(1)}, f32[3,256,128]{2,1,0:T(8,128)}, u32[]{:S(2)}, u32[]{:S(2)}) %collective-permute-start.7) | collective-permute-done | bytes 393248 | tf_op jit(solution)/shard_map/ppermute | solution.py:363
  21.6 3.6 %collective-permute-start.1 = (f32[2,256,128]{2,1,0:T(8,128)S(1)}, f32[2,256,128]{2,1,0:T(8,128)S(1)}, u32[]{:S(2)}, u32[]{:S(2)}) collective-permute-start(f32[2,256,128]{2,1,0:T(8,128)S(1)} %get-tuple-element.48), channel_id=1, source_target_pairs={{0,128},{64,192},{128,0},{192,64},{1,129},{65,193},{129,1},{193,65... | collective-permute-start | bytes 786440 | tf_op jit(solution)/shard_map/ppermute | solution.py:363
  25.2 4.8 %collective-permute-done.5.refs_4_ = f32[3,256,128]{2,1,0:T(8,128)S(1)} collective-permute-done((f32[3,256,128]{2,1,0:T(8,128)S(1)}, f32[3,256,128]{2,1,0:T(8,128)S(1)}, u32[]{:S(2)}, u32[]{:S(2)}) %collective-permute-start.5) | collective-permute-done | bytes 393248 | tf_op jit(solution)/shard_map/ppermute | solution.py:363
  30.0 0.9 collective-permute-start
  30.9 0.6 pad_add_fusion.refs_0_.me_ref
  31.6 4.1 %gram_chunk.3 = (f32[10,128,128]{2,1,0:T(8,128)}, bf16[768,512]{1,0:T(8,128)(2,1)}, bf16[768,512]{1,0:T(8,128)(2,1)}) custom-call(s32[2]{0:T(128)} %pad_add_fusion.refs_0_.me_ref, f32[4,8,256,128]{3,2,1,0:T(8,128)} %bitcast.35, f32[3,256,128]{2,1,0:T(8,128)} %collective-permute-done.6.refs_2_, f32[3,256,128]{2,1,0:T(8,128)} %collective-permute-done.7.refs_3_, ...), custom_call_target="tpu_custom_call" | custom-call | flops 805306368 | bytes 3145728 | tf_op jit(solution)/shard_map/gram_chunk/pallas_call | solution.py:68
  35.7 0.0 collective-permute-done.3.refs_2_
  35.7 2.7 %collective-permute-done.4.refs_3_ = f32[3,256,128]{2,1,0:T(8,128)S(1)} collective-permute-done((f32[3,256,128]{2,1,0:T(8,128)S(1)}, f32[3,256,128]{2,1,0:T(8,128)S(1)}, u32[]{:S(2)}, u32[]{:S(2)}) %collective-permute-start.4) | collective-permute-done | bytes 393248 | tf_op jit(solution)/shard_map/ppermute | solution.py:363
  38.4 0.7 copy-done.5
  39.1 4.3 %gram_chunk.4 = (f32[10,128,128]{2,1,0:T(8,128)}, bf16[768,512]{1,0:T(8,128)(2,1)}, bf16[768,512]{1,0:T(8,128)(2,1)}) custom-call(s32[2]{0:T(128)} %pad_add_fusion.refs_0_.me_ref, f32[4,8,256,128]{3,2,1,0:T(8,128)} %bitcast.36, f32[3,256,128]{2,1,0:T(8,128)} %copy-done.4, f32[3,256,128]{2,1,0:T(8,128)} %copy-done.5, f32[3,256,128]{2,1,0:T(8,128)} %copy-done.3, ...), custom_call_target="tpu_custom_call" | custom-call | flops 805306368 | bytes 3145728 | tf_op jit(solution)/shard_map/gram_chunk/pallas_call | solution.py:68
  43.4 6.4 %collective-permute-done.2.refs_4_ = f32[2,256,128]{2,1,0:T(8,128)S(1)} collective-permute-done((f32[2,256,128]{2,1,0:T(8,128)}, f32[2,256,128]{2,1,0:T(8,128)S(1)}, u32[]{:S(2)}, u32[]{:S(2)}) %collective-permute-start.2) | collective-permute-done | bytes 262176 | tf_op jit(solution)/shard_map/ppermute | solution.py:363
  49.8 0.5 collective-permute-done.refs_2_
  50.3 0.2 copy-done.7
  50.5 0.1 copy-done.8
  50.6 0.4 copy-done.9
  51.0 3.9 %gram_chunk.5 = (f32[10,128,128]{2,1,0:T(8,128)}, bf16[512,512]{1,0:T(8,128)(2,1)}, bf16[512,512]{1,0:T(8,128)(2,1)}) custom-call(s32[2]{0:T(128)} %pad_add_fusion.refs_0_.me_ref, f32[4,8,256,128]{3,2,1,0:T(8,128)} %bitcast.37, f32[2,256,128]{2,1,0:T(8,128)} %copy-done.9, f32[2,256,128]{2,1,0:T(8,128)} %copy-done.8, f32[2,256,128]{2,1,0:T(8,128)} %copy-done.7, ...), custom_call_target="tpu_custom_call" | custom-call | flops 536870912 | bytes 2097152 | tf_op jit(solution)/shard_map/gram_chunk/pallas_call | solution.py:68
  54.9 1.0 constant_dynamic-slice_fusion
  55.9 7.3 %collective-permute-start.9 = (f32[640,128]{1,0:T(8,128)S(1)}, f32[640,128]{1,0:T(8,128)S(1)}, u32[]{:S(2)}, u32[]{:S(2)}) collective-permute-start(f32[640,128]{1,0:T(8,128)S(1)} %constant_dynamic-slice_fusion), channel_id=1, source_target_pairs={{0,1},{1,0},{2,3},{3,2},{4,5},{5,4},{6,7},{7,6},{8,9},{9,8},{10,11... | collective-permute-start | bytes 983048 | tf_op jit(solution)/shard_map/ppermute | solution.py:363
  63.2 1.3 collective-permute-done.9
  64.4 1.0 dynamic-slice_add_fusion
  65.4 9.5 %all_to_all.10 = f32[4,160,128]{2,1,0:T(8,128)S(1)} all-to-all(f32[4,160,128]{2,1,0:T(8,128)S(1)} %bitcast.38), channel_id=1, replica_groups=mesh['x'=4,'y'=4,'z'=8,'core'=2] {'x'}, dimensions={0} | all-to-all | bytes 655360 | tf_op jit(solution)/shard_map/all_to_all | solution.py:372
  75.0 0.1 collective-permute-start.11
  75.1 0.1 collective-permute-start.12
  75.2 2.5 %collective-permute-start.10 = (f32[160,128]{1,0:T(8,128)S(1)}, f32[160,128]{1,0:T(8,128)S(1)}, u32[]{:S(2)}, u32[]{:S(2)}) collective-permute-start(f32[160,128]{1,0:T(8,128)S(1)} %fusion.1), channel_id=1, source_target_pairs={{0,16},{16,0},{32,48},{48,32},{1,17},{17,1},{33,49},{49,33},{2,18}... | collective-permute-start | bytes 245768 | tf_op jit(solution)/shard_map/ppermute | solution.py:363
  77.7 2.3 %collective-permute-done.11 = f32[160,128]{1,0:T(8,128)S(1)} collective-permute-done((f32[160,128]{1,0:T(8,128)S(1)}, f32[160,128]{1,0:T(8,128)S(1)}, u32[]{:S(2)}, u32[]{:S(2)}) %collective-permute-start.11) | collective-permute-done | bytes 81952 | tf_op jit(solution)/shard_map/ppermute | solution.py:363
  80.0 0.6 collective-permute-done.12
  80.6 0.0 collective-permute-done.10
  80.6 0.1 collective-permute-start.13
  80.7 3.3 %collective-permute-done.13 = f32[160,128]{1,0:T(8,128)S(1)} collective-permute-done((f32[160,128]{1,0:T(8,128)S(1)}, f32[160,128]{1,0:T(8,128)S(1)}, u32[]{:S(2)}, u32[]{:S(2)}) %collective-permute-start.13) | collective-permute-done | bytes 81952 | tf_op jit(solution)/shard_map/ppermute | solution.py:363
  84.0 4.0 %collective-permute-start.16 = (f32[160,128]{1,0:T(8,128)S(1)}, f32[160,128]{1,0:T(8,128)S(1)}, u32[]{:S(2)}, u32[]{:S(2)}) collective-permute-start(f32[160,128]{1,0:T(8,128)S(1)} %add.72), channel_id=1, source_target_pairs={{0,12},{2,14},{4,8},{6,10},{8,4},{10,6},{12,0},{14,2},{1,13},{3,15... | collective-permute-start | bytes 245768 | tf_op jit(solution)/shard_map/ppermute | solution.py:363
  88.0 1.2 collective-permute-start.15
  89.2 1.2 collective-permute-start.14
  90.4 5.8 %collective-permute-done.15 = f32[160,128]{1,0:T(8,128)S(1)} collective-permute-done((f32[160,128]{1,0:T(8,128)S(1)}, f32[160,128]{1,0:T(8,128)S(1)}, u32[]{:S(2)}, u32[]{:S(2)}) %collective-permute-start.15) | collective-permute-done | bytes 81952 | tf_op jit(solution)/shard_map/ppermute | solution.py:363
  96.2 0.0 collective-permute-done.14
  96.2 8.3 %all_to_all.11 = f32[4,160,128]{2,1,0:T(8,128)S(1)} all-to-all(f32[4,160,128]{2,1,0:T(8,128)S(1)} %broadcast_in_dim.2), channel_id=1, replica_groups=mesh['x'=4,'y'=4,'z'=8,'core'=2] {'x'}, dimensions={0} | all-to-all | bytes 655360 | tf_op jit(solution)/shard_map/all_to_all | solution.py:382
  104.5 8.4 %all_gather.3 = f32[1280,128]{1,0:T(8,128)} all-gather(f32[640,128]{1,0:T(8,128)S(1)} %bitcast.39), channel_id=1, replica_groups=mesh['x'=4,'y'=4,'z'=8,'core'=2] {'core'}, dimensions={0}, use_global_device_ids=true | all-gather | bytes 983040 | tf_op jit(solution)/shard_map/all_gather | solution.py:384
  112.8 23.6 %basis_or_triangle.1 = (f32[128,512]{1,0:T(8,128)}, f32[512,512]{1,0:T(8,128)}) custom-call(s32[1]{0:T(128)} %bitcast.1.core_ref, f32[10,128,128]{2,1,0:T(8,128)} %bitcast.43, f32[512,128]{1,0:T(8,128)} %seed_ref.1), custom_call_target="tpu_custom_call" | custom-call | flops 40000000000 | bytes 2097152 | tf_op jit(solution)/shard_map/basis_or_triangle/pallas_call | solution.py:226
  136.4 0.0 copy-start.2
  136.5 0.1 collective-permute-start.17
  136.6 1.7 %collective-permute-done.17.refs_2_ = f32[128,512]{1,0:T(8,128)S(1)} collective-permute-done((f32[128,512]{1,0:T(8,128)}, f32[128,512]{1,0:T(8,128)S(1)}, u32[]{:S(2)}, u32[]{:S(2)}) %collective-permute-start.17) | collective-permute-done | bytes 262176 | tf_op jit(solution)/shard_map/ppermute | solution.py:363
  138.3 0.1 collective-permute-start.18
  138.4 0.6 copy-done.10
  139.0 6.0 %core_parts.1 = (f32[512,128]{1,0:T(8,128)}, f32[8,32,256]{2,1,0:T(8,128)}, f32[8,32,256]{2,1,0:T(8,128)}, f32[8,32,256]{2,1,0:T(8,128)}, f32[8,32,256]{2,1,0:T(8,128)}) custom-call(s32[2]{0:T(128)} %pad_add_fusion.refs_0_.me_ref, f32[128,512]{1,0:T(8,128)} %get-tuple-element.30.refs_1_, f32[128,512]{1,0:T(8,128)} %copy-done.10, ...), custom_call_target="tpu_custom_call" | custom-call | flops 805306368 | bytes 5242880 | tf_op jit(solution)/shard_map/core_parts/pallas_call | solution.py:303
  145.0 0.4 collective-permute-start.19
  145.4 1.8 %collective-permute-start.20 = (f32[8,32,256]{2,1,0:T(8,128)}, f32[8,32,256]{2,1,0:T(8,128)S(1)}, u32[]{:S(2)}, u32[]{:S(2)}) collective-permute-start(f32[8,32,256]{2,1,0:T(8,128)} %get-tuple-element.43), channel_id=1, source_target_pairs={{0,128},{64,192},{128,0},{192,64},{1,129},{65,193},{129,1},{193,65... | collective-permute-start | bytes 786440 | tf_op jit(solution)/shard_map/ppermute | solution.py:363
  147.2 1.8 %collective-permute-start.21 = (f32[8,32,256]{2,1,0:T(8,128)}, f32[8,32,256]{2,1,0:T(8,128)S(1)}, u32[]{:S(2)}, u32[]{:S(2)}) collective-permute-start(f32[8,32,256]{2,1,0:T(8,128)} %get-tuple-element.44), channel_id=1, source_target_pairs={{0,192},{64,128},{128,64},{192,0},{1,193},{65,129},{129,65},{193,1... | collective-permute-start | bytes 786440 | tf_op jit(solution)/shard_map/ppermute | solution.py:363
  149.0 1.2 broadcast_select_fusion
  150.1 2.9 %collective-permute-done.19.refs_1_ = f32[8,32,256]{2,1,0:T(8,128)S(1)} collective-permute-done((f32[8,32,256]{2,1,0:T(8,128)}, f32[8,32,256]{2,1,0:T(8,128)S(1)}, u32[]{:S(2)}, u32[]{:S(2)}) %collective-permute-start.19) | collective-permute-done | bytes 262176 | tf_op jit(solution)/shard_map/ppermute | solution.py:363
  153.1 6.3 %collective-permute-done.20.refs_2_ = f32[8,32,256]{2,1,0:T(8,128)S(1)} collective-permute-done((f32[8,32,256]{2,1,0:T(8,128)}, f32[8,32,256]{2,1,0:T(8,128)S(1)}, u32[]{:S(2)}, u32[]{:S(2)}) %collective-permute-start.20) | collective-permute-done | bytes 262176 | tf_op jit(solution)/shard_map/ppermute | solution.py:363
  159.3 2.0 %collective-permute-done.21.refs_3_ = f32[8,32,256]{2,1,0:T(8,128)S(1)} collective-permute-done((f32[8,32,256]{2,1,0:T(8,128)}, f32[8,32,256]{2,1,0:T(8,128)S(1)}, u32[]{:S(2)}, u32[]{:S(2)}) %collective-permute-start.21) | collective-permute-done | bytes 262176 | tf_op jit(solution)/shard_map/ppermute | solution.py:363
  161.4 0.9 copy-done
  162.3 1.6 %placed.1 = f32[4,8,32,256]{3,2,1,0:T(8,128)} custom-call(s32[2]{0:T(128)S(1)} %copy-done.1, f32[8,32,256]{2,1,0:T(8,128)S(1)} %copy-done, f32[8,32,256]{2,1,0:T(8,128)S(1)} %collective-permute-done.19.refs_1_, f32[8,32,256]{2,1,0:T(8,128)S(1)} %collective-permute-done.20.refs_2_, f32[8,32,256]{2,1,0:T(8,128)S(1)} %collective-permute-done.21.refs_3_), custom_call_target="tpu_custom_call" | custom-call | tf_op jit(solution)/shard_map/placed/pallas_call | solution.py:347
  (23 shorter events, 0.1 us)
Async XLA Ops:
  2.0 11.2 %collective-permute-start.8 = (f32[3,256,128]{2,1,0:T(8,128)S(1)}, f32[3,256,128]{2,1,0:T(8,128)S(1)}, u32[]{:S(2)}, u32[]{:S(2)}) collective-permute-start(f32[3,256,128]{2,1,0:T(8,128)S(1)} %get-tuple-element.53), channel_id=1, source_target_pairs={{0,192},{64,128},{128,64},{192,0},{1,193},{65,129},{129,65},{193,1... | collective-permute-start | bytes 1179656 | tf_op jit(solution)/shard_map/ppermute | solution.py:363
  5.4 12.2 %collective-permute-start.6 = (f32[3,256,128]{2,1,0:T(8,128)S(1)}, f32[3,256,128]{2,1,0:T(8,128)}, u32[]{:S(2)}, u32[]{:S(2)}) collective-permute-start(f32[3,256,128]{2,1,0:T(8,128)S(1)} %get-tuple-element.54), channel_id=1, source_target_pairs={{0,64},{64,0},{128,192},{192,128},{1,65},{65,1},{129,193},{193,129... | collective-permute-start | bytes 1179656 | tf_op jit(solution)/shard_map/ppermute | solution.py:363
  5.4 16.2 %collective-permute-start.7 = (f32[3,256,128]{2,1,0:T(8,128)S(1)}, f32[3,256,128]{2,1,0:T(8,128)}, u32[]{:S(2)}, u32[]{:S(2)}) collective-permute-start(f32[3,256,128]{2,1,0:T(8,128)S(1)} %get-tuple-element.55), channel_id=1, source_target_pairs={{0,128},{64,192},{128,0},{192,64},{1,129},{65,193},{129,1},{193,65... | collective-permute-start | bytes 1179656 | tf_op jit(solution)/shard_map/ppermute | solution.py:363
  8.0 22.0 %collective-permute-start.5 = (f32[3,256,128]{2,1,0:T(8,128)S(1)}, f32[3,256,128]{2,1,0:T(8,128)S(1)}, u32[]{:S(2)}, u32[]{:S(2)}) collective-permute-start(f32[3,256,128]{2,1,0:T(8,128)S(1)} %get-tuple-element.50), channel_id=1, source_target_pairs={{0,192},{64,128},{128,64},{192,0},{1,193},{65,129},{129,65},{193,1... | collective-permute-start | bytes 1179656 | tf_op jit(solution)/shard_map/ppermute | solution.py:363
  10.6 25.0 %collective-permute-start.3 = (f32[3,256,128]{2,1,0:T(8,128)S(1)}, f32[3,256,128]{2,1,0:T(8,128)S(1)}, u32[]{:S(2)}, u32[]{:S(2)}) collective-permute-start(f32[3,256,128]{2,1,0:T(8,128)S(1)} %get-tuple-element.51), channel_id=1, source_target_pairs={{0,64},{64,0},{128,192},{192,128},{1,65},{65,1},{129,193},{193,129... | collective-permute-start | bytes 1179656 | tf_op jit(solution)/shard_map/ppermute | solution.py:363
  13.2 18.4 %copy-start.6 = (f32[3,256,128]{2,1,0:T(8,128)}, f32[3,256,128]{2,1,0:T(8,128)S(1)}, u32[]{:S(2)}) copy-start(f32[3,256,128]{2,1,0:T(8,128)S(1)} %collective-permute-done.8.refs_4_) | copy-start | bytes 1179652
  13.2 25.2 %collective-permute-start.4 = (f32[3,256,128]{2,1,0:T(8,128)S(1)}, f32[3,256,128]{2,1,0:T(8,128)S(1)}, u32[]{:S(2)}, u32[]{:S(2)}) collective-permute-start(f32[3,256,128]{2,1,0:T(8,128)S(1)} %get-tuple-element.52), channel_id=1, source_target_pairs={{0,128},{64,192},{128,0},{192,64},{1,129},{65,193},{129,1},{193,65... | collective-permute-start | bytes 1179656 | tf_op jit(solution)/shard_map/ppermute | solution.py:363
  17.6 32.2 %collective-permute-start.2 = (f32[2,256,128]{2,1,0:T(8,128)}, f32[2,256,128]{2,1,0:T(8,128)S(1)}, u32[]{:S(2)}, u32[]{:S(2)}) collective-permute-start(f32[2,256,128]{2,1,0:T(8,128)} %get-tuple-element.47), channel_id=1, source_target_pairs={{0,192},{64,128},{128,64},{192,0},{1,193},{65,129},{129,65},{193,1... | collective-permute-start | bytes 786440 | tf_op jit(solution)/shard_map/ppermute | solution.py:363
  21.6 28.2 %collective-permute-start.1 = (f32[2,256,128]{2,1,0:T(8,128)S(1)}, f32[2,256,128]{2,1,0:T(8,128)S(1)}, u32[]{:S(2)}, u32[]{:S(2)}) collective-permute-start(f32[2,256,128]{2,1,0:T(8,128)S(1)} %get-tuple-element.48), channel_id=1, source_target_pairs={{0,128},{64,192},{128,0},{192,64},{1,129},{65,193},{129,1},{193,65... | collective-permute-start | bytes 786440 | tf_op jit(solution)/shard_map/ppermute | solution.py:363
  30.0 8.4 %copy-start.3 = (f32[3,256,128]{2,1,0:T(8,128)}, f32[3,256,128]{2,1,0:T(8,128)S(1)}, u32[]{:S(2)}) copy-start(f32[3,256,128]{2,1,0:T(8,128)S(1)} %collective-permute-done.5.refs_4_) | copy-start | bytes 1179652
  30.0 20.3 %collective-permute-start = (f32[2,256,128]{2,1,0:T(8,128)S(1)}, f32[2,256,128]{2,1,0:T(8,128)S(1)}, u32[]{:S(2)}, u32[]{:S(2)}) collective-permute-start(f32[2,256,128]{2,1,0:T(8,128)S(1)} %get-tuple-element.49), channel_id=1, source_target_pairs={{0,64},{64,0},{128,192},{192,128},{1,65},{65,1},{129,193},{193,129... | collective-permute-start | bytes 786440 | tf_op jit(solution)/shard_map/ppermute | solution.py:363
  35.7 2.7 %copy-start.4 = (f32[3,256,128]{2,1,0:T(8,128)}, f32[3,256,128]{2,1,0:T(8,128)S(1)}, u32[]{:S(2)}) copy-start(f32[3,256,128]{2,1,0:T(8,128)S(1)} %collective-permute-done.3.refs_2_) | copy-start | bytes 1179652
  38.4 0.8 copy-start.5
  49.8 0.7 copy-start.7
  49.8 0.8 copy-start.8
  50.3 0.7 copy-start.9
  55.9 8.5 %collective-permute-start.9 = (f32[640,128]{1,0:T(8,128)S(1)}, f32[640,128]{1,0:T(8,128)S(1)}, u32[]{:S(2)}, u32[]{:S(2)}) collective-permute-start(f32[640,128]{1,0:T(8,128)S(1)} %constant_dynamic-slice_fusion), channel_id=1, source_target_pairs={{0,1},{1,0},{2,3},{3,2},{4,5},{5,4},{6,7},{7,6},{8,9},{9,8},{10,11... | collective-permute-start | bytes 983048 | tf_op jit(solution)/shard_map/ppermute | solution.py:363
  75.0 5.0 %collective-permute-start.11 = (f32[160,128]{1,0:T(8,128)S(1)}, f32[160,128]{1,0:T(8,128)S(1)}, u32[]{:S(2)}, u32[]{:S(2)}) collective-permute-start(f32[160,128]{1,0:T(8,128)S(1)} %fusion.1), channel_id=1, source_target_pairs={{0,32},{16,48},{32,0},{48,16},{1,33},{17,49},{33,1},{49,17},{2,34}... | collective-permute-start | bytes 245768 | tf_op jit(solution)/shard_map/ppermute | solution.py:363
  75.1 5.5 %collective-permute-start.12 = (f32[160,128]{1,0:T(8,128)S(1)}, f32[160,128]{1,0:T(8,128)S(1)}, u32[]{:S(2)}, u32[]{:S(2)}) collective-permute-start(f32[160,128]{1,0:T(8,128)S(1)} %fusion.1), channel_id=1, source_target_pairs={{0,48},{16,32},{32,16},{48,0},{1,49},{17,33},{33,17},{49,1},{2,50}... | collective-permute-start | bytes 245768 | tf_op jit(solution)/shard_map/ppermute | solution.py:363
  75.2 5.4 %collective-permute-start.10 = (f32[160,128]{1,0:T(8,128)S(1)}, f32[160,128]{1,0:T(8,128)S(1)}, u32[]{:S(2)}, u32[]{:S(2)}) collective-permute-start(f32[160,128]{1,0:T(8,128)S(1)} %fusion.1), channel_id=1, source_target_pairs={{0,16},{16,0},{32,48},{48,32},{1,17},{17,1},{33,49},{49,33},{2,18}... | collective-permute-start | bytes 245768 | tf_op jit(solution)/shard_map/ppermute | solution.py:363
  80.6 3.4 %collective-permute-start.13 = (f32[160,128]{1,0:T(8,128)S(1)}, f32[160,128]{1,0:T(8,128)S(1)}, u32[]{:S(2)}, u32[]{:S(2)}) collective-permute-start(f32[160,128]{1,0:T(8,128)S(1)} %add_add_fusion.1), channel_id=1, source_target_pairs={{0,2},{2,0},{4,6},{6,4},{8,10},{10,8},{12,14},{14,12},{1,3},{3,1},... | collective-permute-start | bytes 245768 | tf_op jit(solution)/shard_map/ppermute | solution.py:363
  84.0 6.4 %collective-permute-start.16 = (f32[160,128]{1,0:T(8,128)S(1)}, f32[160,128]{1,0:T(8,128)S(1)}, u32[]{:S(2)}, u32[]{:S(2)}) collective-permute-start(f32[160,128]{1,0:T(8,128)S(1)} %add.72), channel_id=1, source_target_pairs={{0,12},{2,14},{4,8},{6,10},{8,4},{10,6},{12,0},{14,2},{1,13},{3,15... | collective-permute-start | bytes 245768 | tf_op jit(solution)/shard_map/ppermute | solution.py:363
  88.0 8.2 %collective-permute-start.15 = (f32[160,128]{1,0:T(8,128)S(1)}, f32[160,128]{1,0:T(8,128)S(1)}, u32[]{:S(2)}, u32[]{:S(2)}) collective-permute-start(f32[160,128]{1,0:T(8,128)S(1)} %add.72), channel_id=1, source_target_pairs={{0,8},{2,10},{4,12},{6,14},{8,0},{10,2},{12,4},{14,6},{1,9},{3,11}... | collective-permute-start | bytes 245768 | tf_op jit(solution)/shard_map/ppermute | solution.py:363
  89.2 7.0 %collective-permute-start.14 = (f32[160,128]{1,0:T(8,128)S(1)}, f32[160,128]{1,0:T(8,128)S(1)}, u32[]{:S(2)}, u32[]{:S(2)}) collective-permute-start(f32[160,128]{1,0:T(8,128)S(1)} %add.72), channel_id=1, source_target_pairs={{0,4},{2,6},{4,0},{6,2},{8,12},{10,14},{12,8},{14,10},{1,5},{3,7},... | collective-permute-start | bytes 245768 | tf_op jit(solution)/shard_map/ppermute | solution.py:363
  136.4 12.5 %copy-start.2 = (f32[512,512]{1,0:T(8,128)S(1)}, f32[512,512]{1,0:T(8,128)}, u32[]{:S(2)}) copy-start(f32[512,512]{1,0:T(8,128)} %get-tuple-element.40) | copy-start | bytes 3145732
  136.4 24.9 %copy-start.1 = (s32[2]{0:T(128)S(1)}, s32[2]{0:T(128)}, u32[]{:S(2)}) copy-start(s32[2]{0:T(128)} %pad_add_fusion.refs_0_.me_ref) | copy-start | bytes 28
  136.5 1.8 %collective-permute-start.17 = (f32[128,512]{1,0:T(8,128)}, f32[128,512]{1,0:T(8,128)S(1)}, u32[]{:S(2)}, u32[]{:S(2)}) collective-permute-start(f32[128,512]{1,0:T(8,128)} %get-tuple-element.30.refs_1_), channel_id=1, source_target_pairs={{0,1},{1,0},{2,3},{3,2},{4,5},{5,4},{6,7},{7,6},{8,9},{9,8},{10,11... | collective-permute-start | bytes 786440 | tf_op jit(solution)/shard_map/ppermute | solution.py:363
  138.3 0.7 copy-start.10
  138.3 10.7 %collective-permute-start.18 = (f32[512,512]{1,0:T(8,128)}, f32[512,512]{1,0:T(8,128)S(1)}, u32[]{:S(2)}, u32[]{:S(2)}) collective-permute-start(f32[512,512]{1,0:T(8,128)} %get-tuple-element.40), channel_id=1, source_target_pairs={{0,1},{1,0},{2,3},{3,2},{4,5},{5,4},{6,7},{7,6},{8,9},{9,8},{10,11... | collective-permute-start | bytes 3145736 | tf_op jit(solution)/shard_map/ppermute | solution.py:363
  145.0 8.1 %collective-permute-start.19 = (f32[8,32,256]{2,1,0:T(8,128)}, f32[8,32,256]{2,1,0:T(8,128)S(1)}, u32[]{:S(2)}, u32[]{:S(2)}) collective-permute-start(f32[8,32,256]{2,1,0:T(8,128)} %get-tuple-element.42), channel_id=1, source_target_pairs={{0,64},{64,0},{128,192},{192,128},{1,65},{65,1},{129,193},{193,129... | collective-permute-start | bytes 786440 | tf_op jit(solution)/shard_map/ppermute | solution.py:363
  145.4 14.0 %collective-permute-start.20 = (f32[8,32,256]{2,1,0:T(8,128)}, f32[8,32,256]{2,1,0:T(8,128)S(1)}, u32[]{:S(2)}, u32[]{:S(2)}) collective-permute-start(f32[8,32,256]{2,1,0:T(8,128)} %get-tuple-element.43), channel_id=1, source_target_pairs={{0,128},{64,192},{128,0},{192,64},{1,129},{65,193},{129,1},{193,65... | collective-permute-start | bytes 786440 | tf_op jit(solution)/shard_map/ppermute | solution.py:363
  147.2 14.2 %collective-permute-start.21 = (f32[8,32,256]{2,1,0:T(8,128)}, f32[8,32,256]{2,1,0:T(8,128)S(1)}, u32[]{:S(2)}, u32[]{:S(2)}) collective-permute-start(f32[8,32,256]{2,1,0:T(8,128)} %get-tuple-element.44), channel_id=1, source_target_pairs={{0,192},{64,128},{128,64},{192,0},{1,193},{65,129},{129,65},{193,1... | collective-permute-start | bytes 786440 | tf_op jit(solution)/shard_map/ppermute | solution.py:363
  161.3 1.0 copy-start

commit v4 on v3

--- a/solution.py
+++ b/solution.py
@@ -10,7 +10,7 @@
 NB = 4
 W = 128
 PAIRS = [(k, l) for k in range(NB) for l in range(k, NB)]
-COUNTS = (3, 3, 2)
+COUNTS = (1, 3, 3, 1)
 VMEM_LIMIT = 60 * 1024 * 1024
 
 
@@ -177,23 +177,22 @@
         upper, inverse = factor([rest[pl.ds(start + 8 * p, 8), own] for p in range(W // 8)])
         inverse = jnp.concatenate(inverse, axis=0)
 
-        @pl.when(b < NB - 1)
-        def _():
-            keep = lax.broadcasted_iota(jnp.int32, (W, NB * W), 1) >= (b + 1) * W
-            row = jnp.where(keep, exact(inverse, rest[own, :]), 0.0)
-            out_ref[own, :] = row
-
-            def down(c, carry):
-                at = pl.ds(pl.multiple_of(c * W, W), W)
-                rest[at, :] -= exact(out_ref[own, at].T, out_ref[own, :])
-                return carry
-
-            lax.fori_loop(b + 1, NB, down, 0)
-
+        keep = lax.broadcasted_iota(jnp.int32, (W, NB * W), 1) >= (b + 1) * W
+        row = jnp.where(keep, exact(inverse, rest[own, :]), 0.0)
+        out_ref[own, :] = row
+
+        def down(c, carry):
+            at = pl.ds(pl.multiple_of(c * W, W), W)
+            rest[at, :] -= exact(out_ref[own, at].T, out_ref[own, :])
+            return carry
+
+        lax.fori_loop(b + 1, NB, down, 0)
         out_ref[own, own] = jnp.concatenate(upper, axis=0)
         return carry
 
-    lax.fori_loop(0, NB, step, 0)
+    lax.fori_loop(0, NB - 1, step, 0)
+    last = slice(W * (NB - 1), W * NB)
+    out_ref[last, last] = rest[last, last]
 
 
 def copied(*copies):
@@ -247,6 +246,35 @@
     )(core, gram, seed)
 
 
+def finish_kernel(core_ref, own_ref, other_ref, out_ref, triangle, sems):
+    for flag, source in enumerate((other_ref, own_ref)):
+
+        @pl.when(core_ref[0] == flag)
+        def _(source=source):
+            copied(pltpu.make_async_copy(source, triangle, sems.at[0]))
+
+    last = slice(W * (NB - 1), W * NB)
+    upper, _ = factor(panels_of(triangle[last, last]))
+    triangle[last, last] = jnp.concatenate(upper, axis=0)
+    copied(pltpu.make_async_copy(triangle, out_ref, sems.at[1]))
+
+
+def finished(core, own, other):
+    anywhere = pl.BlockSpec(memory_space=pl.ANY)
+    return pl.pallas_call(
+        finish_kernel,
+        in_specs=[pl.BlockSpec(memory_space=pltpu.SMEM), anywhere, anywhere],
+        out_specs=anywhere,
+        out_shape=jax.ShapeDtypeStruct(own.shape, jnp.float32),
+        scratch_shapes=[pltpu.VMEM(own.shape, jnp.float32), pltpu.SemaphoreType.DMA((2,))],
+        compiler_params=pltpu.CompilerParams(vmem_limit_bytes=VMEM_LIMIT // 6),
+        cost_estimate=pl.CostEstimate(
+            flops=6_000_000_000, bytes_accessed=8 * own.size, transcendentals=0
+        ),
+        name="finished",
+    )(core, own, other)
+
+
 def core_kernel(counts, snaps, me_ref, own_ref, other_ref, *refs):
     n = 2 * len(counts)
     sources, refs = refs[:n], refs[n:]
@@ -259,6 +287,9 @@
         for i, (source, half) in enumerate(zip(sources, halves))
     ]
 
+    for copy in arrivals:
+        copy.start()
+
     @pl.when(me_ref[1] == 0)
     def _():
         copied(pltpu.make_async_copy(own_ref, basis, in_sems.at[n]))
@@ -267,8 +298,6 @@
     def _():
         copied(pltpu.make_async_copy(other_ref, basis, in_sems.at[n]))
 
-    for copy in arrivals:
-        copy.start()
     mode[...] = basis[...].T
     leaving = [pltpu.make_async_copy(mode, mode_ref, out_sems.at[NB])]
     leaving[0].start()
@@ -394,16 +423,16 @@
     counts = COUNTS
 
     gram, halves, start = None, [], 0
-    arrived, later = [], field
-    for count in counts:
-        got, sends = {}, []
+    arrived = []
+    for c, count in enumerate(counts):
+        later, got = field, {}
+        if c >= 2:
+            later, *arrived[c - 2] = lax.optimization_barrier((field, *arrived[c - 2]))
         for bits in (2, 1, 3):
             send = lax.dynamic_slice(
                 later, (me ^ bits, start, 0, 0), (1, count, snaps, width)
             )[0]
             got[bits] = exchanged(send, "x", bits)
-            sends.append(send)
-        later, *_ = lax.optimization_barrier((later, *sends))
         arrived.append([got[bits] for bits in (1, 2, 3)])
         start += count
     start = 0
@@ -419,7 +448,7 @@
     other_triangle = exchanged(triangle, "core", 1)
     mode_factor, *parts = core_parts(place, basis, other_basis, halves, counts, snaps)
     sent = {bits: exchanged(parts[bits], "x", bits) for bits in (2, 1, 3)}
-    triangle = jnp.where(core == 0, other_triangle, triangle)
+    triangle = finished(place[1:], triangle, other_triangle)
     own_part, triangle = lax.optimization_barrier((parts[0], triangle))
     core_tensor = placed(place, [own_part] + [sent[bits] for bits in (1, 2, 3)])
     core_tensor = core_tensor.reshape(cells, -1, snaps).transpose(0, 2, 1)

time: 165 us -> 174 us (1.055)
  Pallas kernels: 43.5 us -> 48.8 us
  starting transfers between devices: 36.1 us -> 39.9 us
  blocking collectives: 26.2 us -> 28.1 us
    pallas_call x0 -> x1, Pallas kernels: none -> 5.62 us  [finished(): pl.pallas_call(finish_kernel, in_specs=[pl.BlockSpec(memory_space=pltpu.S...]
    ppermute x22 -> x25, starting transfers between devices: 36.1 us -> 39.9 us  [exchanged(): return lax.ppermute(block, axis, [(i, i ^ bits) for i in range(count)])]
    pallas_call x1, Pallas kernels: 23.6 us -> 19.9 us  [basis_or_triangle(): pl.pallas_call(either_kernel, in_specs=[pl.BlockSpec(memory_space=pltpu.S...]
    pallas_call x3 -> x4, Pallas kernels: 12.2 us -> 15.4 us  [gram_chunk(): pl.pallas_call(lambda *refs: gram_kernel(scale, start, *refs), in_specs=[...]
    ppermute x22 -> x25, waiting for transfers between devices: 46 us -> 44.4 us  [exchanged(): return lax.ppermute(block, axis, [(i, i ^ bits) for i in range(count)])]
    squeeze x3 -> x4, local copies, waits for them, and re-layouts: 4.49 us -> 5.85 us  [local(): lax.dynamic_slice(later, (me ^ bits, start, 0, 0), (1, count, snaps, width))]
  transfers between devices with their start and end apart: 22 -> 25, of which waited for: 15 -> 12; matrix products, arithmetic and copies ran while one was open for 3% -> 3% of each run, Pallas kernels for 9% -> 14%
where the time goes in v4:
time: 174 us; the launch traced here: 173 us
  Pallas kernels  48.8 us (28%)
  waiting for transfers between devices  44.4 us (26%)
  starting transfers between devices  39.9 us (23%)
  blocking collectives  28.1 us (16%)
  local copies, waits for them, and re-layouts  9.33 us (5%)
  other arithmetic  1.75 us (1%)
    ppermute x25, waiting for transfers between devices, exchanged(): return lax.ppermute(block, axis, [(i, i ^ bits) for i in range(count)])  44.4 us
    ppermute x25, starting transfers between devices, exchanged(): return lax.ppermute(block, axis, [(i, i ^ bits) for i in range(count)])  39.9 us
    pallas_call x1, Pallas kernels, basis_or_triangle(): pl.pallas_call(either_kernel, in_specs=[pl.BlockSpec(memory_space=pltpu.S...  19.9 us
    pallas_call x4, Pallas kernels, gram_chunk(): pl.pallas_call(lambda *refs: gram_kernel(scale, start, *refs), in_specs=[...  15.4 us
    all_to_all x1, blocking collectives, summed_over_devices(): lax.all_to_all(own.reshape(NB, half // NB, W), 'x', split_axis=0, concat_...  11.2 us
    all_gather x1, blocking collectives, summed_over_devices(): return lax.all_gather(whole, 'core', axis=0, tiled=True)  8.57 us
    all_to_all x1, blocking collectives, summed_over_devices(): whole = lax.all_to_all(copies, 'x', split_axis=0, concat_axis=0, tiled=True)  8.25 us
    pallas_call x1, Pallas kernels, core_parts(): pl.pallas_call(lambda *refs: core_kernel(counts, snaps, *refs), in_specs=...  6.21 us
  transfers between devices with their start and end apart: 25, of which 12 were waited for; matrix products, arithmetic and copies ran while one was open for 3% of the time, Pallas kernels for 14%

profile of v4, /device:TPU:1, one launch (start us, length us, event | category | flops | bytes accessed | tf_op | source)
XLA Modules:
  0.0 173.3 jit_solution(3007446939361893185)
XLA Ops:
  0.7 1.3 dynamic-slice_bitcast_fusion.3
  2.0 3.4 %collective-permute-start.2 = (f32[3,256,128]{2,1,0:T(8,128)S(1)}, f32[3,256,128]{2,1,0:T(8,128)S(1)}, u32[]{:S(2)}, u32[]{:S(2)}) collective-permute-start(f32[3,256,128]{2,1,0:T(8,128)S(1)} %get-tuple-element.74), channel_id=1, source_target_pairs={{0,192},{64,128},{128,64},{192,0},{1,193},{65,129},{129,65},{193,1... | collective-permute-start | bytes 1179656 | tf_op jit(solution)/shard_map/ppermute | solution.py:392
  5.4 1.1 dynamic-slice_bitcast_fusion.6
  6.4 0.1 collective-permute-start.8
  6.5 1.7 collective-permute-start.7
  8.2 1.5 collective-permute-start.6
  9.8 0.6 collective-permute-start.1
  10.4 16.8 %collective-permute-done.8.refs_4_ = f32[1,256,128]{2,1,0:T(8,128)S(1)} collective-permute-done((f32[1,256,128]{2,1,0:T(8,128)S(1)}, f32[1,256,128]{2,1,0:T(8,128)S(1)}, u32[]{:S(2)}, u32[]{:S(2)}) %collective-permute-start.8) | collective-permute-done | bytes 131104 | tf_op jit(solution)/shard_map/ppermute | solution.py:392
  27.2 0.6 copy-done.9
  27.8 0.9 collective-permute-start
  28.8 0.0 collective-permute-done.7.refs_3_
  28.8 0.0 collective-permute-done.6.refs_2_
  28.8 0.0 copy-start.11
  28.8 2.1 %dynamic-slice_bitcast_fusion = (f32[3,256,128]{2,1,0:T(8,128)}, f32[3,256,128]{2,1,0:T(8,128)S(1)}, f32[3,256,128]{2,1,0:T(8,128)S(1)}) fusion(f32[4,8,256,128]{3,2,1,0:T(8,128)} %bitcast.40, s32[]{:T(128)S(6)} %select_n.12, s32[]{:T(128)S(6)} %select_n.11, s32[]{:T(128)S(6)} %select_n.10), kind=kLoop, calls=%fused_computation | loop fusion | bytes 2359308 | tf_op jit(solution)/shard_map/squeeze | solution.py:432
  31.0 2.5 %collective-permute-start.11 = (f32[3,256,128]{2,1,0:T(8,128)}, f32[3,256,128]{2,1,0:T(8,128)S(1)}, u32[]{:S(2)}, u32[]{:S(2)}) collective-permute-start(f32[3,256,128]{2,1,0:T(8,128)} %get-tuple-element.65), channel_id=1, source_target_pairs={{0,192},{64,128},{128,64},{192,0},{1,193},{65,129},{129,65},{193,1... | collective-permute-start | bytes 1179656 | tf_op jit(solution)/shard_map/ppermute | solution.py:392
  33.4 1.3 collective-permute-start.10
  34.7 0.0 collective-permute-start.9
  34.7 0.7 pad_add_fusion.refs_0_.me_ref
  35.4 3.3 %gram_chunk.4 = (f32[10,128,128]{2,1,0:T(8,128)}, bf16[256,512]{1,0:T(8,128)(2,1)}, bf16[256,512]{1,0:T(8,128)(2,1)}) custom-call(s32[2]{0:T(128)} %pad_add_fusion.refs_0_.me_ref, f32[4,8,256,128]{3,2,1,0:T(8,128)} %bitcast.41, f32[1,256,128]{2,1,0:T(8,128)} %copy-done.11, f32[1,256,128]{2,1,0:T(8,128)} %copy-done.10, f32[1,256,128]{2,1,0:T(8,128)} %copy-done.9), custom_call_target="tpu_custom_call" | custom-call | flops 268435456 | bytes 1048576 | tf_op jit(solution)/shard_map/gram_chunk/pallas_call | solution.py:68
  38.7 1.3 dynamic-slice_bitcast_fusion.9
  40.0 2.1 %collective-permute-start.5 = (f32[1,256,128]{2,1,0:T(8,128)S(1)}, f32[1,256,128]{2,1,0:T(8,128)S(1)}, u32[]{:S(2)}, u32[]{:S(2)}) collective-permute-start(f32[1,256,128]{2,1,0:T(8,128)S(1)} %get-tuple-element.71), channel_id=1, source_target_pairs={{0,192},{64,128},{128,64},{192,0},{1,193},{65,129},{129,65},{193,1... | collective-permute-start | bytes 393224 | tf_op jit(solution)/shard_map/ppermute | solution.py:392
  42.1 1.2 collective-permute-start.4
  43.3 5.9 %collective-permute-done.11.refs_4_ = f32[3,256,128]{2,1,0:T(8,128)S(1)} collective-permute-done((f32[3,256,128]{2,1,0:T(8,128)}, f32[3,256,128]{2,1,0:T(8,128)S(1)}, u32[]{:S(2)}, u32[]{:S(2)}) %collective-permute-start.11) | collective-permute-done | bytes 393248 | tf_op jit(solution)/shard_map/ppermute | solution.py:392
  49.2 0.4 collective-permute-start.3
  49.7 4.3 %gram_chunk.5 = (f32[10,128,128]{2,1,0:T(8,128)}, bf16[768,512]{1,0:T(8,128)(2,1)}, bf16[768,512]{1,0:T(8,128)(2,1)}) custom-call(s32[2]{0:T(128)} %pad_add_fusion.refs_0_.me_ref, f32[4,8,256,128]{3,2,1,0:T(8,128)} %bitcast.43, f32[3,256,128]{2,1,0:T(8,128)} %copy-done.5, f32[3,256,128]{2,1,0:T(8,128)} %copy-done.4, f32[3,256,128]{2,1,0:T(8,128)} %copy-done.3, ...), custom_call_target="tpu_custom_call" | custom-call | flops 805306368 | bytes 3145728 | tf_op jit(solution)/shard_map/gram_chunk/pallas_call | solution.py:68
  54.0 0.7 copy-done.7
  54.7 4.3 %gram_chunk.6 = (f32[10,128,128]{2,1,0:T(8,128)}, bf16[768,512]{1,0:T(8,128)(2,1)}, bf16[768,512]{1,0:T(8,128)(2,1)}) custom-call(s32[2]{0:T(128)} %pad_add_fusion.refs_0_.me_ref, f32[4,8,256,128]{3,2,1,0:T(8,128)} %bitcast.44, f32[3,256,128]{2,1,0:T(8,128)} %collective-permute-done.9.refs_2_, f32[3,256,128]{2,1,0:T(8,128)} %copy-done.7, ...), custom_call_target="tpu_custom_call" | custom-call | flops 805306368 | bytes 3145728 | tf_op jit(solution)/shard_map/gram_chunk/pallas_call | solution.py:68
  59.1 0.4 collective-permute-done.4.refs_3_
  59.5 0.3 copy-done.12
  59.7 0.4 copy-done.13
  60.1 0.0 copy-done.14
  60.1 3.5 %gram_chunk.7 = (f32[10,128,128]{2,1,0:T(8,128)}, bf16[256,512]{1,0:T(8,128)(2,1)}, bf16[256,512]{1,0:T(8,128)(2,1)}) custom-call(s32[2]{0:T(128)} %pad_add_fusion.refs_0_.me_ref, f32[4,8,256,128]{3,2,1,0:T(8,128)} %bitcast.45, f32[1,256,128]{2,1,0:T(8,128)} %copy-done.14, f32[1,256,128]{2,1,0:T(8,128)} %copy-done.13, f32[1,256,128]{2,1,0:T(8,128)} %copy-done.12, ...), custom_call_target="tpu_custom_call" | custom-call | flops 268435456 | bytes 1048576 | tf_op jit(solution)/shard_map/gram_chunk/pallas_call | solution.py:68
  63.7 1.0 constant_dynamic-slice_fusion
  64.7 4.8 %collective-permute-start.12 = (f32[640,128]{1,0:T(8,128)S(1)}, f32[640,128]{1,0:T(8,128)S(1)}, u32[]{:S(2)}, u32[]{:S(2)}) collective-permute-start(f32[640,128]{1,0:T(8,128)S(1)} %constant_dynamic-slice_fusion), channel_id=1, source_target_pairs={{0,1},{1,0},{2,3},{3,2},{4,5},{5,4},{6,7},{7,6},{8,9},{9,8},{10,11... | collective-permute-start | bytes 983048 | tf_op jit(solution)/shard_map/ppermute | solution.py:392
  69.4 1.3 collective-permute-done.12
  70.7 1.0 dynamic-slice_add_fusion
  71.7 11.2 %all_to_all.10 = f32[4,160,128]{2,1,0:T(8,128)S(1)} all-to-all(f32[4,160,128]{2,1,0:T(8,128)S(1)} %bitcast.46), channel_id=1, replica_groups=mesh['x'=4,'y'=4,'z'=8,'core'=2] {'x'}, dimensions={0} | all-to-all | bytes 655360 | tf_op jit(solution)/shard_map/all_to_all | solution.py:401
  83.0 2.6 %collective-permute-start.14 = (f32[160,128]{1,0:T(8,128)S(1)}, f32[160,128]{1,0:T(8,128)S(1)}, u32[]{:S(2)}, u32[]{:S(2)}) collective-permute-start(f32[160,128]{1,0:T(8,128)S(1)} %fusion.1), channel_id=1, source_target_pairs={{0,32},{16,48},{32,0},{48,16},{1,33},{17,49},{33,1},{49,17},{2,34}... | collective-permute-start | bytes 245768 | tf_op jit(solution)/shard_map/ppermute | solution.py:392
  85.6 0.8 collective-permute-start.15
  86.4 1.5 collective-permute-done.14
  87.8 2.9 %collective-permute-done.15 = f32[160,128]{1,0:T(8,128)S(1)} collective-permute-done((f32[160,128]{1,0:T(8,128)S(1)}, f32[160,128]{1,0:T(8,128)S(1)}, u32[]{:S(2)}, u32[]{:S(2)}) %collective-permute-start.15) | collective-permute-done | bytes 81952 | tf_op jit(solution)/shard_map/ppermute | solution.py:392
  90.8 1.4 collective-permute-start.16
  92.2 2.0 %collective-permute-done.16 = f32[160,128]{1,0:T(8,128)S(1)} collective-permute-done((f32[160,128]{1,0:T(8,128)S(1)}, f32[160,128]{1,0:T(8,128)S(1)}, u32[]{:S(2)}, u32[]{:S(2)}) %collective-permute-start.16) | collective-permute-done | bytes 81952 | tf_op jit(solution)/shard_map/ppermute | solution.py:392
  94.1 5.8 %collective-permute-start.19 = (f32[160,128]{1,0:T(8,128)S(1)}, f32[160,128]{1,0:T(8,128)S(1)}, u32[]{:S(2)}, u32[]{:S(2)}) collective-permute-start(f32[160,128]{1,0:T(8,128)S(1)} %add.75), channel_id=1, source_target_pairs={{0,12},{2,14},{4,8},{6,10},{8,4},{10,6},{12,0},{14,2},{1,13},{3,15... | collective-permute-start | bytes 245768 | tf_op jit(solution)/shard_map/ppermute | solution.py:392
  99.9 1.0 collective-permute-start.18
  100.9 1.2 collective-permute-start.17
  102.1 0.1 collective-permute-done.19
  102.3 5.7 %collective-permute-done.18 = f32[160,128]{1,0:T(8,128)S(1)} collective-permute-done((f32[160,128]{1,0:T(8,128)S(1)}, f32[160,128]{1,0:T(8,128)S(1)}, u32[]{:S(2)}, u32[]{:S(2)}) %collective-permute-start.18) | collective-permute-done | bytes 81952 | tf_op jit(solution)/shard_map/ppermute | solution.py:392
  108.0 8.3 %all_to_all.11 = f32[4,160,128]{2,1,0:T(8,128)S(1)} all-to-all(f32[4,160,128]{2,1,0:T(8,128)S(1)} %broadcast_in_dim.2), channel_id=1, replica_groups=mesh['x'=4,'y'=4,'z'=8,'core'=2] {'x'}, dimensions={0} | all-to-all | bytes 655360 | tf_op jit(solution)/shard_map/all_to_all | solution.py:411
  116.3 8.6 %all_gather.3 = f32[1280,128]{1,0:T(8,128)} all-gather(f32[640,128]{1,0:T(8,128)S(1)} %bitcast.47), channel_id=1, replica_groups=mesh['x'=4,'y'=4,'z'=8,'core'=2] {'core'}, dimensions={0}, use_global_device_ids=true | all-gather | bytes 983040 | tf_op jit(solution)/shard_map/all_gather | solution.py:413
  124.8 19.9 %basis_or_triangle.1 = (f32[128,512]{1,0:T(8,128)}, f32[512,512]{1,0:T(8,128)}) custom-call(s32[1]{0:T(128)} %bitcast.1.core_ref, f32[10,128,128]{2,1,0:T(8,128)} %bitcast.51, f32[512,128]{1,0:T(8,128)} %seed_ref.1), custom_call_target="tpu_custom_call" | custom-call | flops 40000000000 | bytes 2097152 | tf_op jit(solution)/shard_map/basis_or_triangle/pallas_call | solution.py:225
  144.7 0.0 copy-start.2
  144.7 2.3 %collective-permute-start.20 = (f32[128,512]{1,0:T(8,128)}, f32[128,512]{1,0:T(8,128)S(1)}, u32[]{:S(2)}, u32[]{:S(2)}) collective-permute-start(f32[128,512]{1,0:T(8,128)} %get-tuple-element.46.refs_1_), channel_id=1, source_target_pairs={{0,1},{1,0},{2,3},{3,2},{4,5},{5,4},{6,7},{7,6},{8,9},{9,8},{10,11... | collective-permute-start | bytes 786440 | tf_op jit(solution)/shard_map/ppermute | solution.py:392
  147.1 1.4 collective-permute-done.20.refs_2_
  148.4 0.4 collective-permute-start.21
  148.8 0.3 copy-done.8
  149.2 6.2 %core_parts.1 = (f32[512,128]{1,0:T(8,128)}, f32[8,32,256]{2,1,0:T(8,128)}, f32[8,32,256]{2,1,0:T(8,128)}, f32[8,32,256]{2,1,0:T(8,128)}, f32[8,32,256]{2,1,0:T(8,128)}) custom-call(s32[2]{0:T(128)} %pad_add_fusion.refs_0_.me_ref, f32[128,512]{1,0:T(8,128)} %get-tuple-element.46.refs_1_, f32[128,512]{1,0:T(8,128)} %copy-done.8, ...), custom_call_target="tpu_custom_call" | custom-call | flops 805306368 | bytes 5242880 | tf_op jit(solution)/shard_map/core_parts/pallas_call | solution.py:332
  155.4 0.4 collective-permute-start.22
  155.8 1.8 %collective-permute-start.23 = (f32[8,32,256]{2,1,0:T(8,128)}, f32[8,32,256]{2,1,0:T(8,128)S(1)}, u32[]{:S(2)}, u32[]{:S(2)}) collective-permute-start(f32[8,32,256]{2,1,0:T(8,128)} %get-tuple-element.61), channel_id=1, source_target_pairs={{0,128},{64,192},{128,0},{192,64},{1,129},{65,193},{129,1},{193,65... | collective-permute-start | bytes 786440 | tf_op jit(solution)/shard_map/ppermute | solution.py:392
  157.5 1.8 %collective-permute-start.24 = (f32[8,32,256]{2,1,0:T(8,128)}, f32[8,32,256]{2,1,0:T(8,128)S(1)}, u32[]{:S(2)}, u32[]{:S(2)}) collective-permute-start(f32[8,32,256]{2,1,0:T(8,128)} %get-tuple-element.62), channel_id=1, source_target_pairs={{0,192},{64,128},{128,64},{192,0},{1,193},{65,129},{129,65},{193,1... | collective-permute-start | bytes 786440 | tf_op jit(solution)/shard_map/ppermute | solution.py:392
  159.3 5.6 %finished.1 = f32[512,512]{1,0:T(8,128)} custom-call(s32[1]{0:T(128)} %bitcast.1.core_ref, f32[512,512]{1,0:T(8,128)S(1)} %copy-done.2, f32[512,512]{1,0:T(8,128)S(1)} %collective-permute-done.21.other_ref), custom_call_target="tpu_custom_call" | custom-call | flops 6000000000 | bytes 2097152 | tf_op jit(solution)/shard_map/finished/pallas_call | solution.py:264
  165.0 4.5 %collective-permute-done.23.refs_2_ = f32[8,32,256]{2,1,0:T(8,128)S(1)} collective-permute-done((f32[8,32,256]{2,1,0:T(8,128)}, f32[8,32,256]{2,1,0:T(8,128)S(1)}, u32[]{:S(2)}, u32[]{:S(2)}) %collective-permute-start.23) | collective-permute-done | bytes 262176 | tf_op jit(solution)/shard_map/ppermute | solution.py:392
  169.5 2.0 %collective-permute-done.24.refs_3_ = f32[8,32,256]{2,1,0:T(8,128)S(1)} collective-permute-done((f32[8,32,256]{2,1,0:T(8,128)}, f32[8,32,256]{2,1,0:T(8,128)S(1)}, u32[]{:S(2)}, u32[]{:S(2)}) %collective-permute-start.24) | collective-permute-done | bytes 262176 | tf_op jit(solution)/shard_map/ppermute | solution.py:392
  171.5 1.6 placed.1
  (39 shorter events, 0.2 us)
Async XLA Ops:
  2.0 32.7 %collective-permute-start.2 = (f32[3,256,128]{2,1,0:T(8,128)S(1)}, f32[3,256,128]{2,1,0:T(8,128)S(1)}, u32[]{:S(2)}, u32[]{:S(2)}) collective-permute-start(f32[3,256,128]{2,1,0:T(8,128)S(1)} %get-tuple-element.74), channel_id=1, source_target_pairs={{0,192},{64,128},{128,64},{192,0},{1,193},{65,129},{129,65},{193,1... | collective-permute-start | bytes 1179656 | tf_op jit(solution)/shard_map/ppermute | solution.py:392
  6.4 20.8 %collective-permute-start.8 = (f32[1,256,128]{2,1,0:T(8,128)S(1)}, f32[1,256,128]{2,1,0:T(8,128)S(1)}, u32[]{:S(2)}, u32[]{:S(2)}) collective-permute-start(f32[1,256,128]{2,1,0:T(8,128)S(1)} %get-tuple-element.68), channel_id=1, source_target_pairs={{0,192},{64,128},{128,64},{192,0},{1,193},{65,129},{129,65},{193,1... | collective-permute-start | bytes 393224 | tf_op jit(solution)/shard_map/ppermute | solution.py:392
  6.5 22.2 %collective-permute-start.7 = (f32[1,256,128]{2,1,0:T(8,128)S(1)}, f32[1,256,128]{2,1,0:T(8,128)S(1)}, u32[]{:S(2)}, u32[]{:S(2)}) collective-permute-start(f32[1,256,128]{2,1,0:T(8,128)S(1)} %get-tuple-element.69), channel_id=1, source_target_pairs={{0,128},{64,192},{128,0},{192,64},{1,129},{65,193},{129,1},{193,65... | collective-permute-start | bytes 393224 | tf_op jit(solution)/shard_map/ppermute | solution.py:392
  8.2 20.5 %collective-permute-start.6 = (f32[1,256,128]{2,1,0:T(8,128)S(1)}, f32[1,256,128]{2,1,0:T(8,128)S(1)}, u32[]{:S(2)}, u32[]{:S(2)}) collective-permute-start(f32[1,256,128]{2,1,0:T(8,128)S(1)} %get-tuple-element.70), channel_id=1, source_target_pairs={{0,64},{64,0},{128,192},{192,128},{1,65},{65,1},{129,193},{193,129... | collective-permute-start | bytes 393224 | tf_op jit(solution)/shard_map/ppermute | solution.py:392
  9.8 28.9 %collective-permute-start.1 = (f32[3,256,128]{2,1,0:T(8,128)S(1)}, f32[3,256,128]{2,1,0:T(8,128)S(1)}, u32[]{:S(2)}, u32[]{:S(2)}) collective-permute-start(f32[3,256,128]{2,1,0:T(8,128)S(1)} %get-tuple-element.75), channel_id=1, source_target_pairs={{0,128},{64,192},{128,0},{192,64},{1,129},{65,193},{129,1},{193,65... | collective-permute-start | bytes 1179656 | tf_op jit(solution)/shard_map/ppermute | solution.py:392
  27.2 0.6 copy-start.9
  27.8 10.9 %collective-permute-start = (f32[3,256,128]{2,1,0:T(8,128)S(1)}, f32[3,256,128]{2,1,0:T(8,128)S(1)}, u32[]{:S(2)}, u32[]{:S(2)}) collective-permute-start(f32[3,256,128]{2,1,0:T(8,128)S(1)} %get-tuple-element.76), channel_id=1, source_target_pairs={{0,64},{64,0},{128,192},{192,128},{1,65},{65,1},{129,193},{193,129... | collective-permute-start | bytes 1179656 | tf_op jit(solution)/shard_map/ppermute | solution.py:392
  28.8 2.2 %copy-start.10 = (f32[1,256,128]{2,1,0:T(8,128)}, f32[1,256,128]{2,1,0:T(8,128)S(1)}, u32[]{:S(2)}) copy-start(f32[1,256,128]{2,1,0:T(8,128)S(1)} %collective-permute-done.7.refs_3_) | copy-start | bytes 393220
  28.8 2.2 %copy-start.11 = (f32[1,256,128]{2,1,0:T(8,128)}, f32[1,256,128]{2,1,0:T(8,128)S(1)}, u32[]{:S(2)}) copy-start(f32[1,256,128]{2,1,0:T(8,128)S(1)} %collective-permute-done.6.refs_2_) | copy-start | bytes 393220
  31.0 18.3 %collective-permute-start.11 = (f32[3,256,128]{2,1,0:T(8,128)}, f32[3,256,128]{2,1,0:T(8,128)S(1)}, u32[]{:S(2)}, u32[]{:S(2)}) collective-permute-start(f32[3,256,128]{2,1,0:T(8,128)} %get-tuple-element.65), channel_id=1, source_target_pairs={{0,192},{64,128},{128,64},{192,0},{1,193},{65,129},{129,65},{193,1... | collective-permute-start | bytes 1179656 | tf_op jit(solution)/shard_map/ppermute | solution.py:392
  33.4 20.5 %collective-permute-start.10 = (f32[3,256,128]{2,1,0:T(8,128)S(1)}, f32[3,256,128]{2,1,0:T(8,128)S(1)}, u32[]{:S(2)}, u32[]{:S(2)}) collective-permute-start(f32[3,256,128]{2,1,0:T(8,128)S(1)} %get-tuple-element.66), channel_id=1, source_target_pairs={{0,128},{64,192},{128,0},{192,64},{1,129},{65,193},{129,1},{193,65... | collective-permute-start | bytes 1179656 | tf_op jit(solution)/shard_map/ppermute | solution.py:392
  34.7 15.0 %copy-start.3 = (f32[3,256,128]{2,1,0:T(8,128)}, f32[3,256,128]{2,1,0:T(8,128)S(1)}, u32[]{:S(2)}) copy-start(f32[3,256,128]{2,1,0:T(8,128)S(1)} %collective-permute-done.2.refs_4_) | copy-start | bytes 1179652
  34.7 19.3 %collective-permute-start.9 = (f32[3,256,128]{2,1,0:T(8,128)S(1)}, f32[3,256,128]{2,1,0:T(8,128)}, u32[]{:S(2)}, u32[]{:S(2)}) collective-permute-start(f32[3,256,128]{2,1,0:T(8,128)S(1)} %get-tuple-element.67), channel_id=1, source_target_pairs={{0,64},{64,0},{128,192},{192,128},{1,65},{65,1},{129,193},{193,129... | collective-permute-start | bytes 1179656 | tf_op jit(solution)/shard_map/ppermute | solution.py:392
  38.7 11.0 %copy-start.4 = (f32[3,256,128]{2,1,0:T(8,128)}, f32[3,256,128]{2,1,0:T(8,128)S(1)}, u32[]{:S(2)}) copy-start(f32[3,256,128]{2,1,0:T(8,128)S(1)} %collective-permute-done.1.refs_3_) | copy-start | bytes 1179652
  38.7 11.0 %copy-start.5 = (f32[3,256,128]{2,1,0:T(8,128)}, f32[3,256,128]{2,1,0:T(8,128)S(1)}, u32[]{:S(2)}) copy-start(f32[3,256,128]{2,1,0:T(8,128)S(1)} %collective-permute-done.refs_2_) | copy-start | bytes 1179652
  40.0 19.0 %collective-permute-start.5 = (f32[1,256,128]{2,1,0:T(8,128)S(1)}, f32[1,256,128]{2,1,0:T(8,128)S(1)}, u32[]{:S(2)}, u32[]{:S(2)}) collective-permute-start(f32[1,256,128]{2,1,0:T(8,128)S(1)} %get-tuple-element.71), channel_id=1, source_target_pairs={{0,192},{64,128},{128,64},{192,0},{1,193},{65,129},{129,65},{193,1... | collective-permute-start | bytes 393224 | tf_op jit(solution)/shard_map/ppermute | solution.py:392
  42.1 17.3 %collective-permute-start.4 = (f32[1,256,128]{2,1,0:T(8,128)S(1)}, f32[1,256,128]{2,1,0:T(8,128)S(1)}, u32[]{:S(2)}, u32[]{:S(2)}) collective-permute-start(f32[1,256,128]{2,1,0:T(8,128)S(1)} %get-tuple-element.72), channel_id=1, source_target_pairs={{0,128},{64,192},{128,0},{192,64},{1,129},{65,193},{129,1},{193,65... | collective-permute-start | bytes 393224 | tf_op jit(solution)/shard_map/ppermute | solution.py:392
  49.2 4.8 %copy-start.6 = (f32[3,256,128]{2,1,0:T(8,128)}, f32[3,256,128]{2,1,0:T(8,128)S(1)}, u32[]{:S(2)}) copy-start(f32[3,256,128]{2,1,0:T(8,128)S(1)} %collective-permute-done.11.refs_4_) | copy-start | bytes 1179652
  49.2 10.2 %collective-permute-start.3 = (f32[1,256,128]{2,1,0:T(8,128)S(1)}, f32[1,256,128]{2,1,0:T(8,128)S(1)}, u32[]{:S(2)}, u32[]{:S(2)}) collective-permute-start(f32[1,256,128]{2,1,0:T(8,128)S(1)} %get-tuple-element.73), channel_id=1, source_target_pairs={{0,64},{64,0},{128,192},{192,128},{1,65},{65,1},{129,193},{193,129... | collective-permute-start | bytes 393224 | tf_op jit(solution)/shard_map/ppermute | solution.py:392
  54.0 0.8 copy-start.7
  59.1 0.7 copy-start.12
  59.4 0.7 copy-start.13
  59.5 0.7 copy-start.14
  64.7 6.0 %collective-permute-start.12 = (f32[640,128]{1,0:T(8,128)S(1)}, f32[640,128]{1,0:T(8,128)S(1)}, u32[]{:S(2)}, u32[]{:S(2)}) collective-permute-start(f32[640,128]{1,0:T(8,128)S(1)} %constant_dynamic-slice_fusion), channel_id=1, source_target_pairs={{0,1},{1,0},{2,3},{3,2},{4,5},{5,4},{6,7},{7,6},{8,9},{9,8},{10,11... | collective-permute-start | bytes 983048 | tf_op jit(solution)/shard_map/ppermute | solution.py:392
  83.0 4.9 %collective-permute-start.14 = (f32[160,128]{1,0:T(8,128)S(1)}, f32[160,128]{1,0:T(8,128)S(1)}, u32[]{:S(2)}, u32[]{:S(2)}) collective-permute-start(f32[160,128]{1,0:T(8,128)S(1)} %fusion.1), channel_id=1, source_target_pairs={{0,32},{16,48},{32,0},{48,16},{1,33},{17,49},{33,1},{49,17},{2,34}... | collective-permute-start | bytes 245768 | tf_op jit(solution)/shard_map/ppermute | solution.py:392
  85.6 5.1 %collective-permute-start.15 = (f32[160,128]{1,0:T(8,128)S(1)}, f32[160,128]{1,0:T(8,128)S(1)}, u32[]{:S(2)}, u32[]{:S(2)}) collective-permute-start(f32[160,128]{1,0:T(8,128)S(1)} %fusion.1), channel_id=1, source_target_pairs={{0,48},{16,32},{32,16},{48,0},{1,49},{17,33},{33,17},{49,1},{2,50}... | collective-permute-start | bytes 245768 | tf_op jit(solution)/shard_map/ppermute | solution.py:392
  86.4 4.3 %collective-permute-start.13 = (f32[160,128]{1,0:T(8,128)S(1)}, f32[160,128]{1,0:T(8,128)S(1)}, u32[]{:S(2)}, u32[]{:S(2)}) collective-permute-start(f32[160,128]{1,0:T(8,128)S(1)} %fusion.1), channel_id=1, source_target_pairs={{0,16},{16,0},{32,48},{48,32},{1,17},{17,1},{33,49},{49,33},{2,18}... | collective-permute-start | bytes 245768 | tf_op jit(solution)/shard_map/ppermute | solution.py:392
  90.8 3.4 %collective-permute-start.16 = (f32[160,128]{1,0:T(8,128)S(1)}, f32[160,128]{1,0:T(8,128)S(1)}, u32[]{:S(2)}, u32[]{:S(2)}) collective-permute-start(f32[160,128]{1,0:T(8,128)S(1)} %add_add_fusion.1), channel_id=1, source_target_pairs={{0,2},{2,0},{4,6},{6,4},{8,10},{10,8},{12,14},{14,12},{1,3},{3,1},... | collective-permute-start | bytes 245768 | tf_op jit(solution)/shard_map/ppermute | solution.py:392
  94.1 8.1 %collective-permute-start.19 = (f32[160,128]{1,0:T(8,128)S(1)}, f32[160,128]{1,0:T(8,128)S(1)}, u32[]{:S(2)}, u32[]{:S(2)}) collective-permute-start(f32[160,128]{1,0:T(8,128)S(1)} %add.75), channel_id=1, source_target_pairs={{0,12},{2,14},{4,8},{6,10},{8,4},{10,6},{12,0},{14,2},{1,13},{3,15... | collective-permute-start | bytes 245768 | tf_op jit(solution)/shard_map/ppermute | solution.py:392
  99.9 8.0 %collective-permute-start.18 = (f32[160,128]{1,0:T(8,128)S(1)}, f32[160,128]{1,0:T(8,128)S(1)}, u32[]{:S(2)}, u32[]{:S(2)}) collective-permute-start(f32[160,128]{1,0:T(8,128)S(1)} %add.75), channel_id=1, source_target_pairs={{0,8},{2,10},{4,12},{6,14},{8,0},{10,2},{12,4},{14,6},{1,9},{3,11}... | collective-permute-start | bytes 245768 | tf_op jit(solution)/shard_map/ppermute | solution.py:392
  100.9 7.0 %collective-permute-start.17 = (f32[160,128]{1,0:T(8,128)S(1)}, f32[160,128]{1,0:T(8,128)S(1)}, u32[]{:S(2)}, u32[]{:S(2)}) collective-permute-start(f32[160,128]{1,0:T(8,128)S(1)} %add.75), channel_id=1, source_target_pairs={{0,4},{2,6},{4,0},{6,2},{8,12},{10,14},{12,8},{14,10},{1,5},{3,7},... | collective-permute-start | bytes 245768 | tf_op jit(solution)/shard_map/ppermute | solution.py:392
  144.7 14.6 %copy-start.2 = (f32[512,512]{1,0:T(8,128)S(1)}, f32[512,512]{1,0:T(8,128)}, u32[]{:S(2)}) copy-start(f32[512,512]{1,0:T(8,128)} %get-tuple-element.58.own_ref) | copy-start | bytes 3145732
  144.7 3.7 %collective-permute-start.20 = (f32[128,512]{1,0:T(8,128)}, f32[128,512]{1,0:T(8,128)S(1)}, u32[]{:S(2)}, u32[]{:S(2)}) collective-permute-start(f32[128,512]{1,0:T(8,128)} %get-tuple-element.46.refs_1_), channel_id=1, source_target_pairs={{0,1},{1,0},{2,3},{3,2},{4,5},{5,4},{6,7},{7,6},{8,9},{9,8},{10,11... | collective-permute-start | bytes 786440 | tf_op jit(solution)/shard_map/ppermute | solution.py:392
  148.4 0.7 copy-start.8
  148.4 10.9 %collective-permute-start.21 = (f32[512,512]{1,0:T(8,128)}, f32[512,512]{1,0:T(8,128)S(1)}, u32[]{:S(2)}, u32[]{:S(2)}) collective-permute-start(f32[512,512]{1,0:T(8,128)} %get-tuple-element.58.own_ref), channel_id=1, source_target_pairs={{0,1},{1,0},{2,3},{3,2},{4,5},{5,4},{6,7},{7,6},{8,9},{9,8},{10,11... | collective-permute-start | bytes 3145736 | tf_op jit(solution)/shard_map/ppermute | solution.py:392
  155.4 9.6 %collective-permute-start.22 = (f32[8,32,256]{2,1,0:T(8,128)}, f32[8,32,256]{2,1,0:T(8,128)S(1)}, u32[]{:S(2)}, u32[]{:S(2)}) collective-permute-start(f32[8,32,256]{2,1,0:T(8,128)} %get-tuple-element.60), channel_id=1, source_target_pairs={{0,64},{64,0},{128,192},{192,128},{1,65},{65,1},{129,193},{193,129... | collective-permute-start | bytes 786440 | tf_op jit(solution)/shard_map/ppermute | solution.py:392
  155.8 13.7 %collective-permute-start.23 = (f32[8,32,256]{2,1,0:T(8,128)}, f32[8,32,256]{2,1,0:T(8,128)S(1)}, u32[]{:S(2)}, u32[]{:S(2)}) collective-permute-start(f32[8,32,256]{2,1,0:T(8,128)} %get-tuple-element.61), channel_id=1, source_target_pairs={{0,128},{64,192},{128,0},{192,64},{1,129},{65,193},{129,1},{193,65... | collective-permute-start | bytes 786440 | tf_op jit(solution)/shard_map/ppermute | solution.py:392
  157.5 13.9 %copy-start = (f32[8,32,256]{2,1,0:T(8,128)S(1)}, f32[8,32,256]{2,1,0:T(8,128)}, u32[]{:S(2)}) copy-start(f32[8,32,256]{2,1,0:T(8,128)} %get-tuple-element.59.refs_0_) | copy-start | bytes 786436
  157.5 13.9 %copy-start.1 = (s32[2]{0:T(128)S(1)}, s32[2]{0:T(128)}, u32[]{:S(2)}) copy-start(s32[2]{0:T(128)} %pad_add_fusion.refs_0_.me_ref) | copy-start | bytes 28
  157.5 13.9 %collective-permute-start.24 = (f32[8,32,256]{2,1,0:T(8,128)}, f32[8,32,256]{2,1,0:T(8,128)S(1)}, u32[]{:S(2)}, u32[]{:S(2)}) collective-permute-start(f32[8,32,256]{2,1,0:T(8,128)} %get-tuple-element.62), channel_id=1, source_target_pairs={{0,192},{64,128},{128,64},{192,0},{1,193},{65,129},{129,65},{193,1... | collective-permute-start | bytes 786440 | tf_op jit(solution)/shard_map/ppermute | solution.py:392

commit v5 on v4

--- a/solution.py
+++ b/solution.py
@@ -10,7 +10,9 @@
 NB = 4
 W = 128
 PAIRS = [(k, l) for k in range(NB) for l in range(k, NB)]
-COUNTS = (1, 3, 3, 1)
+COUNTS = (2, 6)
+STEP = 2
+SMALL = 14 * 1024 * 1024
 VMEM_LIMIT = 60 * 1024 * 1024
 
 
@@ -23,65 +25,76 @@
     return lax.dot_general(a, b, (dims, ((), ())), preferred_element_type=jnp.float32)
 
 
-def gram_kernel(scale, start, me_ref, field, *refs):
-    others, refs = refs[: NB - 1], refs[NB - 1 :]
-    before, (out_ref, high_ref, low_ref, rows, high, low, total, sems) = refs[:-8], refs[-8:]
-    cells, snaps, size = rows.shape
+def gram_kernel(scale, counts, me_ref, field, *refs):
+    count = (NB - 1) * len(counts)
+    others, refs = refs[:count], refs[count:]
+    out_ref, high_ref, low_ref, rows, high, low, hh, hl, total, in_sems, out_sems = refs
+    _, snaps, size = rows.shape
     me = me_ref[0]
-    copies = []
-    for b, piece in enumerate((field.at[me, pl.ds(start, cells)], *others)):
-        place = pl.multiple_of((me ^ b) * W, W)
-        copies.append(pltpu.make_async_copy(piece, rows.at[:, :, pl.ds(place, W)], sems.at[b]))
-    if before:
-        copies.append(pltpu.make_async_copy(before[0], total, sems.at[NB]))
-    for copy in copies:
-        copy.start()
-    for copy in copies:
-        copy.wait()
-    high[...], low[...] = split(rows[...].reshape(cells * snaps, size))
-    halves = [
-        pltpu.make_async_copy(high, high_ref, sems.at[NB + 1]),
-        pltpu.make_async_copy(low, low_ref, sems.at[NB + 2]),
-    ]
-    for copy in halves:
-        copy.start()
-    left = high[...].T
-    hh = contract(left, high[...], ((1,), (0,)))
-    hl = contract(left, low[...], ((1,), (0,)))
+    groups, start = [], 0
+    for c, cells in enumerate(counts):
+        groups += [(c, at, start + at) for at in range(0, cells, STEP)]
+        start += cells
+    arrivals = []
+    for g, (c, at, cell) in enumerate(groups):
+        pieces = [field.at[me, pl.ds(cell, STEP)]]
+        pieces += [ref.at[pl.ds(at, STEP)] for ref in others[(NB - 1) * c : (NB - 1) * (c + 1)]]
+        arrivals.append([])
+        for b, piece in enumerate(pieces):
+            place = pl.multiple_of((me ^ b) * W, W)
+            target = rows.at[pl.ds(cell, STEP), :, pl.ds(place, W)]
+            arrivals[g].append(pltpu.make_async_copy(piece, target, in_sems.at[g, b]))
+            arrivals[g][b].start()
+    leaving = []
+    for g, (_, _, cell) in enumerate(groups):
+        for copy in arrivals[g]:
+            copy.wait()
+        at = slice(cell * snaps, (cell + STEP) * snaps)
+        part, rest = split(rows[cell : cell + STEP].reshape(STEP * snaps, size))
+        high[at, :], low[at, :] = part, rest
+        for n, (source, target) in enumerate(((high, high_ref), (low, low_ref))):
+            leaving.append(pltpu.make_async_copy(source.at[at], target.at[at], out_sems.at[g, n]))
+            leaving[-1].start()
+        left = part.T
+        for total_ref, right in ((hh, part), (hl, rest)):
+            product = contract(left, right, ((1,), (0,)))
+            total_ref[...] = product if g == 0 else total_ref[...] + product
     for n, (k, l) in enumerate(PAIRS):
         ks, ls = slice(W * k, W * k + W), slice(W * l, W * l + W)
-        part = (hh[ks, ls] + (hl[ks, ls] + hl[ls, ks].T)) * scale
-        total[n] = total[n] + part if before else part
-    result = pltpu.make_async_copy(total, out_ref, sems.at[NB + 3])
-    result.start()
-    for copy in (*halves, result):
+        total[n] = (hh[ks, ls] + (hl[ks, ls] + hl[ls, ks].T)) * scale
+    leaving.append(pltpu.make_async_copy(total, out_ref, out_sems.at[len(groups), 0]))
+    leaving[-1].start()
+    for copy in leaving:
         copy.wait()
 
 
-def gram_chunk(me, field, start, cells, arrived, before, scale):
-    snaps = field.shape[2]
-    rows = cells * snaps
+def gram_blocks(me, field, counts, arrived, scale):
+    _, cells, snaps, _ = field.shape
+    rows, size = cells * snaps, NB * W
     gram = (len(PAIRS), W, W)
-    halves = jax.ShapeDtypeStruct((rows, NB * W), jnp.bfloat16)
+    halves = jax.ShapeDtypeStruct((rows, size), jnp.bfloat16)
     anywhere = pl.BlockSpec(memory_space=pl.ANY)
-    operands = [field, *arrived] + ([] if before is None else [before])
+    operands = [field] + [piece for pieces in arrived for piece in pieces]
     return pl.pallas_call(
-        lambda *refs: gram_kernel(scale, start, *refs),
+        lambda *refs: gram_kernel(scale, counts, *refs),
         in_specs=[pl.BlockSpec(memory_space=pltpu.SMEM)] + [anywhere] * len(operands),
         out_specs=[anywhere] * 3,
         out_shape=[jax.ShapeDtypeStruct(gram, jnp.float32), halves, halves],
         scratch_shapes=[
-            pltpu.VMEM((cells, snaps, NB * W), jnp.float32),
+            pltpu.VMEM((cells, snaps, size), jnp.float32),
             pltpu.VMEM(halves.shape, jnp.bfloat16),
             pltpu.VMEM(halves.shape, jnp.bfloat16),
+            pltpu.VMEM((size, size), jnp.float32),
+            pltpu.VMEM((size, size), jnp.float32),
             pltpu.VMEM(gram, jnp.float32),
-            pltpu.SemaphoreType.DMA((NB + 4,)),
+            pltpu.SemaphoreType.DMA((cells // STEP, NB)),
+            pltpu.SemaphoreType.DMA((cells // STEP + 1, 2)),
         ],
         compiler_params=pltpu.CompilerParams(vmem_limit_bytes=VMEM_LIMIT),
         cost_estimate=pl.CostEstimate(
-            flops=4 * rows * (NB * W) ** 2, bytes_accessed=8 * rows * NB * W, transcendentals=0
+            flops=4 * rows * size**2, bytes_accessed=8 * rows * size, transcendentals=0
         ),
-        name="gram_chunk",
+        name="gram_blocks",
     )(me, *operands)
 
 
@@ -154,7 +167,7 @@
         gram[W * k : W * k + W, W * l : W * l + W] = block
         if k != l:
             gram[W * l : W * l + W, W * k : W * k + W] = block.T
-    basis_ref[...] = seed_ref[...].T
+    basis_ref[...] = seed_ref[...]
 
     def step(_, carry):
         imaged = exact(basis_ref[...], gram[...])
@@ -202,48 +215,34 @@
         copy.wait()
 
 
-def either_kernel(core_ref, g_ref, seed_ref, basis_ref, triangle_ref, gram, blocks, seed, basis, triangle, sems):
-    copied(
-        pltpu.make_async_copy(g_ref, blocks, sems.at[0]),
-        pltpu.make_async_copy(seed_ref, seed, sems.at[1]),
-    )
-
+def either_kernel(core_ref, g_ref, seed_ref, basis_ref, triangle_ref, gram):
     @pl.when(core_ref[0] == 0)
     def _():
-        orthonormal_steps(blocks, seed, basis, gram)
-        copied(pltpu.make_async_copy(basis, basis_ref, sems.at[2]))
+        orthonormal_steps(g_ref, seed_ref, basis_ref, gram)
 
     @pl.when(core_ref[0] != 0)
     def _():
-        triangle_steps(blocks, triangle, gram)
-        copied(pltpu.make_async_copy(triangle, triangle_ref, sems.at[3]))
-
-
-def basis_or_triangle(core, gram, seed):
+        triangle_steps(g_ref, triangle_ref, gram)
+
+
+def basis_or_triangle(core, gram, seed_rows):
     size = NB * W
-    anywhere = pl.BlockSpec(memory_space=pl.ANY)
+    vmem = pl.BlockSpec(memory_space=pltpu.VMEM)
     return pl.pallas_call(
         either_kernel,
-        in_specs=[pl.BlockSpec(memory_space=pltpu.SMEM), anywhere, anywhere],
-        out_specs=[anywhere, anywhere],
+        in_specs=[pl.BlockSpec(memory_space=pltpu.SMEM), vmem, vmem],
+        out_specs=[vmem, vmem],
         out_shape=[
-            jax.ShapeDtypeStruct(seed.shape[::-1], jnp.float32),
+            jax.ShapeDtypeStruct(seed_rows.shape, jnp.float32),
             jax.ShapeDtypeStruct((size, size), jnp.float32),
         ],
-        scratch_shapes=[
-            pltpu.VMEM((size, size), jnp.float32),
-            pltpu.VMEM(gram.shape, jnp.float32),
-            pltpu.VMEM(seed.shape, jnp.float32),
-            pltpu.VMEM(seed.shape[::-1], jnp.float32),
-            pltpu.VMEM((size, size), jnp.float32),
-            pltpu.SemaphoreType.DMA((4,)),
-        ],
-        compiler_params=pltpu.CompilerParams(vmem_limit_bytes=VMEM_LIMIT),
+        scratch_shapes=[pltpu.VMEM((size, size), jnp.float32)],
+        compiler_params=pltpu.CompilerParams(vmem_limit_bytes=SMALL),
         cost_estimate=pl.CostEstimate(
             flops=40_000_000_000, bytes_accessed=8 * size * size, transcendentals=0
         ),
         name="basis_or_triangle",
-    )(core, gram, seed)
+    )(core, gram, seed_rows)
 
 
 def finish_kernel(core_ref, own_ref, other_ref, out_ref, triangle, sems):
@@ -276,74 +275,39 @@
 
 
 def core_kernel(counts, snaps, me_ref, own_ref, other_ref, *refs):
-    n = 2 * len(counts)
-    sources, refs = refs[:n], refs[n:]
-    mode_ref, *out_refs = refs[: 1 + NB]
-    refs = refs[1 + NB :]
-    halves, (basis, mode, parts, in_sems, out_sems) = refs[:n], refs[n:]
-    me, part = me_ref[0], basis.shape[0] // NB
-    arrivals = [
-        pltpu.make_async_copy(source, half, in_sems.at[i])
-        for i, (source, half) in enumerate(zip(sources, halves))
-    ]
-
-    for copy in arrivals:
-        copy.start()
-
-    @pl.when(me_ref[1] == 0)
-    def _():
-        copied(pltpu.make_async_copy(own_ref, basis, in_sems.at[n]))
-
-    @pl.when(me_ref[1] != 0)
-    def _():
-        copied(pltpu.make_async_copy(other_ref, basis, in_sems.at[n]))
-
-    mode[...] = basis[...].T
-    leaving = [pltpu.make_async_copy(mode, mode_ref, out_sems.at[NB])]
-    leaving[0].start()
+    halves, (mode_ref, *outs), basis = refs[: 2 * len(counts)], refs[2 * len(counts) : -1], refs[-1]
+    me, part = me_ref[0], own_ref.shape[0] // NB
+    basis[...] = jnp.where(me_ref[1] == 0, own_ref[...], other_ref[...])
+    mode_ref[...] = basis[...].T
     turned = [basis[pl.ds(pl.multiple_of((me ^ b) * part, part), part), :] for b in range(NB)]
     high, low = split(jnp.concatenate(turned, axis=0).T)
     weights = jnp.concatenate([high, low], axis=1)
     cell = 0
     for c, count in enumerate(counts):
         high_ref, low_ref = halves[2 * c : 2 * c + 2]
-        arrivals[2 * c].wait()
-        arrivals[2 * c + 1].wait()
         for i in range(count):
             rows = slice(snaps * i, snaps * i + snaps)
             both = contract(high_ref[rows, :], weights, ((1,), (0,)))
             more = contract(low_ref[rows, :], high, ((1,), (0,)))
             core = (both[:, :W] + (both[:, W:] + more)).T
             for b in range(NB):
-                parts[b, cell] = core[part * b : part * b + part, :]
+                outs[b][cell] = core[part * b : part * b + part, :]
             cell += 1
-    for b in range(NB):
-        leaving.append(pltpu.make_async_copy(parts.at[b], out_refs[b], out_sems.at[b]))
-        leaving[-1].start()
-    for copy in leaving:
-        copy.wait()
 
 
 def core_parts(place, own_basis, other_basis, halves, counts, snaps):
     rank, size = own_basis.shape
     cells = sum(counts)
     operands = [half for pair in halves for half in pair]
-    anywhere = pl.BlockSpec(memory_space=pl.ANY)
+    vmem = pl.BlockSpec(memory_space=pltpu.VMEM)
     return pl.pallas_call(
         lambda *refs: core_kernel(counts, snaps, *refs),
-        in_specs=[pl.BlockSpec(memory_space=pltpu.SMEM)] + [anywhere] * (2 + len(operands)),
-        out_specs=[anywhere] * (1 + NB),
+        in_specs=[pl.BlockSpec(memory_space=pltpu.SMEM)] + [vmem] * (2 + len(operands)),
+        out_specs=[vmem] * (1 + NB),
         out_shape=[jax.ShapeDtypeStruct((size, rank), jnp.float32)]
         + [jax.ShapeDtypeStruct((cells, rank // NB, snaps), jnp.float32)] * NB,
-        scratch_shapes=[pltpu.VMEM(half.shape, half.dtype) for half in operands]
-        + [
-            pltpu.VMEM((rank, size), jnp.float32),
-            pltpu.VMEM((size, rank), jnp.float32),
-            pltpu.VMEM((NB, cells, rank // NB, snaps), jnp.float32),
-            pltpu.SemaphoreType.DMA((len(operands) + 1,)),
-            pltpu.SemaphoreType.DMA((NB + 1,)),
-        ],
-        compiler_params=pltpu.CompilerParams(vmem_limit_bytes=VMEM_LIMIT),
+        scratch_shapes=[pltpu.VMEM((rank, size), jnp.float32)],
+        compiler_params=pltpu.CompilerParams(vmem_limit_bytes=SMALL),
         cost_estimate=pl.CostEstimate(
             flops=6 * cells * snaps * size * rank,
             bytes_accessed=5 * cells * snaps * size,
@@ -422,31 +386,26 @@
     scale = 1.0 / (cells // NB * snaps * devices)
     counts = COUNTS
 
-    gram, halves, start = None, [], 0
-    arrived = []
-    for c, count in enumerate(counts):
-        later, got = field, {}
-        if c >= 2:
-            later, *arrived[c - 2] = lax.optimization_barrier((field, *arrived[c - 2]))
+    arrived, start, later = [], 0, field
+    for count in counts:
+        got, sends = {}, []
         for bits in (2, 1, 3):
-            send = lax.dynamic_slice(
-                later, (me ^ bits, start, 0, 0), (1, count, snaps, width)
-            )[0]
+            send = lax.dynamic_slice(later, (me ^ bits, start, 0, 0), (1, count, snaps, width))[0]
             got[bits] = exchanged(send, "x", bits)
+            sends.append(send)
+        later, *_ = lax.optimization_barrier((later, *sends))
         arrived.append([got[bits] for bits in (1, 2, 3)])
         start += count
-    start = 0
-    for count, others in zip(counts, arrived):
-        gram, high, low = gram_chunk(place, field, start, count, others, gram, scale)
-        halves.append((high, low))
-        start += count
+    gram, high, low = gram_blocks(place, field, counts, arrived, scale)
 
     gram = summed_over_devices(gram.reshape(-1, W)).reshape(gram.shape)
-    basis, triangle = basis_or_triangle(place[1:], gram, seed_subspace)
+    basis, triangle = basis_or_triangle(place[1:], gram, seed_subspace.T)
     other_basis = exchanged(basis, "core", 1)
     triangle, other_basis = lax.optimization_barrier((triangle, other_basis))
     other_triangle = exchanged(triangle, "core", 1)
-    mode_factor, *parts = core_parts(place, basis, other_basis, halves, counts, snaps)
+    mode_factor, *parts = core_parts(
+        place, basis, other_basis, [(high, low)], [cells // NB], snaps
+    )
     sent = {bits: exchanged(parts[bits], "x", bits) for bits in (2, 1, 3)}
     triangle = finished(place[1:], triangle, other_triangle)
     own_part, triangle = lax.optimization_barrier((parts[0], triangle))

time: 174 us -> 166 us (0.954)
  waiting for transfers between devices: 44.4 us -> 71.4 us
  Pallas kernels: 48.8 us -> 32.6 us
  blocking collectives: 28.1 us -> 16.4 us
  local copies, waits for them, and re-layouts: 9.33 us -> 4.88 us
  starting transfers between devices: 39.9 us -> 37.5 us
    ppermute x25 -> x19, waiting for transfers between devices: 44.4 us -> 65.7 us  [exchanged(): return lax.ppermute(block, axis, [(i, i ^ bits) for i in range(count)])]
    pallas_call x4 -> x1, Pallas kernels: 15.4 us -> 5.79 us  [gram_blocks(): pl.pallas_call(lambda *refs: gram_kernel(scale, counts, *refs), in_specs=...]
    all_to_all x1 -> x0, blocking collectives: 8.25 us -> none  [summed_over_devices(): whole = lax.all_to_all(copies, 'x', split_axis=0, concat_axis=0, tiled=True)]
    ppermute x25 -> x19, starting transfers between devices: 39.9 us -> 34.1 us  [exchanged(): return lax.ppermute(block, axis, [(i, i ^ bits) for i in range(count)])]
    all_to_all x0 -> x1, waiting for transfers between devices: none -> 5.7 us  [summed_over_devices(): whole = lax.all_to_all(copies, 'x', split_axis=0, concat_axis=0, tiled=True)]
    pallas_call x1, Pallas kernels: 6.21 us -> 2.01 us  [core_parts(): pl.pallas_call(lambda *refs: core_kernel(counts, snaps, *refs), in_specs=...]
    all_to_all x0 -> x1, starting transfers between devices: none -> 3.45 us  [summed_over_devices(): whole = lax.all_to_all(copies, 'x', split_axis=0, concat_axis=0, tiled=True)]
    squeeze x4 -> x2, local copies, waits for them, and re-layouts: 5.85 us -> 2.94 us  [local(): lax.dynamic_slice(later, (me ^ bits, start, 0, 0), (1, count, snaps, width))]
  transfers between devices with their start and end apart: 25 -> 20, of which waited for: 12 -> 13; matrix products, arithmetic and copies ran while one was open for 3% -> 0% of each run, Pallas kernels for 14% -> 4%
where the time goes in v5:
time: 166 us; the launch traced here: 165 us
  waiting for transfers between devices  71.4 us (43%)
  starting transfers between devices  37.5 us (23%)
  Pallas kernels  32.6 us (20%)
  blocking collectives  16.4 us (10%)
  local copies, waits for them, and re-layouts  4.88 us (3%)
  other arithmetic  1.68 us (1%)
    ppermute x19, waiting for transfers between devices, exchanged(): return lax.ppermute(block, axis, [(i, i ^ bits) for i in range(count)])  65.7 us
    ppermute x19, starting transfers between devices, exchanged(): return lax.ppermute(block, axis, [(i, i ^ bits) for i in range(count)])  34.1 us
    pallas_call x1, Pallas kernels, basis_or_triangle(): pl.pallas_call(either_kernel, in_specs=[pl.BlockSpec(memory_space=pltpu.S...  17.8 us
    all_to_all x1, blocking collectives, summed_over_devices(): lax.all_to_all(own.reshape(NB, half // NB, W), 'x', split_axis=0, concat_...  9.2 us
    all_gather x1, blocking collectives, summed_over_devices(): return lax.all_gather(whole, 'core', axis=0, tiled=True)  7.17 us
    pallas_call x1, Pallas kernels, gram_blocks(): pl.pallas_call(lambda *refs: gram_kernel(scale, counts, *refs), in_specs=...  5.79 us
    all_to_all x1, waiting for transfers between devices, summed_over_devices(): whole = lax.all_to_all(copies, 'x', split_axis=0, concat_axis=0, tiled=True)  5.7 us
    pallas_call x1, Pallas kernels, finished(): pl.pallas_call(finish_kernel, in_specs=[pl.BlockSpec(memory_space=pltpu.S...  5.37 us
  transfers between devices with their start and end apart: 20, of which 13 were waited for; matrix products, arithmetic and copies ran while one was open for 0% of the time, Pallas kernels for 4%

profile of v5, /device:TPU:1, one launch (start us, length us, event | category | flops | bytes accessed | tf_op | source)
XLA Modules:
  0.0 165.4 jit_solution(702553401832429272)
XLA Ops:
  0.7 1.2 dynamic-slice_bitcast_fusion.3
  1.8 1.8 %dynamic-slice_bitcast_fusion = (f32[6,256,128]{2,1,0:T(8,128)S(1)}, f32[6,256,128]{2,1,0:T(8,128)S(1)}, f32[6,256,128]{2,1,0:T(8,128)S(1)}) fusion(f32[4,8,256,128]{3,2,1,0:T(8,128)} %bitcast.30, s32[]{:T(128)S(6)} %select_n.20, s32[]{:T(128)S(6)} %select_n.19, s32[]{:T(128)S(6)} %select_n.18), kind=kLoop, calls=%fused_computation | loop fusion | bytes 4718604 | tf_op jit(solution)/shard_map/squeeze | solution.py:393
  3.6 2.1 %collective-permute-start.3 = (f32[6,256,128]{2,1,0:T(8,128)S(1)}, f32[6,256,128]{2,1,0:T(8,128)}, u32[]{:S(2)}, u32[]{:S(2)}) collective-permute-start(f32[6,256,128]{2,1,0:T(8,128)S(1)} %get-tuple-element.35), channel_id=1, source_target_pairs={{0,64},{64,0},{128,192},{192,128},{1,65},{65,1},{129,193},{193,129... | collective-permute-start | bytes 2359304 | tf_op jit(solution)/shard_map/ppermute | solution.py:356
  5.7 2.5 %collective-permute-start.4 = (f32[6,256,128]{2,1,0:T(8,128)S(1)}, f32[6,256,128]{2,1,0:T(8,128)}, u32[]{:S(2)}, u32[]{:S(2)}) collective-permute-start(f32[6,256,128]{2,1,0:T(8,128)S(1)} %get-tuple-element.34), channel_id=1, source_target_pairs={{0,128},{64,192},{128,0},{192,64},{1,129},{65,193},{129,1},{193,65... | collective-permute-start | bytes 2359304 | tf_op jit(solution)/shard_map/ppermute | solution.py:356
  8.2 0.0 collective-permute-start.5
  8.2 0.2 collective-permute-start
  8.4 3.7 %collective-permute-start.1 = (f32[2,256,128]{2,1,0:T(8,128)S(1)}, f32[2,256,128]{2,1,0:T(8,128)S(1)}, u32[]{:S(2)}, u32[]{:S(2)}) collective-permute-start(f32[2,256,128]{2,1,0:T(8,128)S(1)} %get-tuple-element.37), channel_id=1, source_target_pairs={{0,128},{64,192},{128,0},{192,64},{1,129},{65,193},{129,1},{193,65... | collective-permute-start | bytes 786440 | tf_op jit(solution)/shard_map/ppermute | solution.py:356
  12.0 32.1 %collective-permute-done.refs_2_ = f32[2,256,128]{2,1,0:T(8,128)S(1)} collective-permute-done((f32[2,256,128]{2,1,0:T(8,128)S(1)}, f32[2,256,128]{2,1,0:T(8,128)S(1)}, u32[]{:S(2)}, u32[]{:S(2)}) %collective-permute-start) | collective-permute-done | bytes 262176 | tf_op jit(solution)/shard_map/ppermute | solution.py:356
  44.2 0.0 copy-start.4
  44.2 3.8 %collective-permute-start.2 = (f32[2,256,128]{2,1,0:T(8,128)S(1)}, f32[2,256,128]{2,1,0:T(8,128)}, u32[]{:S(2)}, u32[]{:S(2)}) collective-permute-start(f32[2,256,128]{2,1,0:T(8,128)S(1)} %get-tuple-element.36), channel_id=1, source_target_pairs={{0,192},{64,128},{128,64},{192,0},{1,193},{65,129},{129,65},{193,1... | collective-permute-start | bytes 786440 | tf_op jit(solution)/shard_map/ppermute | solution.py:356
  47.9 0.6 pad_add_fusion.refs_0_.me_ref
  48.5 4.8 %collective-permute-done.1.refs_3_ = f32[2,256,128]{2,1,0:T(8,128)S(1)} collective-permute-done((f32[2,256,128]{2,1,0:T(8,128)S(1)}, f32[2,256,128]{2,1,0:T(8,128)S(1)}, u32[]{:S(2)}, u32[]{:S(2)}) %collective-permute-start.1) | collective-permute-done | bytes 262176 | tf_op jit(solution)/shard_map/ppermute | solution.py:356
  53.3 0.0 copy-start.5
  53.3 5.9 %collective-permute-done.2.refs_4_ = f32[2,256,128]{2,1,0:T(8,128)} collective-permute-done((f32[2,256,128]{2,1,0:T(8,128)S(1)}, f32[2,256,128]{2,1,0:T(8,128)}, u32[]{:S(2)}, u32[]{:S(2)}) %collective-permute-start.2) | collective-permute-done | bytes 262176 | tf_op jit(solution)/shard_map/ppermute | solution.py:356
  59.2 0.0 collective-permute-done.3.refs_5_
  59.2 0.0 collective-permute-done.4.refs_6_
  59.2 0.0 collective-permute-done.5.refs_7_
  59.2 0.0 copy-done.4
  59.2 0.0 copy-done.5
  59.2 5.8 %gram_blocks.1 = (f32[10,128,128]{2,1,0:T(8,128)}, bf16[2048,512]{1,0:T(8,128)(2,1)}, bf16[2048,512]{1,0:T(8,128)(2,1)}) custom-call(s32[2]{0:T(128)} %pad_add_fusion.refs_0_.me_ref, f32[4,8,256,128]{3,2,1,0:T(8,128)} %bitcast.31, f32[2,256,128]{2,1,0:T(8,128)} %copy-done.4, f32[2,256,128]{2,1,0:T(8,128)} %copy-done.5, ...), custom_call_target="tpu_custom_call" | custom-call | flops 2147483648 | bytes 8388608 | tf_op jit(solution)/shard_map/gram_blocks/pallas_call | solution.py:78
  65.0 0.0 copy-start.3
  65.0 1.0 constant_dynamic-slice_fusion
  66.1 1.0 collective-permute-start.6
  67.1 1.3 collective-permute-done.6
  68.4 1.0 dynamic-slice_add_fusion
  69.4 9.2 %all_to_all.10 = f32[4,160,128]{2,1,0:T(8,128)S(1)} all-to-all(f32[4,160,128]{2,1,0:T(8,128)S(1)} %bitcast.32), channel_id=1, replica_groups=mesh['x'=4,'y'=4,'z'=8,'core'=2] {'x'}, dimensions={0} | all-to-all | bytes 655360 | tf_op jit(solution)/shard_map/all_to_all | solution.py:365
  78.6 1.5 collective-permute-start.7
  80.1 2.6 %collective-permute-start.8 = (f32[160,128]{1,0:T(8,128)S(1)}, f32[160,128]{1,0:T(8,128)S(1)}, u32[]{:S(2)}, u32[]{:S(2)}) collective-permute-start(f32[160,128]{1,0:T(8,128)S(1)} %fusion.1), channel_id=1, source_target_pairs={{0,32},{16,48},{32,0},{48,16},{1,33},{17,49},{33,1},{49,17},{2,34}... | collective-permute-start | bytes 245768 | tf_op jit(solution)/shard_map/ppermute | solution.py:356
  82.8 0.0 collective-permute-start.9
  82.8 0.0 collective-permute-done.7
  82.8 2.7 %collective-permute-done.8 = f32[160,128]{1,0:T(8,128)S(1)} collective-permute-done((f32[160,128]{1,0:T(8,128)S(1)}, f32[160,128]{1,0:T(8,128)S(1)}, u32[]{:S(2)}, u32[]{:S(2)}) %collective-permute-start.8) | collective-permute-done | bytes 81952 | tf_op jit(solution)/shard_map/ppermute | solution.py:356
  85.5 2.7 %collective-permute-done.9 = f32[160,128]{1,0:T(8,128)S(1)} collective-permute-done((f32[160,128]{1,0:T(8,128)S(1)}, f32[160,128]{1,0:T(8,128)S(1)}, u32[]{:S(2)}, u32[]{:S(2)}) %collective-permute-start.9) | collective-permute-done | bytes 81952 | tf_op jit(solution)/shard_map/ppermute | solution.py:356
  88.2 1.7 %collective-permute-start.10 = (f32[160,128]{1,0:T(8,128)S(1)}, f32[160,128]{1,0:T(8,128)S(1)}, u32[]{:S(2)}, u32[]{:S(2)}) collective-permute-start(f32[160,128]{1,0:T(8,128)S(1)} %add_add_fusion.1), channel_id=1, source_target_pairs={{0,2},{2,0},{4,6},{6,4},{8,10},{10,8},{12,14},{14,12},{1,3},{3,1},... | collective-permute-start | bytes 245768 | tf_op jit(solution)/shard_map/ppermute | solution.py:356
  89.9 1.8 %collective-permute-done.10 = f32[160,128]{1,0:T(8,128)S(1)} collective-permute-done((f32[160,128]{1,0:T(8,128)S(1)}, f32[160,128]{1,0:T(8,128)S(1)}, u32[]{:S(2)}, u32[]{:S(2)}) %collective-permute-start.10) | collective-permute-done | bytes 81952 | tf_op jit(solution)/shard_map/ppermute | solution.py:356
  91.7 3.1 %collective-permute-start.11 = (f32[160,128]{1,0:T(8,128)S(1)}, f32[160,128]{1,0:T(8,128)S(1)}, u32[]{:S(2)}, u32[]{:S(2)}) collective-permute-start(f32[160,128]{1,0:T(8,128)S(1)} %add.69), channel_id=1, source_target_pairs={{0,4},{2,6},{4,0},{6,2},{8,12},{10,14},{12,8},{14,10},{1,5},{3,7},... | collective-permute-start | bytes 245768 | tf_op jit(solution)/shard_map/ppermute | solution.py:356
  94.8 4.9 %collective-permute-start.12 = (f32[160,128]{1,0:T(8,128)S(1)}, f32[160,128]{1,0:T(8,128)S(1)}, u32[]{:S(2)}, u32[]{:S(2)}) collective-permute-start(f32[160,128]{1,0:T(8,128)S(1)} %add.69), channel_id=1, source_target_pairs={{0,8},{2,10},{4,12},{6,14},{8,0},{10,2},{12,4},{14,6},{1,9},{3,11}... | collective-permute-start | bytes 245768 | tf_op jit(solution)/shard_map/ppermute | solution.py:356
  99.7 0.0 collective-permute-start.13
  99.8 0.0 collective-permute-done.11
  99.8 2.8 %collective-permute-done.12 = f32[160,128]{1,0:T(8,128)S(1)} collective-permute-done((f32[160,128]{1,0:T(8,128)S(1)}, f32[160,128]{1,0:T(8,128)S(1)}, u32[]{:S(2)}, u32[]{:S(2)}) %collective-permute-start.12) | collective-permute-done | bytes 81952 | tf_op jit(solution)/shard_map/ppermute | solution.py:356
  102.6 3.7 %collective-permute-done.13 = f32[160,128]{1,0:T(8,128)S(1)} collective-permute-done((f32[160,128]{1,0:T(8,128)S(1)}, f32[160,128]{1,0:T(8,128)S(1)}, u32[]{:S(2)}, u32[]{:S(2)}) %collective-permute-start.13) | collective-permute-done | bytes 81952 | tf_op jit(solution)/shard_map/ppermute | solution.py:356
  106.2 0.7 broadcast_in_dim.2
  107.0 3.5 %all-to-all-start.1 = ((f32[4,160,128]{2,1,0:T(8,128)}), f32[4,160,128]{2,1,0:T(8,128)S(1)}, u32[]{:S(2)}, u32[]{:S(2)}) async-start(f32[4,160,128]{2,1,0:T(8,128)} %broadcast_in_dim.2), calls=%async_computation.1 | async-start | bytes 655360 | tf_op jit(solution)/shard_map/all_to_all | solution.py:375
  110.4 0.0 copy-done.3
  110.4 0.1 copy.5
  110.6 5.7 %all-to-all-done.1 = f32[4,160,128]{2,1,0:T(8,128)S(1)} async-done(((f32[4,160,128]{2,1,0:T(8,128)}), f32[4,160,128]{2,1,0:T(8,128)S(1)}, u32[]{:S(2)}, u32[]{:S(2)}) %all-to-all-start.1) | async-done | bytes 327712 | tf_op jit(solution)/shard_map/all_to_all | solution.py:375
  116.3 7.2 %all_gather.3 = f32[1280,128]{1,0:T(8,128)S(1)} all-gather(f32[640,128]{1,0:T(8,128)S(1)} %bitcast.33), channel_id=1, replica_groups=mesh['x'=4,'y'=4,'z'=8,'core'=2] {'core'}, dimensions={0}, use_global_device_ids=true | all-gather | bytes 983040 | tf_op jit(solution)/shard_map/all_gather | solution.py:377
  123.5 0.0 copy-start
  123.5 17.8 %basis_or_triangle.1 = (f32[128,512]{1,0:T(8,128)S(1)}, f32[512,512]{1,0:T(8,128)S(1)}) custom-call(s32[1]{0:T(128)} %bitcast.1.core_ref, f32[10,128,128]{2,1,0:T(8,128)S(1)} %bitcast.27, f32[128,512]{1,0:T(8,128)S(1)} %bitcast.28), custom_call_target="tpu_custom_call" | custom-call | flops 40000000000 | bytes 2097152 | tf_op jit(solution)/shard_map/basis_or_triangle/pallas_call | solution.py:231
  141.3 2.7 %collective-permute-start.14 = (f32[128,512]{1,0:T(8,128)S(1)}, f32[128,512]{1,0:T(8,128)S(1)}, u32[]{:S(2)}, u32[]{:S(2)}) collective-permute-start(f32[128,512]{1,0:T(8,128)S(1)} %get-tuple-element.20.refs_1_), channel_id=1, source_target_pairs={{0,1},{1,0},{2,3},{3,2},{4,5},{5,4},{6,7},{7,6},{8,9},{9,8},{10,11... | collective-permute-start | bytes 786440 | tf_op jit(solution)/shard_map/ppermute | solution.py:356
  143.9 1.2 collective-permute-done.14.refs_2_
  145.1 0.4 collective-permute-start.15
  145.5 0.0 copy-done
  145.5 0.0 copy-done.1
  145.5 0.0 copy-done.2
  145.5 2.0 %core_parts.1 = (f32[512,128]{1,0:T(8,128)}, f32[8,32,256]{2,1,0:T(8,128)S(1)}, f32[8,32,256]{2,1,0:T(8,128)S(1)}, f32[8,32,256]{2,1,0:T(8,128)S(1)}, f32[8,32,256]{2,1,0:T(8,128)S(1)}) custom-call(s32[2]{0:T(128)S(1)} %copy-done.2, f32[128,512]{1,0:T(8,128)S(1)} %get-tuple-element.20.refs_1_, f32[128,512]{1,0:T(8,128)S(1)} %collective-permute-done.14.refs_2_, ...), custom_call_target="tpu_custom_call" | custom-call | flops 805306368 | bytes 5242880 | tf_op jit(solution)/shard_map/core_parts/pallas_call | solution.py:303
  147.5 0.4 collective-permute-start.16
  147.9 1.8 %collective-permute-start.17 = (f32[8,32,256]{2,1,0:T(8,128)S(1)}, f32[8,32,256]{2,1,0:T(8,128)S(1)}, u32[]{:S(2)}, u32[]{:S(2)}) collective-permute-start(f32[8,32,256]{2,1,0:T(8,128)S(1)} %get-tuple-element.29), channel_id=1, source_target_pairs={{0,128},{64,192},{128,0},{192,64},{1,129},{65,193},{129,1},{193,65... | collective-permute-start | bytes 786440 | tf_op jit(solution)/shard_map/ppermute | solution.py:356
  149.6 1.8 %collective-permute-start.18 = (f32[8,32,256]{2,1,0:T(8,128)S(1)}, f32[8,32,256]{2,1,0:T(8,128)S(1)}, u32[]{:S(2)}, u32[]{:S(2)}) collective-permute-start(f32[8,32,256]{2,1,0:T(8,128)S(1)} %get-tuple-element.30), channel_id=1, source_target_pairs={{0,192},{64,128},{128,64},{192,0},{1,193},{65,129},{129,65},{193,1... | collective-permute-start | bytes 786440 | tf_op jit(solution)/shard_map/ppermute | solution.py:356
  151.4 0.0 collective-permute-done.15.other_ref
  151.4 5.4 %finished.1 = f32[512,512]{1,0:T(8,128)} custom-call(s32[1]{0:T(128)} %bitcast.1.core_ref, f32[512,512]{1,0:T(8,128)S(1)} %get-tuple-element.26.own_ref, f32[512,512]{1,0:T(8,128)S(1)} %collective-permute-done.15.other_ref), custom_call_target="tpu_custom_call" | custom-call | flops 6000000000 | bytes 2097152 | tf_op jit(solution)/shard_map/finished/pallas_call | solution.py:263
  156.8 0.0 collective-permute-done.16.refs_1_
  156.8 4.8 %collective-permute-done.17.refs_2_ = f32[8,32,256]{2,1,0:T(8,128)S(1)} collective-permute-done((f32[8,32,256]{2,1,0:T(8,128)S(1)}, f32[8,32,256]{2,1,0:T(8,128)S(1)}, u32[]{:S(2)}, u32[]{:S(2)}) %collective-permute-start.17) | collective-permute-done | bytes 262176 | tf_op jit(solution)/shard_map/ppermute | solution.py:356
  161.6 2.0 %collective-permute-done.18.refs_3_ = f32[8,32,256]{2,1,0:T(8,128)S(1)} collective-permute-done((f32[8,32,256]{2,1,0:T(8,128)S(1)}, f32[8,32,256]{2,1,0:T(8,128)S(1)}, u32[]{:S(2)}, u32[]{:S(2)}) %collective-permute-start.18) | collective-permute-done | bytes 262176 | tf_op jit(solution)/shard_map/ppermute | solution.py:356
  163.6 1.6 placed.1
  (6 shorter events, 0.1 us)
Async XLA Ops:
  3.6 55.6 %collective-permute-start.3 = (f32[6,256,128]{2,1,0:T(8,128)S(1)}, f32[6,256,128]{2,1,0:T(8,128)}, u32[]{:S(2)}, u32[]{:S(2)}) collective-permute-start(f32[6,256,128]{2,1,0:T(8,128)S(1)} %get-tuple-element.35), channel_id=1, source_target_pairs={{0,64},{64,0},{128,192},{192,128},{1,65},{65,1},{129,193},{193,129... | collective-permute-start | bytes 2359304 | tf_op jit(solution)/shard_map/ppermute | solution.py:356
  5.7 53.5 %collective-permute-start.4 = (f32[6,256,128]{2,1,0:T(8,128)S(1)}, f32[6,256,128]{2,1,0:T(8,128)}, u32[]{:S(2)}, u32[]{:S(2)}) collective-permute-start(f32[6,256,128]{2,1,0:T(8,128)S(1)} %get-tuple-element.34), channel_id=1, source_target_pairs={{0,128},{64,192},{128,0},{192,64},{1,129},{65,193},{129,1},{193,65... | collective-permute-start | bytes 2359304 | tf_op jit(solution)/shard_map/ppermute | solution.py:356
  8.2 51.0 %collective-permute-start.5 = (f32[6,256,128]{2,1,0:T(8,128)S(1)}, f32[6,256,128]{2,1,0:T(8,128)}, u32[]{:S(2)}, u32[]{:S(2)}) collective-permute-start(f32[6,256,128]{2,1,0:T(8,128)S(1)} %get-tuple-element.33), channel_id=1, source_target_pairs={{0,192},{64,128},{128,64},{192,0},{1,193},{65,129},{129,65},{193,1... | collective-permute-start | bytes 2359304 | tf_op jit(solution)/shard_map/ppermute | solution.py:356
  8.2 35.9 %collective-permute-start = (f32[2,256,128]{2,1,0:T(8,128)S(1)}, f32[2,256,128]{2,1,0:T(8,128)S(1)}, u32[]{:S(2)}, u32[]{:S(2)}) collective-permute-start(f32[2,256,128]{2,1,0:T(8,128)S(1)} %get-tuple-element.38), channel_id=1, source_target_pairs={{0,64},{64,0},{128,192},{192,128},{1,65},{65,1},{129,193},{193,129... | collective-permute-start | bytes 786440 | tf_op jit(solution)/shard_map/ppermute | solution.py:356
  8.4 44.9 %collective-permute-start.1 = (f32[2,256,128]{2,1,0:T(8,128)S(1)}, f32[2,256,128]{2,1,0:T(8,128)S(1)}, u32[]{:S(2)}, u32[]{:S(2)}) collective-permute-start(f32[2,256,128]{2,1,0:T(8,128)S(1)} %get-tuple-element.37), channel_id=1, source_target_pairs={{0,128},{64,192},{128,0},{192,64},{1,129},{65,193},{129,1},{193,65... | collective-permute-start | bytes 786440 | tf_op jit(solution)/shard_map/ppermute | solution.py:356
  44.2 15.0 %copy-start.4 = (f32[2,256,128]{2,1,0:T(8,128)}, f32[2,256,128]{2,1,0:T(8,128)S(1)}, u32[]{:S(2)}) copy-start(f32[2,256,128]{2,1,0:T(8,128)S(1)} %collective-permute-done.refs_2_) | copy-start | bytes 786436
  44.2 15.0 %collective-permute-start.2 = (f32[2,256,128]{2,1,0:T(8,128)S(1)}, f32[2,256,128]{2,1,0:T(8,128)}, u32[]{:S(2)}, u32[]{:S(2)}) collective-permute-start(f32[2,256,128]{2,1,0:T(8,128)S(1)} %get-tuple-element.36), channel_id=1, source_target_pairs={{0,192},{64,128},{128,64},{192,0},{1,193},{65,129},{129,65},{193,1... | collective-permute-start | bytes 786440 | tf_op jit(solution)/shard_map/ppermute | solution.py:356
  53.3 5.9 %copy-start.5 = (f32[2,256,128]{2,1,0:T(8,128)}, f32[2,256,128]{2,1,0:T(8,128)S(1)}, u32[]{:S(2)}) copy-start(f32[2,256,128]{2,1,0:T(8,128)S(1)} %collective-permute-done.1.refs_3_) | copy-start | bytes 786436
  65.0 45.4 %copy-start.3 = (f32[512,128]{1,0:T(8,128)S(1)}, f32[512,128]{1,0:T(8,128)}, u32[]{:S(2)}) copy-start(f32[512,128]{1,0:T(8,128)} %param.3) | copy-start | bytes 786436
  66.1 2.3 %collective-permute-start.6 = (f32[640,128]{1,0:T(8,128)S(1)}, f32[640,128]{1,0:T(8,128)S(1)}, u32[]{:S(2)}, u32[]{:S(2)}) collective-permute-start(f32[640,128]{1,0:T(8,128)S(1)} %constant_dynamic-slice_fusion), channel_id=1, source_target_pairs={{0,1},{1,0},{2,3},{3,2},{4,5},{5,4},{6,7},{7,6},{8,9},{9,8},{10,11... | collective-permute-start | bytes 983048 | tf_op jit(solution)/shard_map/ppermute | solution.py:356
  78.6 4.2 %collective-permute-start.7 = (f32[160,128]{1,0:T(8,128)S(1)}, f32[160,128]{1,0:T(8,128)S(1)}, u32[]{:S(2)}, u32[]{:S(2)}) collective-permute-start(f32[160,128]{1,0:T(8,128)S(1)} %fusion.1), channel_id=1, source_target_pairs={{0,16},{16,0},{32,48},{48,32},{1,17},{17,1},{33,49},{49,33},{2,18}... | collective-permute-start | bytes 245768 | tf_op jit(solution)/shard_map/ppermute | solution.py:356
  80.1 5.3 %collective-permute-start.8 = (f32[160,128]{1,0:T(8,128)S(1)}, f32[160,128]{1,0:T(8,128)S(1)}, u32[]{:S(2)}, u32[]{:S(2)}) collective-permute-start(f32[160,128]{1,0:T(8,128)S(1)} %fusion.1), channel_id=1, source_target_pairs={{0,32},{16,48},{32,0},{48,16},{1,33},{17,49},{33,1},{49,17},{2,34}... | collective-permute-start | bytes 245768 | tf_op jit(solution)/shard_map/ppermute | solution.py:356
  82.8 5.4 %collective-permute-start.9 = (f32[160,128]{1,0:T(8,128)S(1)}, f32[160,128]{1,0:T(8,128)S(1)}, u32[]{:S(2)}, u32[]{:S(2)}) collective-permute-start(f32[160,128]{1,0:T(8,128)S(1)} %fusion.1), channel_id=1, source_target_pairs={{0,48},{16,32},{32,16},{48,0},{1,49},{17,33},{33,17},{49,1},{2,50}... | collective-permute-start | bytes 245768 | tf_op jit(solution)/shard_map/ppermute | solution.py:356
  88.2 3.6 %collective-permute-start.10 = (f32[160,128]{1,0:T(8,128)S(1)}, f32[160,128]{1,0:T(8,128)S(1)}, u32[]{:S(2)}, u32[]{:S(2)}) collective-permute-start(f32[160,128]{1,0:T(8,128)S(1)} %add_add_fusion.1), channel_id=1, source_target_pairs={{0,2},{2,0},{4,6},{6,4},{8,10},{10,8},{12,14},{14,12},{1,3},{3,1},... | collective-permute-start | bytes 245768 | tf_op jit(solution)/shard_map/ppermute | solution.py:356
  91.7 8.0 %collective-permute-start.11 = (f32[160,128]{1,0:T(8,128)S(1)}, f32[160,128]{1,0:T(8,128)S(1)}, u32[]{:S(2)}, u32[]{:S(2)}) collective-permute-start(f32[160,128]{1,0:T(8,128)S(1)} %add.69), channel_id=1, source_target_pairs={{0,4},{2,6},{4,0},{6,2},{8,12},{10,14},{12,8},{14,10},{1,5},{3,7},... | collective-permute-start | bytes 245768 | tf_op jit(solution)/shard_map/ppermute | solution.py:356
  94.8 7.7 %collective-permute-start.12 = (f32[160,128]{1,0:T(8,128)S(1)}, f32[160,128]{1,0:T(8,128)S(1)}, u32[]{:S(2)}, u32[]{:S(2)}) collective-permute-start(f32[160,128]{1,0:T(8,128)S(1)} %add.69), channel_id=1, source_target_pairs={{0,8},{2,10},{4,12},{6,14},{8,0},{10,2},{12,4},{14,6},{1,9},{3,11}... | collective-permute-start | bytes 245768 | tf_op jit(solution)/shard_map/ppermute | solution.py:356
  99.7 6.5 %collective-permute-start.13 = (f32[160,128]{1,0:T(8,128)S(1)}, f32[160,128]{1,0:T(8,128)S(1)}, u32[]{:S(2)}, u32[]{:S(2)}) collective-permute-start(f32[160,128]{1,0:T(8,128)S(1)} %add.69), channel_id=1, source_target_pairs={{0,12},{2,14},{4,8},{6,10},{8,4},{10,6},{12,0},{14,2},{1,13},{3,15... | collective-permute-start | bytes 245768 | tf_op jit(solution)/shard_map/ppermute | solution.py:356
  107.0 9.3 %all-to-all-start.1 = ((f32[4,160,128]{2,1,0:T(8,128)}), f32[4,160,128]{2,1,0:T(8,128)S(1)}, u32[]{:S(2)}, u32[]{:S(2)}) async-start(f32[4,160,128]{2,1,0:T(8,128)} %broadcast_in_dim.2), calls=%async_computation.1 | async-start | bytes 655360 | tf_op jit(solution)/shard_map/all_to_all | solution.py:375
  123.5 22.0 %copy-start = (bf16[2048,512]{1,0:T(8,128)(2,1)S(1)}, bf16[2048,512]{1,0:T(8,128)(2,1)}, u32[]{:S(2)}) copy-start(bf16[2048,512]{1,0:T(8,128)(2,1)} %get-tuple-element.23.refs_3_) | copy-start | bytes 6291460
  123.5 22.0 %copy-start.1 = (bf16[2048,512]{1,0:T(8,128)(2,1)S(1)}, bf16[2048,512]{1,0:T(8,128)(2,1)}, u32[]{:S(2)}) copy-start(bf16[2048,512]{1,0:T(8,128)(2,1)} %get-tuple-element.24.refs_4_) | copy-start | bytes 6291460
  123.5 22.0 %copy-start.2 = (s32[2]{0:T(128)S(1)}, s32[2]{0:T(128)}, u32[]{:S(2)}) copy-start(s32[2]{0:T(128)} %pad_add_fusion.refs_0_.me_ref) | copy-start | bytes 28
  141.3 3.8 %collective-permute-start.14 = (f32[128,512]{1,0:T(8,128)S(1)}, f32[128,512]{1,0:T(8,128)S(1)}, u32[]{:S(2)}, u32[]{:S(2)}) collective-permute-start(f32[128,512]{1,0:T(8,128)S(1)} %get-tuple-element.20.refs_1_), channel_id=1, source_target_pairs={{0,1},{1,0},{2,3},{3,2},{4,5},{5,4},{6,7},{7,6},{8,9},{9,8},{10,11... | collective-permute-start | bytes 786440 | tf_op jit(solution)/shard_map/ppermute | solution.py:356
  145.1 6.3 %collective-permute-start.15 = (f32[512,512]{1,0:T(8,128)S(1)}, f32[512,512]{1,0:T(8,128)S(1)}, u32[]{:S(2)}, u32[]{:S(2)}) collective-permute-start(f32[512,512]{1,0:T(8,128)S(1)} %get-tuple-element.26.own_ref), channel_id=1, source_target_pairs={{0,1},{1,0},{2,3},{3,2},{4,5},{5,4},{6,7},{7,6},{8,9},{9,8},{10,11... | collective-permute-start | bytes 3145736 | tf_op jit(solution)/shard_map/ppermute | solution.py:356
  147.5 9.3 %collective-permute-start.16 = (f32[8,32,256]{2,1,0:T(8,128)S(1)}, f32[8,32,256]{2,1,0:T(8,128)S(1)}, u32[]{:S(2)}, u32[]{:S(2)}) collective-permute-start(f32[8,32,256]{2,1,0:T(8,128)S(1)} %get-tuple-element.28), channel_id=1, source_target_pairs={{0,64},{64,0},{128,192},{192,128},{1,65},{65,1},{129,193},{193,129... | collective-permute-start | bytes 786440 | tf_op jit(solution)/shard_map/ppermute | solution.py:356
  147.9 13.7 %collective-permute-start.17 = (f32[8,32,256]{2,1,0:T(8,128)S(1)}, f32[8,32,256]{2,1,0:T(8,128)S(1)}, u32[]{:S(2)}, u32[]{:S(2)}) collective-permute-start(f32[8,32,256]{2,1,0:T(8,128)S(1)} %get-tuple-element.29), channel_id=1, source_target_pairs={{0,128},{64,192},{128,0},{192,64},{1,129},{65,193},{129,1},{193,65... | collective-permute-start | bytes 786440 | tf_op jit(solution)/shard_map/ppermute | solution.py:356
  149.6 14.0 %collective-permute-start.18 = (f32[8,32,256]{2,1,0:T(8,128)S(1)}, f32[8,32,256]{2,1,0:T(8,128)S(1)}, u32[]{:S(2)}, u32[]{:S(2)}) collective-permute-start(f32[8,32,256]{2,1,0:T(8,128)S(1)} %get-tuple-element.30), channel_id=1, source_target_pairs={{0,192},{64,128},{128,64},{192,0},{1,193},{65,129},{129,65},{193,1... | collective-permute-start | bytes 786440 | tf_op jit(solution)/shard_map/ppermute | solution.py:356

commit v6 on v5

--- a/solution.py
+++ b/solution.py
@@ -10,7 +10,7 @@
 NB = 4
 W = 128
 PAIRS = [(k, l) for k in range(NB) for l in range(k, NB)]
-COUNTS = (2, 6)
+COUNTS = (8,)
 STEP = 2
 SMALL = 14 * 1024 * 1024
 VMEM_LIMIT = 60 * 1024 * 1024
@@ -388,12 +388,11 @@
 
     arrived, start, later = [], 0, field
     for count in counts:
-        got, sends = {}, []
+        got = {}
         for bits in (2, 1, 3):
             send = lax.dynamic_slice(later, (me ^ bits, start, 0, 0), (1, count, snaps, width))[0]
             got[bits] = exchanged(send, "x", bits)
-            sends.append(send)
-        later, *_ = lax.optimization_barrier((later, *sends))
+            later, _ = lax.optimization_barrier((later, send))
         arrived.append([got[bits] for bits in (1, 2, 3)])
         start += count
     gram, high, low = gram_blocks(place, field, counts, arrived, scale)

time: 166 us -> 165 us (level)
  starting transfers between devices: 37.5 us -> 32.8 us
    ppermute x19 -> x16, starting transfers between devices: 34.1 us -> 29.3 us  [exchanged(): return lax.ppermute(block, axis, [(i, i ^ bits) for i in range(count)])]
    ppermute x19 -> x16, waiting for transfers between devices: 65.7 us -> 67.2 us  [exchanged(): return lax.ppermute(block, axis, [(i, i ^ bits) for i in range(count)])]
    squeeze x2 -> x3, local copies, waits for them, and re-layouts: 2.94 us -> 3.9 us  [local(): lax.dynamic_slice(later, (me ^ bits, start, 0, 0), (1, count, snaps, width))]
  transfers between devices with their start and end apart: 20 -> 17, of which waited for: 13 -> 14; matrix products, arithmetic and copies ran while one was open for 0% -> 0% of each run, Pallas kernels for 4% -> 4%
where the time goes in v6:
time: 165 us; the launch traced here: 164 us
  waiting for transfers between devices  72.9 us (44%)
  starting transfers between devices  32.8 us (20%)
  Pallas kernels  32.6 us (20%)
  blocking collectives  17.7 us (11%)
  local copies, waits for them, and re-layouts  5.83 us (4%)
  other arithmetic  1.7 us (1%)
    ppermute x16, waiting for transfers between devices, exchanged(): return lax.ppermute(block, axis, [(i, i ^ bits) for i in range(count)])  67.2 us
    ppermute x16, starting transfers between devices, exchanged(): return lax.ppermute(block, axis, [(i, i ^ bits) for i in range(count)])  29.3 us
    pallas_call x1, Pallas kernels, basis_or_triangle(): pl.pallas_call(either_kernel, in_specs=[pl.BlockSpec(memory_space=pltpu.S...  17.8 us
    all_to_all x1, blocking collectives, summed_over_devices(): lax.all_to_all(own.reshape(NB, half // NB, W), 'x', split_axis=0, concat_...  10.5 us
    all_gather x1, blocking collectives, summed_over_devices(): return lax.all_gather(whole, 'core', axis=0, tiled=True)  7.23 us
    pallas_call x1, Pallas kernels, gram_blocks(): pl.pallas_call(lambda *refs: gram_kernel(scale, counts, *refs), in_specs=...  5.79 us
    all_to_all x1, waiting for transfers between devices, summed_over_devices(): whole = lax.all_to_all(copies, 'x', split_axis=0, concat_axis=0, tiled=True)  5.7 us
    pallas_call x1, Pallas kernels, finished(): pl.pallas_call(finish_kernel, in_specs=[pl.BlockSpec(memory_space=pltpu.S...  5.37 us
  transfers between devices with their start and end apart: 17, of which 14 were waited for; matrix products, arithmetic and copies ran while one was open for 0% of the time, Pallas kernels for 4%

profile of v6, /device:TPU:1, one launch (start us, length us, event | category | flops | bytes accessed | tf_op | source)
XLA Modules:
  0.0 164.4 jit_solution(14292010997126570737)
XLA Ops:
  0.6 1.3 dynamic-slice_bitcast_fusion.2
  2.0 1.3 dynamic-slice_bitcast_fusion.1
  3.3 1.3 dynamic-slice_bitcast_fusion
  4.6 3.4 %collective-permute-start.2 = (f32[8,256,128]{2,1,0:T(8,128)S(1)}, f32[8,256,128]{2,1,0:T(8,128)}, u32[]{:S(2)}, u32[]{:S(2)}) collective-permute-start(f32[8,256,128]{2,1,0:T(8,128)S(1)} %dynamic-slice_bitcast_fusion), channel_id=1, source_target_pairs={{0,192},{64,128},{128,64},{192,0},{1,193},{65,129},{129,65},{193,1... | collective-permute-start | bytes 3145736 | tf_op jit(solution)/shard_map/ppermute | solution.py:356
  8.0 0.0 collective-permute-start
  8.0 1.3 collective-permute-start.1
  9.3 0.6 pad_add_fusion.refs_0_.me_ref
  9.9 19.9 %collective-permute-done.2.refs_4_ = f32[8,256,128]{2,1,0:T(8,128)} collective-permute-done((f32[8,256,128]{2,1,0:T(8,128)S(1)}, f32[8,256,128]{2,1,0:T(8,128)}, u32[]{:S(2)}, u32[]{:S(2)}) %collective-permute-start.2) | collective-permute-done | bytes 1048608 | tf_op jit(solution)/shard_map/ppermute | solution.py:356
  29.8 2.0 %collective-permute-done.refs_2_ = f32[8,256,128]{2,1,0:T(8,128)} collective-permute-done((f32[8,256,128]{2,1,0:T(8,128)S(1)}, f32[8,256,128]{2,1,0:T(8,128)}, u32[]{:S(2)}, u32[]{:S(2)}) %collective-permute-start) | collective-permute-done | bytes 1048608 | tf_op jit(solution)/shard_map/ppermute | solution.py:356
  31.8 20.4 %collective-permute-done.1.refs_3_ = f32[8,256,128]{2,1,0:T(8,128)} collective-permute-done((f32[8,256,128]{2,1,0:T(8,128)S(1)}, f32[8,256,128]{2,1,0:T(8,128)}, u32[]{:S(2)}, u32[]{:S(2)}) %collective-permute-start.1) | collective-permute-done | bytes 1048608 | tf_op jit(solution)/shard_map/ppermute | solution.py:356
  52.2 5.8 %gram_blocks.1 = (f32[10,128,128]{2,1,0:T(8,128)}, bf16[2048,512]{1,0:T(8,128)(2,1)}, bf16[2048,512]{1,0:T(8,128)(2,1)}) custom-call(s32[2]{0:T(128)} %pad_add_fusion.refs_0_.me_ref, f32[4,8,256,128]{3,2,1,0:T(8,128)} %bitcast.26, f32[8,256,128]{2,1,0:T(8,128)} %collective-permute-done.refs_2_, f32[8,256,128]{2,1,0:T(8,128)} %collective-permute-done.1.refs_3_, ...), custom_call_target="tpu_custom_call" | custom-call | flops 2147483648 | bytes 8388608 | tf_op jit(solution)/shard_map/gram_blocks/pallas_call | solution.py:78
  58.0 0.0 copy-start.3
  58.0 1.0 constant_dynamic-slice_fusion
  59.1 3.8 %collective-permute-start.3 = (f32[640,128]{1,0:T(8,128)S(1)}, f32[640,128]{1,0:T(8,128)S(1)}, u32[]{:S(2)}, u32[]{:S(2)}) collective-permute-start(f32[640,128]{1,0:T(8,128)S(1)} %constant_dynamic-slice_fusion), channel_id=1, source_target_pairs={{0,1},{1,0},{2,3},{3,2},{4,5},{5,4},{6,7},{7,6},{8,9},{9,8},{10,11... | collective-permute-start | bytes 983048 | tf_op jit(solution)/shard_map/ppermute | solution.py:356
  62.9 1.3 collective-permute-done.3
  64.1 1.0 dynamic-slice_add_fusion
  65.1 10.5 %all_to_all.10 = f32[4,160,128]{2,1,0:T(8,128)S(1)} all-to-all(f32[4,160,128]{2,1,0:T(8,128)S(1)} %bitcast.27), channel_id=1, replica_groups=mesh['x'=4,'y'=4,'z'=8,'core'=2] {'x'}, dimensions={0} | all-to-all | bytes 655360 | tf_op jit(solution)/shard_map/all_to_all | solution.py:365
  75.6 1.4 collective-permute-start.4
  77.0 2.6 %collective-permute-start.5 = (f32[160,128]{1,0:T(8,128)S(1)}, f32[160,128]{1,0:T(8,128)S(1)}, u32[]{:S(2)}, u32[]{:S(2)}) collective-permute-start(f32[160,128]{1,0:T(8,128)S(1)} %fusion.1), channel_id=1, source_target_pairs={{0,32},{16,48},{32,0},{48,16},{1,33},{17,49},{33,1},{49,17},{2,34}... | collective-permute-start | bytes 245768 | tf_op jit(solution)/shard_map/ppermute | solution.py:356
  79.6 0.0 collective-permute-start.6
  79.6 0.0 collective-permute-done.4
  79.6 2.7 %collective-permute-done.5 = f32[160,128]{1,0:T(8,128)S(1)} collective-permute-done((f32[160,128]{1,0:T(8,128)S(1)}, f32[160,128]{1,0:T(8,128)S(1)}, u32[]{:S(2)}, u32[]{:S(2)}) %collective-permute-start.5) | collective-permute-done | bytes 81952 | tf_op jit(solution)/shard_map/ppermute | solution.py:356
  82.3 2.7 %collective-permute-done.6 = f32[160,128]{1,0:T(8,128)S(1)} collective-permute-done((f32[160,128]{1,0:T(8,128)S(1)}, f32[160,128]{1,0:T(8,128)S(1)}, u32[]{:S(2)}, u32[]{:S(2)}) %collective-permute-start.6) | collective-permute-done | bytes 81952 | tf_op jit(solution)/shard_map/ppermute | solution.py:356
  85.0 1.7 %collective-permute-start.7 = (f32[160,128]{1,0:T(8,128)S(1)}, f32[160,128]{1,0:T(8,128)S(1)}, u32[]{:S(2)}, u32[]{:S(2)}) collective-permute-start(f32[160,128]{1,0:T(8,128)S(1)} %add_add_fusion.1), channel_id=1, source_target_pairs={{0,2},{2,0},{4,6},{6,4},{8,10},{10,8},{12,14},{14,12},{1,3},{3,1},... | collective-permute-start | bytes 245768 | tf_op jit(solution)/shard_map/ppermute | solution.py:356
  86.8 1.8 %collective-permute-done.7 = f32[160,128]{1,0:T(8,128)S(1)} collective-permute-done((f32[160,128]{1,0:T(8,128)S(1)}, f32[160,128]{1,0:T(8,128)S(1)}, u32[]{:S(2)}, u32[]{:S(2)}) %collective-permute-start.7) | collective-permute-done | bytes 81952 | tf_op jit(solution)/shard_map/ppermute | solution.py:356
  88.6 5.9 %collective-permute-start.10 = (f32[160,128]{1,0:T(8,128)S(1)}, f32[160,128]{1,0:T(8,128)S(1)}, u32[]{:S(2)}, u32[]{:S(2)}) collective-permute-start(f32[160,128]{1,0:T(8,128)S(1)} %add.66), channel_id=1, source_target_pairs={{0,12},{2,14},{4,8},{6,10},{8,4},{10,6},{12,0},{14,2},{1,13},{3,15... | collective-permute-start | bytes 245768 | tf_op jit(solution)/shard_map/ppermute | solution.py:356
  94.5 1.2 collective-permute-start.8
  95.7 1.0 collective-permute-start.9
  96.7 0.4 collective-permute-done.10
  97.1 3.4 %collective-permute-done.8 = f32[160,128]{1,0:T(8,128)S(1)} collective-permute-done((f32[160,128]{1,0:T(8,128)S(1)}, f32[160,128]{1,0:T(8,128)S(1)}, u32[]{:S(2)}, u32[]{:S(2)}) %collective-permute-start.8) | collective-permute-done | bytes 81952 | tf_op jit(solution)/shard_map/ppermute | solution.py:356
  100.5 4.6 %collective-permute-done.9 = f32[160,128]{1,0:T(8,128)S(1)} collective-permute-done((f32[160,128]{1,0:T(8,128)S(1)}, f32[160,128]{1,0:T(8,128)S(1)}, u32[]{:S(2)}, u32[]{:S(2)}) %collective-permute-start.9) | collective-permute-done | bytes 81952 | tf_op jit(solution)/shard_map/ppermute | solution.py:356
  105.2 0.7 broadcast_in_dim.2
  105.9 3.5 %all-to-all-start.1 = ((f32[4,160,128]{2,1,0:T(8,128)}), f32[4,160,128]{2,1,0:T(8,128)S(1)}, u32[]{:S(2)}, u32[]{:S(2)}) async-start(f32[4,160,128]{2,1,0:T(8,128)} %broadcast_in_dim.2), calls=%async_computation.1 | async-start | bytes 655360 | tf_op jit(solution)/shard_map/all_to_all | solution.py:375
  109.4 0.0 copy-done.3
  109.4 0.1 copy.5
  109.5 5.7 %all-to-all-done.1 = f32[4,160,128]{2,1,0:T(8,128)S(1)} async-done(((f32[4,160,128]{2,1,0:T(8,128)}), f32[4,160,128]{2,1,0:T(8,128)S(1)}, u32[]{:S(2)}, u32[]{:S(2)}) %all-to-all-start.1) | async-done | bytes 327712 | tf_op jit(solution)/shard_map/all_to_all | solution.py:375
  115.2 7.2 %all_gather.3 = f32[1280,128]{1,0:T(8,128)S(1)} all-gather(f32[640,128]{1,0:T(8,128)S(1)} %bitcast.28), channel_id=1, replica_groups=mesh['x'=4,'y'=4,'z'=8,'core'=2] {'core'}, dimensions={0}, use_global_device_ids=true | all-gather | bytes 983040 | tf_op jit(solution)/shard_map/all_gather | solution.py:377
  122.4 0.0 copy-start
  122.4 0.0 copy-start.1
  122.4 0.0 copy-start.2
  122.4 17.8 %basis_or_triangle.1 = (f32[128,512]{1,0:T(8,128)S(1)}, f32[512,512]{1,0:T(8,128)S(1)}) custom-call(s32[1]{0:T(128)} %bitcast.1.core_ref, f32[10,128,128]{2,1,0:T(8,128)S(1)} %bitcast.21, f32[128,512]{1,0:T(8,128)S(1)} %bitcast.22), custom_call_target="tpu_custom_call" | custom-call | flops 40000000000 | bytes 2097152 | tf_op jit(solution)/shard_map/basis_or_triangle/pallas_call | solution.py:231
  140.2 2.7 %collective-permute-start.11 = (f32[128,512]{1,0:T(8,128)S(1)}, f32[128,512]{1,0:T(8,128)S(1)}, u32[]{:S(2)}, u32[]{:S(2)}) collective-permute-start(f32[128,512]{1,0:T(8,128)S(1)} %get-tuple-element.22.refs_1_), channel_id=1, source_target_pairs={{0,1},{1,0},{2,3},{3,2},{4,5},{5,4},{6,7},{7,6},{8,9},{9,8},{10,11... | collective-permute-start | bytes 786440 | tf_op jit(solution)/shard_map/ppermute | solution.py:356
  142.9 1.2 collective-permute-done.11.refs_2_
  144.1 0.4 collective-permute-start.12
  144.4 0.0 copy-done
  144.4 0.0 copy-done.1
  144.4 0.0 copy-done.2
  144.4 2.0 %core_parts.1 = (f32[512,128]{1,0:T(8,128)}, f32[8,32,256]{2,1,0:T(8,128)S(1)}, f32[8,32,256]{2,1,0:T(8,128)S(1)}, f32[8,32,256]{2,1,0:T(8,128)S(1)}, f32[8,32,256]{2,1,0:T(8,128)S(1)}) custom-call(s32[2]{0:T(128)S(1)} %copy-done.2, f32[128,512]{1,0:T(8,128)S(1)} %get-tuple-element.22.refs_1_, f32[128,512]{1,0:T(8,128)S(1)} %collective-permute-done.11.refs_2_, ...), custom_call_target="tpu_custom_call" | custom-call | flops 805306368 | bytes 5242880 | tf_op jit(solution)/shard_map/core_parts/pallas_call | solution.py:303
  146.5 0.4 collective-permute-start.13
  146.8 1.8 %collective-permute-start.14 = (f32[8,32,256]{2,1,0:T(8,128)S(1)}, f32[8,32,256]{2,1,0:T(8,128)S(1)}, u32[]{:S(2)}, u32[]{:S(2)}) collective-permute-start(f32[8,32,256]{2,1,0:T(8,128)S(1)} %get-tuple-element.31), channel_id=1, source_target_pairs={{0,128},{64,192},{128,0},{192,64},{1,129},{65,193},{129,1},{193,65... | collective-permute-start | bytes 786440 | tf_op jit(solution)/shard_map/ppermute | solution.py:356
  148.6 1.8 %collective-permute-start.15 = (f32[8,32,256]{2,1,0:T(8,128)S(1)}, f32[8,32,256]{2,1,0:T(8,128)S(1)}, u32[]{:S(2)}, u32[]{:S(2)}) collective-permute-start(f32[8,32,256]{2,1,0:T(8,128)S(1)} %get-tuple-element.32), channel_id=1, source_target_pairs={{0,192},{64,128},{128,64},{192,0},{1,193},{65,129},{129,65},{193,1... | collective-permute-start | bytes 786440 | tf_op jit(solution)/shard_map/ppermute | solution.py:356
  150.4 0.0 collective-permute-done.12.other_ref
  150.4 5.4 %finished.1 = f32[512,512]{1,0:T(8,128)} custom-call(s32[1]{0:T(128)} %bitcast.1.core_ref, f32[512,512]{1,0:T(8,128)S(1)} %get-tuple-element.28.own_ref, f32[512,512]{1,0:T(8,128)S(1)} %collective-permute-done.12.other_ref), custom_call_target="tpu_custom_call" | custom-call | flops 6000000000 | bytes 2097152 | tf_op jit(solution)/shard_map/finished/pallas_call | solution.py:263
  155.8 0.0 collective-permute-done.13.refs_1_
  155.8 4.8 %collective-permute-done.14.refs_2_ = f32[8,32,256]{2,1,0:T(8,128)S(1)} collective-permute-done((f32[8,32,256]{2,1,0:T(8,128)S(1)}, f32[8,32,256]{2,1,0:T(8,128)S(1)}, u32[]{:S(2)}, u32[]{:S(2)}) %collective-permute-start.14) | collective-permute-done | bytes 262176 | tf_op jit(solution)/shard_map/ppermute | solution.py:356
  160.6 2.0 %collective-permute-done.15.refs_3_ = f32[8,32,256]{2,1,0:T(8,128)S(1)} collective-permute-done((f32[8,32,256]{2,1,0:T(8,128)S(1)}, f32[8,32,256]{2,1,0:T(8,128)S(1)}, u32[]{:S(2)}, u32[]{:S(2)}) %collective-permute-start.15) | collective-permute-done | bytes 262176 | tf_op jit(solution)/shard_map/ppermute | solution.py:356
  162.6 1.6 %placed.1 = f32[4,8,32,256]{3,2,1,0:T(8,128)} custom-call(s32[2]{0:T(128)S(1)} %copy-done.2, f32[8,32,256]{2,1,0:T(8,128)S(1)} %get-tuple-element.29.refs_0_, f32[8,32,256]{2,1,0:T(8,128)S(1)} %collective-permute-done.13.refs_1_, f32[8,32,256]{2,1,0:T(8,128)S(1)} %collective-permute-done.14.refs_2_, f32[8,32,256]{2,1,0:T(8,128)S(1)} %collective-permute-done.15.refs_3_), custom_call_target="tpu_custom_call" | custom-call | tf_op jit(solution)/shard_map/placed/pallas_call | solution.py:340
  (4 shorter events, 0.1 us)
Async XLA Ops:
  4.6 25.2 %collective-permute-start.2 = (f32[8,256,128]{2,1,0:T(8,128)S(1)}, f32[8,256,128]{2,1,0:T(8,128)}, u32[]{:S(2)}, u32[]{:S(2)}) collective-permute-start(f32[8,256,128]{2,1,0:T(8,128)S(1)} %dynamic-slice_bitcast_fusion), channel_id=1, source_target_pairs={{0,192},{64,128},{128,64},{192,0},{1,193},{65,129},{129,65},{193,1... | collective-permute-start | bytes 3145736 | tf_op jit(solution)/shard_map/ppermute | solution.py:356
  8.0 23.8 %collective-permute-start = (f32[8,256,128]{2,1,0:T(8,128)S(1)}, f32[8,256,128]{2,1,0:T(8,128)}, u32[]{:S(2)}, u32[]{:S(2)}) collective-permute-start(f32[8,256,128]{2,1,0:T(8,128)S(1)} %dynamic-slice_bitcast_fusion.1), channel_id=1, source_target_pairs={{0,64},{64,0},{128,192},{192,128},{1,65},{65,1},{129,193},{193,129... | collective-permute-start | bytes 3145736 | tf_op jit(solution)/shard_map/ppermute | solution.py:356
  8.0 44.3 %collective-permute-start.1 = (f32[8,256,128]{2,1,0:T(8,128)S(1)}, f32[8,256,128]{2,1,0:T(8,128)}, u32[]{:S(2)}, u32[]{:S(2)}) collective-permute-start(f32[8,256,128]{2,1,0:T(8,128)S(1)} %dynamic-slice_bitcast_fusion.2), channel_id=1, source_target_pairs={{0,128},{64,192},{128,0},{192,64},{1,129},{65,193},{129,1},{193,65... | collective-permute-start | bytes 3145736 | tf_op jit(solution)/shard_map/ppermute | solution.py:356
  58.0 51.3 %copy-start.3 = (f32[512,128]{1,0:T(8,128)S(1)}, f32[512,128]{1,0:T(8,128)}, u32[]{:S(2)}) copy-start(f32[512,128]{1,0:T(8,128)} %param.3) | copy-start | bytes 786436
  59.1 5.1 %collective-permute-start.3 = (f32[640,128]{1,0:T(8,128)S(1)}, f32[640,128]{1,0:T(8,128)S(1)}, u32[]{:S(2)}, u32[]{:S(2)}) collective-permute-start(f32[640,128]{1,0:T(8,128)S(1)} %constant_dynamic-slice_fusion), channel_id=1, source_target_pairs={{0,1},{1,0},{2,3},{3,2},{4,5},{5,4},{6,7},{7,6},{8,9},{9,8},{10,11... | collective-permute-start | bytes 983048 | tf_op jit(solution)/shard_map/ppermute | solution.py:356
  75.6 4.0 %collective-permute-start.4 = (f32[160,128]{1,0:T(8,128)S(1)}, f32[160,128]{1,0:T(8,128)S(1)}, u32[]{:S(2)}, u32[]{:S(2)}) collective-permute-start(f32[160,128]{1,0:T(8,128)S(1)} %fusion.1), channel_id=1, source_target_pairs={{0,16},{16,0},{32,48},{48,32},{1,17},{17,1},{33,49},{49,33},{2,18}... | collective-permute-start | bytes 245768 | tf_op jit(solution)/shard_map/ppermute | solution.py:356
  77.0 5.3 %collective-permute-start.5 = (f32[160,128]{1,0:T(8,128)S(1)}, f32[160,128]{1,0:T(8,128)S(1)}, u32[]{:S(2)}, u32[]{:S(2)}) collective-permute-start(f32[160,128]{1,0:T(8,128)S(1)} %fusion.1), channel_id=1, source_target_pairs={{0,32},{16,48},{32,0},{48,16},{1,33},{17,49},{33,1},{49,17},{2,34}... | collective-permute-start | bytes 245768 | tf_op jit(solution)/shard_map/ppermute | solution.py:356
  79.6 5.4 %collective-permute-start.6 = (f32[160,128]{1,0:T(8,128)S(1)}, f32[160,128]{1,0:T(8,128)S(1)}, u32[]{:S(2)}, u32[]{:S(2)}) collective-permute-start(f32[160,128]{1,0:T(8,128)S(1)} %fusion.1), channel_id=1, source_target_pairs={{0,48},{16,32},{32,16},{48,0},{1,49},{17,33},{33,17},{49,1},{2,50}... | collective-permute-start | bytes 245768 | tf_op jit(solution)/shard_map/ppermute | solution.py:356
  85.0 3.6 %collective-permute-start.7 = (f32[160,128]{1,0:T(8,128)S(1)}, f32[160,128]{1,0:T(8,128)S(1)}, u32[]{:S(2)}, u32[]{:S(2)}) collective-permute-start(f32[160,128]{1,0:T(8,128)S(1)} %add_add_fusion.1), channel_id=1, source_target_pairs={{0,2},{2,0},{4,6},{6,4},{8,10},{10,8},{12,14},{14,12},{1,3},{3,1},... | collective-permute-start | bytes 245768 | tf_op jit(solution)/shard_map/ppermute | solution.py:356
  88.6 8.5 %collective-permute-start.10 = (f32[160,128]{1,0:T(8,128)S(1)}, f32[160,128]{1,0:T(8,128)S(1)}, u32[]{:S(2)}, u32[]{:S(2)}) collective-permute-start(f32[160,128]{1,0:T(8,128)S(1)} %add.66), channel_id=1, source_target_pairs={{0,12},{2,14},{4,8},{6,10},{8,4},{10,6},{12,0},{14,2},{1,13},{3,15... | collective-permute-start | bytes 245768 | tf_op jit(solution)/shard_map/ppermute | solution.py:356
  94.5 6.0 %collective-permute-start.8 = (f32[160,128]{1,0:T(8,128)S(1)}, f32[160,128]{1,0:T(8,128)S(1)}, u32[]{:S(2)}, u32[]{:S(2)}) collective-permute-start(f32[160,128]{1,0:T(8,128)S(1)} %add.66), channel_id=1, source_target_pairs={{0,4},{2,6},{4,0},{6,2},{8,12},{10,14},{12,8},{14,10},{1,5},{3,7},... | collective-permute-start | bytes 245768 | tf_op jit(solution)/shard_map/ppermute | solution.py:356
  95.7 9.4 %collective-permute-start.9 = (f32[160,128]{1,0:T(8,128)S(1)}, f32[160,128]{1,0:T(8,128)S(1)}, u32[]{:S(2)}, u32[]{:S(2)}) collective-permute-start(f32[160,128]{1,0:T(8,128)S(1)} %add.66), channel_id=1, source_target_pairs={{0,8},{2,10},{4,12},{6,14},{8,0},{10,2},{12,4},{14,6},{1,9},{3,11}... | collective-permute-start | bytes 245768 | tf_op jit(solution)/shard_map/ppermute | solution.py:356
  105.9 9.3 %all-to-all-start.1 = ((f32[4,160,128]{2,1,0:T(8,128)}), f32[4,160,128]{2,1,0:T(8,128)S(1)}, u32[]{:S(2)}, u32[]{:S(2)}) async-start(f32[4,160,128]{2,1,0:T(8,128)} %broadcast_in_dim.2), calls=%async_computation.1 | async-start | bytes 655360 | tf_op jit(solution)/shard_map/all_to_all | solution.py:375
  122.4 22.0 %copy-start = (bf16[2048,512]{1,0:T(8,128)(2,1)S(1)}, bf16[2048,512]{1,0:T(8,128)(2,1)}, u32[]{:S(2)}) copy-start(bf16[2048,512]{1,0:T(8,128)(2,1)} %get-tuple-element.25.refs_3_) | copy-start | bytes 6291460
  122.4 22.0 %copy-start.1 = (bf16[2048,512]{1,0:T(8,128)(2,1)S(1)}, bf16[2048,512]{1,0:T(8,128)(2,1)}, u32[]{:S(2)}) copy-start(bf16[2048,512]{1,0:T(8,128)(2,1)} %get-tuple-element.26.refs_4_) | copy-start | bytes 6291460
  122.4 22.0 %copy-start.2 = (s32[2]{0:T(128)S(1)}, s32[2]{0:T(128)}, u32[]{:S(2)}) copy-start(s32[2]{0:T(128)} %pad_add_fusion.refs_0_.me_ref) | copy-start | bytes 28
  140.2 3.8 %collective-permute-start.11 = (f32[128,512]{1,0:T(8,128)S(1)}, f32[128,512]{1,0:T(8,128)S(1)}, u32[]{:S(2)}, u32[]{:S(2)}) collective-permute-start(f32[128,512]{1,0:T(8,128)S(1)} %get-tuple-element.22.refs_1_), channel_id=1, source_target_pairs={{0,1},{1,0},{2,3},{3,2},{4,5},{5,4},{6,7},{7,6},{8,9},{9,8},{10,11... | collective-permute-start | bytes 786440 | tf_op jit(solution)/shard_map/ppermute | solution.py:356
  144.1 6.3 %collective-permute-start.12 = (f32[512,512]{1,0:T(8,128)S(1)}, f32[512,512]{1,0:T(8,128)S(1)}, u32[]{:S(2)}, u32[]{:S(2)}) collective-permute-start(f32[512,512]{1,0:T(8,128)S(1)} %get-tuple-element.28.own_ref), channel_id=1, source_target_pairs={{0,1},{1,0},{2,3},{3,2},{4,5},{5,4},{6,7},{7,6},{8,9},{9,8},{10,11... | collective-permute-start | bytes 3145736 | tf_op jit(solution)/shard_map/ppermute | solution.py:356
  146.5 9.3 %collective-permute-start.13 = (f32[8,32,256]{2,1,0:T(8,128)S(1)}, f32[8,32,256]{2,1,0:T(8,128)S(1)}, u32[]{:S(2)}, u32[]{:S(2)}) collective-permute-start(f32[8,32,256]{2,1,0:T(8,128)S(1)} %get-tuple-element.30), channel_id=1, source_target_pairs={{0,64},{64,0},{128,192},{192,128},{1,65},{65,1},{129,193},{193,129... | collective-permute-start | bytes 786440 | tf_op jit(solution)/shard_map/ppermute | solution.py:356
  146.8 13.7 %collective-permute-start.14 = (f32[8,32,256]{2,1,0:T(8,128)S(1)}, f32[8,32,256]{2,1,0:T(8,128)S(1)}, u32[]{:S(2)}, u32[]{:S(2)}) collective-permute-start(f32[8,32,256]{2,1,0:T(8,128)S(1)} %get-tuple-element.31), channel_id=1, source_target_pairs={{0,128},{64,192},{128,0},{192,64},{1,129},{65,193},{129,1},{193,65... | collective-permute-start | bytes 786440 | tf_op jit(solution)/shard_map/ppermute | solution.py:356
  148.6 14.0 %collective-permute-start.15 = (f32[8,32,256]{2,1,0:T(8,128)S(1)}, f32[8,32,256]{2,1,0:T(8,128)S(1)}, u32[]{:S(2)}, u32[]{:S(2)}) collective-permute-start(f32[8,32,256]{2,1,0:T(8,128)S(1)} %get-tuple-element.32), channel_id=1, source_target_pairs={{0,192},{64,128},{128,64},{192,0},{1,193},{65,129},{129,65},{193,1... | collective-permute-start | bytes 786440 | tf_op jit(solution)/shard_map/ppermute | solution.py:356
